TPU v7x, 512 devices: a whole 4x4x16 slice. The times are simulated.
512 devices in a mesh: row: 16 (over x, y), col: 32 (over z, core).
Axes of the slice: x: 4, y: 4, z: 16, core: 2. Of those that a mesh axis runs over, the one named last changes fastest.
Arguments:
- distances: float32 [4096, 4096], P('row', 'col'), may hold values from 0.5 to 8
- neighbor_ids: int32 [10, 4096], replicated, may hold values from 0 to 4095
- edge_lengths: float32 [10, 4096], P(None, ('row', 'col')), may hold values from 0.125 to 1
- pivots: int32 [2], replicated, may hold values from 0 to 127
Outputs:
- geodesic: float32 [4096, 4096], P('row', 'col')
All inputs are finite; a program needn't handle non-finite values.
Results may differ from a plain program's by a relative error of at most 0.00002.
Values sent between devices are 32-bit elements; how exact they have to be, the bound alone decides.
No kernel may reach another device: no remote copies, remote signals or barrier semaphores. Data moves between devices by JAX's collectives and lax.ppermute only.
A program may use at most 64 MiB of HBM per device.

v0:
```python
import jax
import jax.numpy as jnp
from jax import lax
from jax.sharding import PartitionSpec as P

NEIGHBORS = 10
PIVOT = 32


def broadcast(value, axis, source):
    kept = jnp.where(lax.axis_index(axis) == source, value, 0).astype(value.dtype)
    return lax.psum(kept, axis)


def locate(pivot, rows_here, cols_here):
    base = pivot * PIVOT
    row_root = base // rows_here
    col_root = base // cols_here
    return (row_root, col_root, base - row_root * rows_here, base - col_root * cols_here)


def closure(block):

    def relax_one(t, current):
        column = lax.dynamic_slice_in_dim(current, t, 1, 1)
        row_line = lax.dynamic_slice_in_dim(current, t, 1, 0)
        return jnp.minimum(current, column + row_line)

    return lax.fori_loop(0, block.shape[0], relax_one, block)


def minplus(left, right):
    return jnp.min(left[:, :, None] + right[None, :, :], axis=1)


def apply_panels(matrix, cols_panel, rows_panel):
    rows_here = matrix.shape[0]
    width = cols_panel.shape[0]
    block = min(64, rows_here)
    left = cols_panel.T.reshape(rows_here // block, block, width)
    better = lax.map(lambda piece: minplus(piece, rows_panel), left)
    return jnp.minimum(matrix, better.reshape(rows_here, matrix.shape[1]))


def on_device(distances, neighbor_ids, edge_lengths, pivots):
    rows_here, cols_here = distances.shape
    all_lengths = lax.all_gather(edge_lengths, ("row", "col"), axis=1, tiled=True)
    row_start = lax.axis_index("row") * rows_here
    col_start = lax.axis_index("col") * cols_here
    row_ids = row_start + jnp.arange(rows_here, dtype=jnp.int32)
    col_ids = col_start + jnp.arange(cols_here, dtype=jnp.int32)
    matrix = distances
    for k in range(NEIGHBORS):
        ids_rows = lax.dynamic_slice_in_dim(neighbor_ids[k], row_start, rows_here)
        len_rows = lax.dynamic_slice_in_dim(all_lengths[k], row_start, rows_here)
        ids_cols = lax.dynamic_slice_in_dim(neighbor_ids[k], col_start, cols_here)
        len_cols = lax.dynamic_slice_in_dim(all_lengths[k], col_start, cols_here)
        forward = jnp.where(ids_rows[:, None] == col_ids[None, :], len_rows[:, None], jnp.inf)
        backward = jnp.where(row_ids[:, None] == ids_cols[None, :], len_cols[None, :], jnp.inf)
        matrix = jnp.minimum(matrix, jnp.minimum(forward, backward))
    matrix = jnp.where(row_ids[:, None] == col_ids[None, :], jnp.float32(0.0), matrix)
    for q in range(2):
        row_root, col_root, row_off, col_off = locate(pivots[q], rows_here, cols_here)
        own_rows = lax.dynamic_slice_in_dim(matrix, row_off, PIVOT, 0)
        own_cols = lax.dynamic_slice_in_dim(matrix, col_off, PIVOT, 1).T
        panel_rows = broadcast(own_rows, "row", row_root)
        panel_cols = broadcast(own_cols, "col", col_root)
        corner = lax.dynamic_slice_in_dim(own_rows, col_off, PIVOT, 1)
        corner = broadcast(corner, ("row", "col"), row_root * lax.axis_size("col") + col_root)
        closed = closure(corner)
        matrix = apply_panels(matrix, panel_cols, minplus(closed, panel_rows))
    return matrix


def solution(mesh):
    placed = (P("row", "col"), P(), P(None, ("row", "col")), P())
    return jax.shard_map(
        on_device, mesh=mesh, in_specs=placed, out_specs=P("row", "col"), check_vma=False
    )
```

profile of v0, /device:TPU:1, one launch (start us, length us, event | category | flops | bytes accessed | tf_op | source)
XLA Modules:
  0.0 686.0 jit_solution(11622199700328884202)
XLA Ops:
  0.0 123.8 %all_gather.3 = f32[10,4096]{0,1:T(8,128)S(1)} all-gather(f32[10,8]{0,1:T(8,128)} %param.14), channel_id=1, replica_groups=mesh['row'=16,'col'=32] {'row','col'}, dimensions={1}, use_global_device_ids=true | all-gather | bytes 164160 | tf_op jit(solution)/shard_map/all_gather | solution.py:47
  123.8 7.9 %fusion.12 = (f32[1,4096]{0,1:T(8,128)S(1)}, f32[1,4096]{0,1:T(8,128)S(1)}, f32[1,4096]{0,1:T(8,128)}, f32[1,4096]{0,1:T(8,128)}, f32[1,4096]{0,1:T(8,128)}, /*i...) fusion(f32[10,4096]{0,1:T(8,128)S(1)} %all_gather.3), kind=kLoop, calls=%fused_computation.77 | loop fusion | bytes 327680 | tf_op jit(solution)/shard_map/slice | solution.py:55
  131.7 1.3 copy-done
  133.2 0.5 copy-done.1
  133.6 1.0 dynamic-slice_reduce_fusion.20
  134.6 1.1 dynamic-slice_reduce_fusion.8
  135.7 1.0 dynamic-slice_reduce_fusion.18
  136.7 1.1 dynamic-slice_reduce_fusion.6
  137.8 1.0 dynamic-slice_reduce_fusion.16
  138.8 1.1 dynamic-slice_reduce_fusion.4
  140.0 1.0 dynamic-slice_reduce_fusion.14
  140.9 1.1 dynamic-slice_reduce_fusion.2
  142.0 1.0 dynamic-slice_reduce_fusion.12
  143.3 0.8 minimum_select_fusion
  144.1 0.7 fusion.14
  145.5 99.9 %psum.43 = f32[32,32]{1,0:T(8,128)S(1)} all-reduce(f32[32,32]{1,0:T(8,128)S(1)} %dynamic-slice_select_fusion.5), channel_id=1, replica_groups=mesh['row'=16,'col'=32] {'row','col'}, use_global_device_ids=true, to_apply=%region_1.2 | all-reduce | flops 1024 | bytes 8192 | tf_op jit(solution)/shard_map/psum | solution.py:12
  245.4 8.8 %while.46 = (s32[]{:T(128)}, f32[32,32]{1,0:T(8,128)S(1)}, s32[]{:T(128)}) while((s32[]{:T(128)}, f32[32,32]{1,0:T(8,128)S(1)}, s32[]{:T(128)}) %tuple.116), condition=%wide.region_3.4_spmd, body=%wide.region_2.3_spmd.sunk | while | flops 2050 | bytes 9013 | solution.py:29
  245.7 0.2 dynamic-slice_reduce_fusion.24
  245.9 0.2 dynamic-slice_reduce_fusion.24
  246.2 0.2 dynamic-slice_reduce_fusion.24
  246.5 0.2 dynamic-slice_reduce_fusion.24
  246.7 0.2 dynamic-slice_reduce_fusion.24
  247.0 0.2 dynamic-slice_reduce_fusion.24
  247.3 0.2 dynamic-slice_reduce_fusion.24
  247.6 0.2 dynamic-slice_reduce_fusion.24
  247.8 0.2 dynamic-slice_reduce_fusion.24
  248.1 0.2 dynamic-slice_reduce_fusion.24
  248.4 0.2 dynamic-slice_reduce_fusion.24
  248.9 0.2 dynamic-slice_reduce_fusion.24
  249.2 0.2 dynamic-slice_reduce_fusion.24
  249.5 0.2 dynamic-slice_reduce_fusion.24
  249.8 0.2 dynamic-slice_reduce_fusion.24
  250.0 0.2 dynamic-slice_reduce_fusion.24
  250.3 0.2 dynamic-slice_reduce_fusion.24
  250.6 0.2 dynamic-slice_reduce_fusion.24
  250.9 0.2 dynamic-slice_reduce_fusion.24
  251.1 0.2 dynamic-slice_reduce_fusion.24
  251.4 0.2 dynamic-slice_reduce_fusion.24
  251.7 0.2 dynamic-slice_reduce_fusion.24
  252.0 0.2 dynamic-slice_reduce_fusion.24
  252.2 0.2 dynamic-slice_reduce_fusion.24
  252.5 0.2 dynamic-slice_reduce_fusion.24
  252.8 0.2 dynamic-slice_reduce_fusion.24
  253.1 0.2 dynamic-slice_reduce_fusion.24
  254.2 56.8 %psum.44 = f32[32,128]{1,0:T(8,128)S(1)} all-reduce(f32[32,128]{1,0:T(8,128)S(1)} %dynamic-slice_select_fusion.4), channel_id=1, replica_groups=mesh['row'=16,'col'=32] {'row'}, use_global_device_ids=true, to_apply=%region_4.5 | all-reduce | flops 4096 | bytes 32768 | tf_op jit(solution)/shard_map/psum | solution.py:12
  310.9 0.2 add_reduce_fusion.3
  311.3 101.3 %psum.42 = f32[4,64,32]{2,1,0:T(8,128)S(1)} all-reduce(f32[4,64,32]{2,1,0:T(8,128)S(1)} %bitcast.62), channel_id=1, replica_groups=mesh['row'=16,'col'=32] {'col'}, use_global_device_ids=true, to_apply=%region_0.1 | all-reduce | flops 8192 | bytes 65536 | tf_op jit(solution)/shard_map/psum | solution.py:12
  412.6 1.7 while.47
  412.6 0.4 add_reduce_fusion.6
  413.0 0.4 add_reduce_fusion.6
  413.5 0.4 add_reduce_fusion.6
  413.9 0.4 add_reduce_fusion.6
  414.3 0.8 bitcast_minimum_fusion.1
  416.0 100.4 %psum.46 = f32[32,32]{1,0:T(8,128)S(1)} all-reduce(f32[32,32]{1,0:T(8,128)S(1)} %dynamic-slice_select_fusion.3), channel_id=1, replica_groups=mesh['row'=16,'col'=32] {'row','col'}, use_global_device_ids=true, to_apply=%region_10.11 | all-reduce | flops 1024 | bytes 8192 | tf_op jit(solution)/shard_map/psum | solution.py:12
  516.4 8.8 %while.48 = (s32[]{:T(128)}, f32[32,32]{1,0:T(8,128)S(1)}, s32[]{:T(128)}) while((s32[]{:T(128)}, f32[32,32]{1,0:T(8,128)S(1)}, s32[]{:T(128)}) %tuple.122), condition=%wide.region_12.13_spmd, body=%wide.region_11.12_spmd.sunk | while | flops 2050 | bytes 9013 | solution.py:29
  525.2 57.4 %psum.47 = f32[32,128]{1,0:T(8,128)S(1)} all-reduce(f32[32,128]{1,0:T(8,128)S(1)} %dynamic-slice_select_fusion.2), channel_id=1, replica_groups=mesh['row'=16,'col'=32] {'row'}, use_global_device_ids=true, to_apply=%region_13.14 | all-reduce | flops 4096 | bytes 32768 | tf_op jit(solution)/shard_map/psum | solution.py:12
  582.6 0.2 add_reduce_fusion.2
  582.9 100.7 %psum.45 = f32[4,64,32]{2,1,0:T(8,128)S(1)} all-reduce(f32[4,64,32]{2,1,0:T(8,128)S(1)} %bitcast.63), channel_id=1, replica_groups=mesh['row'=16,'col'=32] {'col'}, use_global_device_ids=true, to_apply=%region_9.10 | all-reduce | flops 8192 | bytes 65536 | tf_op jit(solution)/shard_map/psum | solution.py:12
  683.6 1.7 while.49
  683.6 0.4 add_reduce_fusion.7
  684.0 0.4 add_reduce_fusion.7
  684.5 0.4 add_reduce_fusion.7
  684.9 0.4 add_reduce_fusion.7
  685.3 0.7 bitcast_minimum_fusion
  (211 shorter events, 13.0 us)
Async XLA Ops:
  131.7 1.4 copy-start
  131.7 2.0 copy-start.1
  131.7 11.3 %copy-start.3 = (s32[10,4096]{1,0:T(8,128)S(1)}, s32[10,4096]{1,0:T(8,128)}, u32[]{:S(2)}) copy-start(s32[10,4096]{1,0:T(8,128)} %param.13) | copy-start | bytes 491524
  131.7 11.6 %copy-start.2 = (f32[256,128]{1,0:T(8,128)S(1)}, f32[256,128]{1,0:T(8,128)}, u32[]{:S(2)}) copy-start(f32[256,128]{1,0:T(8,128)} %param.12) | copy-start | bytes 393220
  131.7 12.4 %copy-start.4 = (s32[2]{0:T(128)S(1)}, s32[2]{0:T(128)}, u32[]{:S(2)}) copy-start(s32[2]{0:T(128)} %param.15) | copy-start | bytes 28
where the time goes:
time: 687 us; the launch traced here: 686 us
  blocking collectives  640 us (93%)
  local copies, waits for them, and re-layouts  32.5 us (5%)
  other arithmetic  10.8 us (2%)
    psum x6, blocking collectives, broadcast(): return lax.psum(kept, axis)  516 us
    all_gather x1, blocking collectives, on_device(): lax.all_gather(edge_lengths, ('row', 'col'), axis=1, tiled=True)  124 us

commit v1 on v0

v1 whole, which is shorter than its diff:
```python
import jax
import jax.numpy as jnp
from jax import lax
from jax.experimental import pallas as pl
from jax.experimental.pallas import tpu as pltpu
from jax.sharding import Mesh, PartitionSpec as P

NEIGHBORS = 10
PIVOT = 32
ROWS = 256
COLS = 128
NXY = 16
NZ = 16
F32 = jnp.float32
INF = float("inf")
VMEM_LIMIT = 48 * 1024 * 1024

XY_RQ, XY_K, XY_L, XY_ROWS = 32, 64, 80, 96
Z_K, Z_L, Z_ROWS = 16, 32, 48


def lanes(rows):
    return lax.broadcasted_iota(jnp.int32, (rows, 128), 1)


def shift_lanes(x, amount):
    return pltpu.roll(x, lax.rem(amount + 1024, 128), 1)


def role(piv):
    core = lax.axis_index("core")
    p, q = piv[0], piv[1]
    first = core == 0
    return core, p, q, jnp.where(first, p, q), jnp.where(first, q, p)


def pack_kernel(piv, dist, keep, send):
    _, _, _, mine, other = role(piv)
    block = lanes(64) // PIVOT
    for ref, pivot in ((keep, mine), (send, other)):
        off = lax.rem(pivot, 4) * PIVOT
        packed = shift_lanes(dist[0:64, :], 0 - off)
        for b in range(1, 4):
            part = shift_lanes(dist[64 * b : 64 * b + 64, :], 32 * b - off)
            packed = jnp.where(block == b, part, packed)
        ref[...] = packed


def spread_kernel(piv, dist, keep, got, lengths, xy, piece0, piece1, piece2, piece3, cols, held):
    core, p, q, mine, _ = role(piv)
    z = lax.axis_index("z")
    row = lax.axis_index("row")
    own = lax.rem(mine // 4, 2) == core
    cols[...] = jnp.where(own, keep[...], got[1 - core])
    for m, piece in enumerate((piece0, piece1, piece2, piece3)):
        part = lax.rem(z, 4) ^ m
        piece[...] = cols[pl.ds(pl.multiple_of(16 * part, 16), 16), :]
    block = lanes(16) // PIVOT
    corner = jnp.zeros((16, 128), F32)
    for i, pivot in enumerate((p, q)):
        off = lax.rem(pivot, 8) * PIVOT
        b = off // 64
        a = off - 64 * b
        for h in range(2):
            part = cols[pl.ds(pl.multiple_of(a + 16 * h, 16), 16), :]
            part = shift_lanes(part, 32 * (2 * i + h) - 32 * b)
            corner = jnp.where(block == 2 * i + h, part, corner)
    held[...] = jnp.zeros_like(held)
    held[0:NEIGHBORS, 0:8] = lengths[...]
    own_lengths = shift_lanes(held[...], 8 * row)
    rows_p = dist[pl.ds(pl.multiple_of(lax.rem(p, 8) * PIVOT, 32), 32), :]
    rows_q = dist[pl.ds(pl.multiple_of(lax.rem(q, 8) * PIVOT, 32), 32), :]
    for d in range(NXY):
        xy[d, 0:XY_RQ] = rows_p
        xy[d, XY_RQ:XY_K] = rows_q
        xy[d, XY_K:XY_L] = corner
        xy[d, XY_L:XY_ROWS] = own_lengths


def gather_kernel(piv, xy, piece0, piece1, piece2, piece3, zchunk, rows):
    _, p, q, mine, _ = role(piv)
    z = lax.axis_index("z")
    row_p, row_q = p // 8, q // 8
    rows[0:32] = xy[row_p, 0:XY_RQ]
    rows[32:64] = xy[row_q, XY_RQ:XY_K]
    m = (mine // 8) ^ z
    piece = piece0[...]
    for i, ref in ((1, piece1), (2, piece2), (3, piece3)):
        piece = jnp.where(m == i, ref[...], piece)
    corner = jnp.where(lanes(16) < 64, xy[row_p, XY_K:XY_L], xy[row_q, XY_K:XY_L])
    lengths = xy[0, XY_L:XY_ROWS]
    for d in range(1, NXY):
        lengths = jnp.maximum(lengths, xy[d, XY_L:XY_ROWS])
    for d in range(NZ):
        zchunk[d, 0:Z_K] = piece
        zchunk[d, Z_K:Z_L] = corner
        zchunk[d, Z_L:Z_ROWS] = lengths


def take_lengths(zed, first, row, count, at):
    out = None
    for u in range(count):
        col = first + u
        part = shift_lanes(zed[lax.rem(col, 2), col // 2, Z_L:Z_ROWS], at + 8 * u - 8 * row)
        out = part if out is None else jnp.where(lanes(16) // 8 >= at // 8 + u, part, out)
    return out


def relax(entry, col_v, row_v, row_ids, row_len, col_ids, col_len):
    for k in range(NEIGHBORS):
        forward = jnp.where(row_ids[k] == col_v, row_len[k], INF)
        backward = jnp.where(col_ids[k : k + 1, :] == row_v, col_len[k : k + 1, :], INF)
        entry = jnp.minimum(entry, jnp.minimum(forward, backward))
    return jnp.where(row_v == col_v, 0.0, entry)


def final_kernel(piv, dist, rows, zed, ids, out, turned, cids, clen, pids, plen, cpan, rstar):
    p, q = piv[0], piv[1]
    row = lax.axis_index("row")
    z = lax.axis_index("z")
    core = lax.axis_index("core")
    col = 2 * z + core
    lane16 = lanes(16)

    def pad_ids(x):
        return jnp.concatenate([x.astype(F32), jnp.zeros((6, 128), F32)], 0)

    def pivot_ids(pivot, at):
        base = pl.multiple_of(pivot // 4 * 128, 128)
        return shift_lanes(pad_ids(ids[:, pl.ds(base, 128)]), at - lax.rem(pivot, 4) * PIVOT)

    cids[...] = pad_ids(ids[:, pl.ds(pl.multiple_of(128 * col, 128), 128)])
    clen[...] = take_lengths(zed, 16 * core, z, 16, 0)
    pids[...] = jnp.where(lane16 < 32, pivot_ids(p, 0), pivot_ids(q, 32))
    plen[...] = jnp.where(
        lane16 < 32,
        take_lengths(zed, lax.rem(p, 8) * 4, p // 8, 4, 0),
        take_lengths(zed, lax.rem(q, 8) * 4, q // 8, 4, 32),
    )
    for h in range(2):
        base = pl.multiple_of(256 * row + 128 * h, 128)
        square = jnp.concatenate(
            [
                pad_ids(ids[:, pl.ds(base, 128)]),
                take_lengths(zed, 16 * h, row, 16, 0),
                pids[...],
                plen[...],
                jnp.zeros((64, 128), F32),
            ],
            0,
        )
        turned[128 * h : 128 * h + 128, :] = square.T

    lane = lanes(8)
    sub = lax.broadcasted_iota(jnp.int32, (8, 128), 0)
    col_v0 = (128 * col + lane).astype(F32)
    col_v1 = jnp.where(lane < 32, 32 * p + lane, jnp.where(lane < 64, 32 * q + lane - 32, -1)).astype(F32)

    def columns(tile, at):
        return [jnp.broadcast_to(tile[:, at + k : at + k + 1], (8, 128)) for k in range(NEIGHBORS)]

    group_p, group_q = p // 32 * 4, q // 32 * 4
    for quarter in range(4):
        part_p = zed[0, group_p + quarter, 0:Z_K]
        part_q = zed[1, group_q + quarter, 0:Z_K]
        for b in range(4):
            left = shift_lanes(part_p, -32 * b)
            right = shift_lanes(part_q, 32 - 32 * b)
            at = 64 * b + 16 * quarter
            cpan[at : at + 16, :] = jnp.where(lane16 < 32, left, right)
    corner_p = zed[0, p // 8, Z_K:Z_L]
    corner_q = zed[1, q // 8, Z_K:Z_L]
    corner, line = [], []
    for b in range(4):
        both = jnp.where(lane16 < 32, shift_lanes(corner_p, -32 * b), shift_lanes(corner_q, 32 - 32 * b))
        both = jnp.where(lane16 < 64, both, INF)
        for h in range(2):
            tile = 2 * b + h
            vertex = (32 * p + 8 * tile) if tile < 4 else (32 * q + 8 * tile - 32)
            row_v = (vertex + sub).astype(F32)
            turn = turned[8 * tile : 8 * tile + 8, :]
            row_ids, row_len = columns(turn, 32), columns(turn, 48)
            corner.append(
                relax(both[8 * h : 8 * h + 8], col_v1, row_v, row_ids, row_len, pids[...], plen[...])
            )
            line.append(
                relax(rows[8 * tile : 8 * tile + 8, :], col_v0, row_v, row_ids, row_len, cids[...], clen[...])
            )
    corner = jnp.concatenate(corner, 0)
    line = jnp.concatenate(line, 0)
    for t in range(2 * PIVOT):
        step = corner[:, t : t + 1]
        line = jnp.minimum(line, step + line[t : t + 1, :])
        corner = jnp.minimum(corner, step + corner[t : t + 1, :])
    rstar[...] = line

    def body(i, carry):
        for j in range(2):
            at = pl.multiple_of(16 * i + 8 * j, 8)
            turn = turned[pl.ds(at, 8), :]
            row_v = (256 * row + at + sub).astype(F32)
            row_ids, row_len = columns(turn, 0), columns(turn, 16)
            here = relax(dist[pl.ds(at, 8), :], col_v0, row_v, row_ids, row_len, cids[...], clen[...])
            panel = relax(cpan[pl.ds(at, 8), :], col_v1, row_v, row_ids, row_len, pids[...], plen[...])
            for t in range(2 * PIVOT):
                here = jnp.minimum(here, panel[:, t : t + 1] + rstar[t : t + 1, :])
            out[pl.ds(at, 8), :] = here
        return carry

    lax.fori_loop(0, ROWS // 16, body, 0)


VM = pl.BlockSpec(memory_space=pltpu.VMEM)
SM = pl.BlockSpec(memory_space=pltpu.SMEM)


def call(kernel, shapes, scratch, n_in):
    return pl.pallas_call(
        kernel,
        out_shape=[jax.ShapeDtypeStruct(s, F32) for s in shapes],
        in_specs=[SM] + [VM] * n_in,
        out_specs=[VM] * len(shapes),
        scratch_shapes=[pltpu.VMEM(s, F32) for s in scratch],
        compiler_params=pltpu.CompilerParams(vmem_limit_bytes=VMEM_LIMIT),
    )


def on_device(distances, neighbor_ids, edge_lengths, pivots):
    keep, send = call(pack_kernel, [(64, 128)] * 2, [], 1)(pivots, distances)
    got = lax.all_gather(send, "core")
    xy, *pieces = call(
        spread_kernel, [(NXY, XY_ROWS, 128)] + [(16, 128)] * 4, [(64, 128), (16, 128)], 4
    )(pivots, distances, keep, got, edge_lengths)
    pieces = [pieces[0]] + [
        lax.ppermute(pieces[m], "z", [(i, i ^ m) for i in range(NZ)]) for m in range(1, 4)
    ]
    xy = lax.all_to_all(xy, "row", 0, 0)
    zed, rows = call(gather_kernel, [(NZ, Z_ROWS, 128), (64, 128)], [], 5)(pivots, xy, *pieces)
    zed = lax.all_to_all(zed, "z", 0, 0)
    zed = lax.all_gather(zed, "core")
    (out,) = call(
        final_kernel,
        [(ROWS, COLS)],
        [(256, 128)] + [(16, 128)] * 4 + [(256, 128), (64, 128)],
        4,
    )(pivots, distances, rows, zed, neighbor_ids)
    return out


def solution(mesh):
    fine = Mesh(mesh.devices.reshape(16, 16, 2), ("row", "z", "core"))
    placed = (P("row", ("z", "core")), P(), P(None, ("row", "z", "core")), P())
    return jax.shard_map(
        on_device, mesh=fine, in_specs=placed, out_specs=P("row", ("z", "core")), check_vma=False
    )
```

time: 687 us -> 82.7 us (0.12)
  blocking collectives: 640 us -> 46.6 us
  local copies, waits for them, and re-layouts: 32.5 us -> 1.7 us
  Pallas kernels: 0 us -> 17.1 us
  starting transfers between devices: 0 us -> 12.9 us
  other arithmetic: 10.8 us -> 0 us
    psum x6 -> x0, blocking collectives: 516 us -> none  [broadcast(): return lax.psum(kept, axis)]
    all_gather x1 -> x2, blocking collectives: 124 us -> 19.4 us  [the longest x1 11 us: on_device(): zed = lax.all_gather(zed, 'core')]
    all_to_all x0 -> x1, blocking collectives: none -> 27.2 us  [on_device(): zed = lax.all_to_all(zed, 'z', 0, 0)]
    dynamic_slice x79 -> x0, local copies, waits for them, and re-layouts: 21.1 us -> none  [the longest x64 11.6 us: relax_one(): column = lax.dynamic_slice_in_dim(current, t, 1, 1)]
    pallas_call x0 -> x4, Pallas kernels: none -> 17.1 us  [the longest x1 14.3 us: on_device(): call(final_kernel, [(ROWS, COLS)], [(256, 128)] + [(16, 128)] * 4 + [(256...]
    ppermute x0 -> x3, starting transfers between devices: none -> 9.27 us  [on_device(): lax.ppermute(pieces[m], 'z', [(i, i ^ m) for i in range(NZ)])]
    slice x3 -> x0, local copies, waits for them, and re-layouts: 8.7 us -> none  [the longest x1 7.92 us: on_device(): len_rows = lax.dynamic_slice_in_dim(all_lengths[k], row_start, rows_here)]
  transfers between devices with their start and end apart: 0 -> 4, of which waited for: 0 -> 2; matrix products, arithmetic and copies ran while one was open for 0% -> 0% of each run, Pallas kernels for 0% -> 0%
where the time goes in v1:
time: 82.7 us; the launch traced here: 82.3 us
  blocking collectives  46.6 us (56%)
  Pallas kernels  17.1 us (21%)
  starting transfers between devices  12.9 us (16%)
  waiting for transfers between devices  3.96 us (5%)
  local copies, waits for them, and re-layouts  1.7 us (2%)
    all_to_all x1, blocking collectives, on_device(): zed = lax.all_to_all(zed, 'z', 0, 0)  27.2 us
    pallas_call x1, Pallas kernels, on_device(): call(final_kernel, [(ROWS, COLS)], [(256, 128)] + [(16, 128)] * 4 + [(256...  14.3 us
    all_gather x1, blocking collectives, on_device(): zed = lax.all_gather(zed, 'core')  11 us
    ppermute x3, starting transfers between devices, on_device(): lax.ppermute(pieces[m], 'z', [(i, i ^ m) for i in range(NZ)])  9.27 us
    all_gather x1, blocking collectives, on_device(): got = lax.all_gather(send, 'core')  8.38 us
    all_to_all x1, starting transfers between devices, on_device(): xy = lax.all_to_all(xy, 'row', 0, 0)  3.61 us
    ppermute x3, waiting for transfers between devices, on_device(): lax.ppermute(pieces[m], 'z', [(i, i ^ m) for i in range(NZ)])  3.41 us
    unnamed x9, local copies, waits for them, and re-layouts  1.7 us
  transfers between devices with their start and end apart: 4, of which 2 were waited for; matrix products, arithmetic and copies ran while one was open for 0% of the time, Pallas kernels for 0%

profile of v1, /device:TPU:1, one launch (start us, length us, event | category | flops | bytes accessed | tf_op | source)
XLA Modules:
  0.0 82.3 jit_solution(12429282441589934985)
XLA Ops:
  0.0 0.0 copy-start.3
  0.0 0.8 copy.6.lengths
  0.8 0.0 copy-done.3
  0.8 0.0 copy-start
  0.8 0.9 %copy-done = f32[256,128]{1,0:T(8,128)S(1)} copy-done((f32[256,128]{1,0:T(8,128)S(1)}, f32[256,128]{1,0:T(8,128)}, u32[]{:S(2)}) %copy-start) | copy-done | bytes 131096
  1.7 0.7 shard_map.46
  2.4 8.4 %all-gather = f32[128,128]{1,0:T(8,128)S(1)} all-gather(f32[64,128]{1,0:T(8,128)S(1)} %get-tuple-element.15), channel_id=2, replica_groups=mesh['row'=16,'z'=16,'core'=2] {'core'}, dimensions={0}, use_global_device_ids=true | all-gather | bytes 98304 | tf_op jit(solution)/shard_map/all_gather | solution.py:230
  10.8 1.6 %shard_map.47 = (f32[16,96,128]{2,1,0:T(8,128)}, f32[16,128]{1,0:T(8,128)S(1)}, f32[16,128]{1,0:T(8,128)S(1)}, f32[16,128]{1,0:T(8,128)S(1)}, f32[16,128]{1,0:T(8,128)S(1)}) custom-call(s32[2]{0:T(128)S(1)} %copy-done.3, f32[256,128]{1,0:T(8,128)S(1)} %copy-done, f32[64,128]{1,0:T(8,128)S(1)} %get-tuple-element.14.keep, f32[2,64,128]{2,1,0:T(8,128)S(1)} %bitcast.3, ...), custom_call_target="tpu_custom_call" | custom-call | tf_op jit(solution)/shard_map/pallas_call | solution.py:231
  12.3 3.6 %all-to-all-start = ((f32[16,96,128]{2,1,0:T(8,128)}), f32[16,96,128]{2,1,0:T(8,128)S(1)}, u32[]{:S(2)}, u32[]{:S(2)}) async-start(f32[16,96,128]{2,1,0:T(8,128)} %get-tuple-element.16), calls=%async_computation | async-start | bytes 1572864 | tf_op jit(solution)/shard_map/all_to_all | solution.py:237
  16.0 1.9 %collective-permute-start = (f32[16,128]{1,0:T(8,128)S(1)}, f32[16,128]{1,0:T(8,128)S(1)}, u32[]{:S(2)}, u32[]{:S(2)}) collective-permute-start(f32[16,128]{1,0:T(8,128)S(1)} %get-tuple-element.18), channel_id=1, source_target_pairs={{0,2},{2,0},{4,6},{6,4},{8,10},{10,8},{12,14},{14,12},{16,18},{18,... | collective-permute-start | bytes 24584 | tf_op jit(solution)/shard_map/ppermute | solution.py:235
  17.9 4.3 %collective-permute-start.1 = (f32[16,128]{1,0:T(8,128)S(1)}, f32[16,128]{1,0:T(8,128)S(1)}, u32[]{:S(2)}, u32[]{:S(2)}) collective-permute-start(f32[16,128]{1,0:T(8,128)S(1)} %get-tuple-element.19), channel_id=1, source_target_pairs={{0,4},{2,6},{4,0},{6,2},{8,12},{10,14},{12,8},{14,10},{16,20},{18,... | collective-permute-start | bytes 24584 | tf_op jit(solution)/shard_map/ppermute | solution.py:235
  22.2 3.1 %collective-permute-start.2 = (f32[16,128]{1,0:T(8,128)S(1)}, f32[16,128]{1,0:T(8,128)S(1)}, u32[]{:S(2)}, u32[]{:S(2)}) collective-permute-start(f32[16,128]{1,0:T(8,128)S(1)} %get-tuple-element.20), channel_id=1, source_target_pairs={{0,6},{2,4},{4,2},{6,0},{8,14},{10,12},{12,10},{14,8},{16,22},{18,... | collective-permute-start | bytes 24584 | tf_op jit(solution)/shard_map/ppermute | solution.py:235
  25.3 0.0 collective-permute-done.piece1
  25.3 0.0 collective-permute-done.1.piece2
  25.3 3.4 %collective-permute-done.2.piece3 = f32[16,128]{1,0:T(8,128)S(1)} collective-permute-done((f32[16,128]{1,0:T(8,128)S(1)}, f32[16,128]{1,0:T(8,128)S(1)}, u32[]{:S(2)}, u32[]{:S(2)}) %collective-permute-start.2) | collective-permute-done | bytes 8224 | tf_op jit(solution)/shard_map/ppermute | solution.py:235
  28.7 0.6 all-to-all-done.xy
  29.2 0.6 shard_map.48
  29.8 27.2 %all_to_all.10 = f32[16,48,128]{2,1,0:T(8,128)S(1)} all-to-all(f32[16,48,128]{2,1,0:T(8,128)S(1)} %get-tuple-element.22), channel_id=1, replica_groups=mesh['row'=16,'z'=16,'core'=2] {'z'}, dimensions={0} | all-to-all | bytes 786432 | tf_op jit(solution)/shard_map/all_to_all | solution.py:239
  57.0 0.0 copy-start.1
  57.0 0.0 copy-start.2
  57.0 11.0 %all-gather.1 = f32[32,48,128]{2,1,0:T(8,128)S(1)} all-gather(f32[16,48,128]{2,1,0:T(8,128)S(1)} %all_to_all.10), channel_id=3, replica_groups=mesh['row'=16,'z'=16,'core'=2] {'core'}, dimensions={0}, use_global_device_ids=true | all-gather | bytes 1179648 | tf_op jit(solution)/shard_map/all_gather | solution.py:240
  68.0 0.0 copy-done.1
  68.0 0.0 copy-done.2
  68.0 14.3 %shard_map.49 = f32[256,128]{1,0:T(8,128)} custom-call(s32[2]{0:T(128)S(1)} %copy-done.3, f32[256,128]{1,0:T(8,128)S(1)} %copy-done.1, f32[64,128]{1,0:T(8,128)S(1)} %get-tuple-element.21.rows, f32[2,16,48,128]{3,2,1,0:T(8,128)S(1)} %bitcast.2, s32[10,4096]{1,0:T(8,128)S(1)} %copy-done.2), custom_call_target="tpu_custom_call" | custom-call | tf_op jit(solution)/shard_map/pallas_call | solution.py:241
Async XLA Ops:
  0.0 0.8 copy-start.3
  0.8 0.9 %copy-start = (f32[256,128]{1,0:T(8,128)S(1)}, f32[256,128]{1,0:T(8,128)}, u32[]{:S(2)}) copy-start(f32[256,128]{1,0:T(8,128)} %dist.5) | copy-start | bytes 393220
  12.3 16.9 %all-to-all-start = ((f32[16,96,128]{2,1,0:T(8,128)}), f32[16,96,128]{2,1,0:T(8,128)S(1)}, u32[]{:S(2)}, u32[]{:S(2)}) async-start(f32[16,96,128]{2,1,0:T(8,128)} %get-tuple-element.16), calls=%async_computation | async-start | bytes 1572864 | tf_op jit(solution)/shard_map/all_to_all | solution.py:237
  16.0 9.3 %collective-permute-start = (f32[16,128]{1,0:T(8,128)S(1)}, f32[16,128]{1,0:T(8,128)S(1)}, u32[]{:S(2)}, u32[]{:S(2)}) collective-permute-start(f32[16,128]{1,0:T(8,128)S(1)} %get-tuple-element.18), channel_id=1, source_target_pairs={{0,2},{2,0},{4,6},{6,4},{8,10},{10,8},{12,14},{14,12},{16,18},{18,... | collective-permute-start | bytes 24584 | tf_op jit(solution)/shard_map/ppermute | solution.py:235
  17.9 7.4 %collective-permute-start.1 = (f32[16,128]{1,0:T(8,128)S(1)}, f32[16,128]{1,0:T(8,128)S(1)}, u32[]{:S(2)}, u32[]{:S(2)}) collective-permute-start(f32[16,128]{1,0:T(8,128)S(1)} %get-tuple-element.19), channel_id=1, source_target_pairs={{0,4},{2,6},{4,0},{6,2},{8,12},{10,14},{12,8},{14,10},{16,20},{18,... | collective-permute-start | bytes 24584 | tf_op jit(solution)/shard_map/ppermute | solution.py:235
  22.2 6.5 %collective-permute-start.2 = (f32[16,128]{1,0:T(8,128)S(1)}, f32[16,128]{1,0:T(8,128)S(1)}, u32[]{:S(2)}, u32[]{:S(2)}) collective-permute-start(f32[16,128]{1,0:T(8,128)S(1)} %get-tuple-element.20), channel_id=1, source_target_pairs={{0,6},{2,4},{4,2},{6,0},{8,14},{10,12},{12,10},{14,8},{16,22},{18,... | collective-permute-start | bytes 24584 | tf_op jit(solution)/shard_map/ppermute | solution.py:235
  57.0 11.0 %copy-start.1 = (f32[256,128]{1,0:T(8,128)S(1)}, f32[256,128]{1,0:T(8,128)}, u32[]{:S(2)}) copy-start(f32[256,128]{1,0:T(8,128)} %dist.5) | copy-start | bytes 393220
  57.0 11.0 %copy-start.2 = (s32[10,4096]{1,0:T(8,128)S(1)}, s32[10,4096]{1,0:T(8,128)}, u32[]{:S(2)}) copy-start(s32[10,4096]{1,0:T(8,128)} %ids.1) | copy-start | bytes 491524

commit v2 on v1

v2 whole, which is shorter than its diff:
```python
import jax
import jax.numpy as jnp
from jax import lax
from jax.experimental import pallas as pl
from jax.experimental.pallas import tpu as pltpu
from jax.sharding import Mesh, PartitionSpec as P

NEIGHBORS = 10
PIVOT = 32
ROWS = 256
COLS = 128
NXY = 16
NZ = 16
F32 = jnp.float32
INF = float("inf")
VMEM_LIMIT = 48 * 1024 * 1024

XY_RQ, XY_K, XY_L, XY_ROWS = 32, 64, 80, 96
Z_K, Z_L, Z_ROWS = 16, 32, 40


def lanes(rows):
    return lax.broadcasted_iota(jnp.int32, (rows, 128), 1)


def shift_lanes(x, amount):
    if isinstance(amount, int):
        return pltpu.roll(x, amount % 128, 1) if amount % 128 else x
    return pltpu.roll(x, lax.rem(amount + 1024, 128), 1)


def role(piv):
    core = lax.axis_index("core")
    p, q = piv[0], piv[1]
    first = core == 0
    return core, p, q, jnp.where(first, p, q), jnp.where(first, q, p)


def pack_kernel(piv, dist, keep, send, mt):
    _, _, _, mine, other = role(piv)
    for h in range(2):
        mt[:, 128 * h : 128 * h + 128] = dist[128 * h : 128 * h + 128, :].T
    for ref, pivot in ((keep, mine), (send, other)):
        off = pl.multiple_of(lax.rem(pivot, 4) * PIVOT, 32)
        for h in range(2):
            ref[32 * h : 32 * h + 32, :] = mt[pl.ds(off, 32), 128 * h : 128 * h + 128]


def spread_kernel(piv, dist, keep, got, lengths, xy, piece0, piece1, piece2, piece3, cols, held):
    core, p, q, mine, _ = role(piv)
    z = lax.axis_index("z")
    row = lax.axis_index("row")
    own = lax.rem(mine // 4, 2) == core
    cols[...] = jnp.where(own, keep[...], got[1 - core])
    for m, piece in enumerate((piece0, piece1, piece2, piece3)):
        part = lax.rem(z, 4) ^ m
        piece[...] = cols[pl.ds(pl.multiple_of(16 * part, 16), 16), :]
    part_of = lanes(16) // PIVOT
    corner = None
    for i, pivot in enumerate((p, q)):
        off = lax.rem(pivot, 8) * PIVOT
        half = off // 128
        for h in range(2):
            part = cols[pl.ds(pl.multiple_of(32 * half + 16 * h, 16), 16), :]
            part = shift_lanes(part, 64 * h + 32 * i - off)
            corner = part if corner is None else jnp.where(part_of == 2 * h + i, part, corner)
    held[...] = jnp.zeros_like(held)
    held[0:8, 0:NEIGHBORS] = lengths[...]
    own_lengths = shift_lanes(held[...].T[0:16], 8 * row)
    rows_p = dist[pl.ds(pl.multiple_of(lax.rem(p, 8) * PIVOT, 32), 32), :]
    rows_q = dist[pl.ds(pl.multiple_of(lax.rem(q, 8) * PIVOT, 32), 32), :]
    for d in range(NXY):
        xy[d, 0:XY_RQ] = rows_p
        xy[d, XY_RQ:XY_K] = rows_q
        xy[d, XY_K:XY_L] = corner
        xy[d, XY_L:XY_ROWS] = own_lengths


def gather_kernel(piv, xy, piece0, piece1, piece2, piece3, zchunk, rows):
    _, p, q, mine, _ = role(piv)
    z = lax.axis_index("z")
    row = lax.axis_index("row")
    row_p, row_q = p // 8, q // 8
    rows[0:32] = xy[row_p, 0:XY_RQ]
    rows[32:64] = xy[row_q, XY_RQ:XY_K]
    m = (mine // 8) ^ z
    piece = piece0[...]
    for i, ref in ((1, piece1), (2, piece2), (3, piece3)):
        piece = jnp.where(m == i, ref[...], piece)
    corner = jnp.where(lax.rem(lanes(16), 64) < 32, xy[row_p, XY_K:XY_L], xy[row_q, XY_K:XY_L])
    lengths = xy[0, XY_L:XY_ROWS]
    for d in range(1, NXY):
        lengths = jnp.maximum(lengths, xy[d, XY_L:XY_ROWS])
    group = lanes(8) // 8
    fixed = None
    for h in range(2):
        part = lengths[8 * h : 8 * h + 8]
        for g, src in ((0, row), (2, row_p), (3, row_q)):
            moved = shift_lanes(part, 32 * h + 8 * g - 8 * src)
            fixed = moved if fixed is None else jnp.where(group == 4 * h + g, moved, fixed)
    for d in range(NZ):
        low = shift_lanes(lengths[0:8], 8 - 8 * d)
        high = shift_lanes(lengths[8:16], 40 - 8 * d)
        zchunk[d, 0:Z_K] = piece
        zchunk[d, Z_K:Z_L] = corner
        zchunk[d, Z_L:Z_ROWS] = jnp.where(group == 1, low, jnp.where(group == 5, high, fixed))


def ids_kernel(piv, ids, lane_ids, sub_ids, held):
    p, q = piv[0], piv[1]
    row = lax.axis_index("row")
    col = 2 * lax.axis_index("z") + lax.axis_index("core")

    def block(base):
        x = ids[:, pl.ds(pl.multiple_of(base, 128), 128)].astype(F32)
        return jnp.concatenate([x, jnp.zeros((6, 128), F32)], 0)

    for h in range(2):
        lane_ids[h] = block(256 * row + 128 * h)
    pivot_p = shift_lanes(block(p // 4 * 128), 0 - lax.rem(p, 4) * PIVOT)
    pivot_q = shift_lanes(block(q // 4 * 128), 32 - lax.rem(q, 4) * PIVOT)
    pivots = jnp.where(lanes(16) < 32, pivot_p, pivot_q)
    lane_ids[2] = pivots
    held[...] = jnp.zeros_like(held)
    held[0:16] = block(128 * col)
    held[16:32] = pivots
    turned = held[...].T
    for tile in range(24):
        at = 8 * (tile % 16)
        for k in range(NEIGHBORS):
            lane = 16 * (tile // 16) + k
            sub_ids[tile, k] = jnp.broadcast_to(turned[at : at + 8, lane : lane + 1], (8, 128))


def final_kernel(piv, mt, rows, zed, lane_ids, sub_ids, out, lane_len, turned, ct, kt, rt, spread, new):
    p, q = piv[0], piv[1]
    row = lax.axis_index("row")
    z = lax.axis_index("z")
    core = lax.axis_index("core")
    col = 2 * z + core

    def lengths_at(first, count, group, at):
        parts = []
        for h in range(2):
            out = None
            for u in range(count):
                device = first + u
                tile = zed[lax.rem(device, 2), device // 2, Z_L:Z_ROWS]
                tile = shift_lanes(tile, at + 8 * u - 8 * group - 32 * h)
                out = tile if out is None else jnp.where(lanes(8) // 8 >= at // 8 + u, tile, out)
            parts.append(out)
        return jnp.concatenate(parts, 0)

    lane_len[0] = lengths_at(0, 16, 0, 0)
    lane_len[1] = lengths_at(16, 16, 0, 0)
    lane_len[2] = jnp.where(
        lanes(16) < 32,
        lengths_at(lax.rem(p, 8) * 4, 4, 2, 0),
        lengths_at(lax.rem(q, 8) * 4, 4, 3, 32),
    )
    square = jnp.concatenate([lengths_at(16 * core, 16, 1, 0), lane_len[2], jnp.zeros((96, 128), F32)], 0)
    turned[...] = square.T
    rt[:, 0:64] = rows[...].T

    group_p, group_q = p // 32 * 4, q // 32 * 4
    for i, (pivot, group) in enumerate(((p, group_p), (q, group_q))):
        for quarter in range(4):
            at = 32 * i + 16 * (quarter % 2)
            half = 128 * (quarter // 2)
            ct[at : at + 16, half : half + 128] = zed[i, group + quarter, 0:Z_K]
        corner = zed[i, pivot // 8, Z_K:Z_L]
        kt[32 * i : 32 * i + 16, :] = corner
        kt[32 * i + 16 : 32 * i + 32, :] = shift_lanes(corner, 64)

    lane = lanes(8)
    sub = lax.broadcasted_iota(jnp.int32, (8, 128), 0)
    vertex = [
        (256 * row + lane).astype(F32),
        (256 * row + 128 + lane).astype(F32),
        jnp.where(lane < 32, 32 * p + lane, jnp.where(lane < 64, 32 * q + lane - 32, -1)).astype(F32),
    ]

    def relax(entries, vertices, tile, base):
        own = (base + sub).astype(F32)
        at, shift = 8 * (tile % 16), 16 * (tile // 16)
        turn = turned[at : at + 8, :]
        entries = list(entries)
        for k in range(NEIGHBORS):
            own_ids = sub_ids[tile, k]
            own_len = jnp.broadcast_to(turn[:, shift + k : shift + k + 1], (8, 128))
            for n, kind in enumerate(vertices):
                there = jnp.where(own_ids == vertex[kind], own_len, INF)
                back = jnp.where(lane_ids[kind, k : k + 1, :] == own, lane_len[kind, k : k + 1, :], INF)
                entries[n] = jnp.minimum(entries[n], jnp.minimum(there, back))
        return [jnp.where(own == vertex[kind], 0.0, e) for kind, e in zip(vertices, entries)]

    left, right, corner = [], [], []
    for tile in range(8):
        at = 8 * tile
        base = (32 * p + at) if tile < 4 else (32 * q + at - 32)
        a, b, c = relax(
            [ct[at : at + 8, 0:128], ct[at : at + 8, 128:256], kt[at : at + 8, :]], (0, 1, 2), 16 + tile, base
        )
        left.append(a)
        right.append(b)
        corner.append(c)
    left = jnp.concatenate(left, 0)
    right = jnp.concatenate(right, 0)
    corner = jnp.concatenate(corner, 0)
    for tile in range(16):
        for t in range(4 * tile, 4 * tile + 4):
            step = corner[:, t : t + 1]
            left = jnp.minimum(left, step + left[t : t + 1, :])
            right = jnp.minimum(right, step + right[t : t + 1, :])
            corner = jnp.minimum(corner, step + corner[t : t + 1, :])
        at = 8 * tile
        a, b, c = relax(
            [mt[at : at + 8, 0:128], mt[at : at + 8, 128:256], rt[at : at + 8, :]], (0, 1, 2), tile, 128 * col + at
        )
        new[at : at + 8, 0:128] = a
        new[at : at + 8, 128:256] = b
        for t in range(2 * PIVOT):
            spread[t, at : at + 8, :] = jnp.broadcast_to(c[:, t : t + 1], (8, 128))
    ct[:, 0:128] = left
    ct[:, 128:256] = right

    def body(i, carry):
        at = pl.multiple_of(32 * i, 32)
        for half in (0, 128):
            here = new[pl.ds(at, 32), half : half + 128]
            for t in range(2 * PIVOT):
                here = jnp.minimum(here, spread[t, pl.ds(at, 32), :] + ct[t : t + 1, half : half + 128])
            new[pl.ds(at, 32), half : half + 128] = here
        return carry

    lax.fori_loop(0, COLS // 32, body, 0)
    for h in range(2):
        out[128 * h : 128 * h + 128, :] = new[:, 128 * h : 128 * h + 128].T


VM = pl.BlockSpec(memory_space=pltpu.VMEM)
SM = pl.BlockSpec(memory_space=pltpu.SMEM)


def call(kernel, shapes, scratch, n_in):
    return pl.pallas_call(
        kernel,
        out_shape=[jax.ShapeDtypeStruct(s, F32) for s in shapes],
        in_specs=[SM] + [VM] * n_in,
        out_specs=[VM] * len(shapes),
        scratch_shapes=[pltpu.VMEM(s, F32) for s in scratch],
        compiler_params=pltpu.CompilerParams(vmem_limit_bytes=VMEM_LIMIT),
    )


FINAL_SCRATCH = [(3, 16, 128), (128, 128), (64, 256), (64, 128), (128, 128), (64, 128, 128), (128, 256)]


def on_device(distances, neighbor_ids, edge_lengths, pivots):
    keep, send, mt = call(pack_kernel, [(64, 128)] * 2 + [(COLS, ROWS)], [], 1)(pivots, distances)
    got = lax.all_gather(send, "core")
    xy, *pieces = call(
        spread_kernel, [(NXY, XY_ROWS, 128)] + [(16, 128)] * 4, [(64, 128), (128, 128)], 4
    )(pivots, distances, keep, got, edge_lengths.T)
    pieces = [pieces[0]] + [
        lax.ppermute(pieces[m], "z", [(i, i ^ m) for i in range(NZ)]) for m in range(1, 4)
    ]
    lane_ids, sub_ids = call(ids_kernel, [(3, 16, 128), (24, NEIGHBORS, 8, 128)], [(128, 128)], 1)(
        pivots, neighbor_ids
    )
    xy = lax.all_to_all(xy, "row", 0, 0)
    zed, rows = call(gather_kernel, [(NZ, Z_ROWS, 128), (64, 128)], [], 5)(pivots, xy, *pieces)
    zed = lax.all_to_all(zed, "z", 0, 0)
    zed = lax.all_gather(zed, "core")
    (out,) = call(final_kernel, [(ROWS, COLS)], FINAL_SCRATCH, 5)(pivots, mt, rows, zed, lane_ids, sub_ids)
    return out


def solution(mesh):
    fine = Mesh(mesh.devices.reshape(16, 16, 2), ("row", "z", "core"))
    placed = (P("row", ("z", "core")), P(), P(None, ("row", "z", "core")), P())
    return jax.shard_map(
        on_device, mesh=fine, in_specs=placed, out_specs=P("row", ("z", "core")), check_vma=False
    )
```

time: 82.7 us -> 76.7 us (0.927)
  blocking collectives: 46.6 us -> 18.6 us
  starting transfers between devices: 12.9 us -> 25.2 us
  waiting for transfers between devices: 3.96 us -> 16.2 us
  Pallas kernels: 17.1 us -> 14 us
    all_to_all x1 -> x0, blocking collectives: 27.2 us -> none  [on_device(): zed = lax.all_to_all(zed, 'z', 0, 0)]
    all_to_all x0 -> x1, waiting for transfers between devices: none -> 12.3 us  [on_device(): zed = lax.all_to_all(zed, 'z', 0, 0)]
    all_to_all x0 -> x1, starting transfers between devices: none -> 12.3 us  [on_device(): zed = lax.all_to_all(zed, 'z', 0, 0)]
    pallas_call x2 -> x3, Pallas kernels: 14.9 us -> 11 us  [the longest x1 9.11 us: on_device(): call(final_kernel, [(ROWS, COLS)], FINAL_SCRATCH, 5)]
    all_gather x1, blocking collectives: 11 us -> 10.2 us  [on_device(): zed = lax.all_gather(zed, 'core')]
    unnamed x9 -> x10, local copies, waits for them, and re-layouts: 1.7 us -> 2.25 us
  transfers between devices with their start and end apart: 4 -> 5, of which waited for: 2 -> 3; matrix products, arithmetic and copies ran while one was open for 0% -> 0% of each run, Pallas kernels for 0% -> 2%
where the time goes in v2:
time: 76.7 us; the launch traced here: 76.3 us
  starting transfers between devices  25.2 us (33%)
  blocking collectives  18.6 us (24%)
  waiting for transfers between devices  16.2 us (21%)
  Pallas kernels  14 us (18%)
  local copies, waits for them, and re-layouts  2.25 us (3%)
    all_to_all x1, waiting for transfers between devices, on_device(): zed = lax.all_to_all(zed, 'z', 0, 0)  12.3 us
    all_to_all x1, starting transfers between devices, on_device(): zed = lax.all_to_all(zed, 'z', 0, 0)  12.3 us
    all_gather x1, blocking collectives, on_device(): zed = lax.all_gather(zed, 'core')  10.2 us
    ppermute x3, starting transfers between devices, on_device(): lax.ppermute(pieces[m], 'z', [(i, i ^ m) for i in range(NZ)])  9.27 us
    pallas_call x1, Pallas kernels, on_device(): call(final_kernel, [(ROWS, COLS)], FINAL_SCRATCH, 5)  9.11 us
    all_gather x1, blocking collectives, on_device(): got = lax.all_gather(send, 'core')  8.38 us
    all_to_all x1, starting transfers between devices, on_device(): xy = lax.all_to_all(xy, 'row', 0, 0)  3.61 us
    ppermute x3, waiting for transfers between devices, on_device(): lax.ppermute(pieces[m], 'z', [(i, i ^ m) for i in range(NZ)])  3.41 us
  transfers between devices with their start and end apart: 5, of which 3 were waited for; matrix products, arithmetic and copies ran while one was open for 0% of the time, Pallas kernels for 2%

profile of v2, /device:TPU:1, one launch (start us, length us, event | category | flops | bytes accessed | tf_op | source)
XLA Modules:
  0.0 76.3 jit_solution(11333423384710788684)
XLA Ops:
  0.0 0.0 copy-start
  0.0 0.9 %copy-done = f32[256,128]{1,0:T(8,128)S(1)} copy-done((f32[256,128]{1,0:T(8,128)S(1)}, f32[256,128]{1,0:T(8,128)}, u32[]{:S(2)}) %copy-start) | copy-done | bytes 131096
  0.9 0.0 copy-start.2
  0.9 0.7 copy-done.2
  1.6 0.6 shard_map.46
  2.2 8.4 %all-gather = f32[128,128]{1,0:T(8,128)S(1)} all-gather(f32[64,128]{1,0:T(8,128)S(1)} %get-tuple-element.19), channel_id=2, replica_groups=mesh['row'=16,'z'=16,'core'=2] {'core'}, dimensions={0}, use_global_device_ids=true | all-gather | bytes 98304 | tf_op jit(solution)/shard_map/all_gather | solution.py:261
  10.6 0.0 copy-start.4
  10.6 0.7 copy-done.4
  11.3 1.6 %shard_map.47 = (f32[16,96,128]{2,1,0:T(8,128)}, f32[16,128]{1,0:T(8,128)S(1)}, f32[16,128]{1,0:T(8,128)S(1)}, f32[16,128]{1,0:T(8,128)S(1)}, f32[16,128]{1,0:T(8,128)S(1)}) custom-call(s32[2]{0:T(128)S(1)} %copy-done.2, f32[256,128]{1,0:T(8,128)S(1)} %copy-done, f32[64,128]{1,0:T(8,128)S(1)} %get-tuple-element.18.keep, f32[2,64,128]{2,1,0:T(8,128)S(1)} %bitcast.4, ...), custom_call_target="tpu_custom_call" | custom-call | tf_op jit(solution)/shard_map/pallas_call | solution.py:262
  12.9 3.6 %all-to-all-start = ((f32[16,96,128]{2,1,0:T(8,128)}), f32[16,96,128]{2,1,0:T(8,128)S(1)}, u32[]{:S(2)}, u32[]{:S(2)}) async-start(f32[16,96,128]{2,1,0:T(8,128)} %get-tuple-element.20), calls=%async_computation | async-start | bytes 1572864 | tf_op jit(solution)/shard_map/all_to_all | solution.py:271
  16.5 1.9 %collective-permute-start = (f32[16,128]{1,0:T(8,128)S(1)}, f32[16,128]{1,0:T(8,128)S(1)}, u32[]{:S(2)}, u32[]{:S(2)}) collective-permute-start(f32[16,128]{1,0:T(8,128)S(1)} %get-tuple-element.22), channel_id=1, source_target_pairs={{0,2},{2,0},{4,6},{6,4},{8,10},{10,8},{12,14},{14,12},{16,18},{18,... | collective-permute-start | bytes 24584 | tf_op jit(solution)/shard_map/ppermute | solution.py:266
  18.4 4.3 %collective-permute-start.1 = (f32[16,128]{1,0:T(8,128)S(1)}, f32[16,128]{1,0:T(8,128)S(1)}, u32[]{:S(2)}, u32[]{:S(2)}) collective-permute-start(f32[16,128]{1,0:T(8,128)S(1)} %get-tuple-element.23), channel_id=1, source_target_pairs={{0,4},{2,6},{4,0},{6,2},{8,12},{10,14},{12,8},{14,10},{16,20},{18,... | collective-permute-start | bytes 24584 | tf_op jit(solution)/shard_map/ppermute | solution.py:266
  22.7 0.0 copy-start.3
  22.7 3.1 %collective-permute-start.2 = (f32[16,128]{1,0:T(8,128)S(1)}, f32[16,128]{1,0:T(8,128)S(1)}, u32[]{:S(2)}, u32[]{:S(2)}) collective-permute-start(f32[16,128]{1,0:T(8,128)S(1)} %get-tuple-element.24), channel_id=1, source_target_pairs={{0,6},{2,4},{4,2},{6,0},{8,14},{10,12},{12,10},{14,8},{16,22},{18,... | collective-permute-start | bytes 24584 | tf_op jit(solution)/shard_map/ppermute | solution.py:266
  25.8 0.0 collective-permute-done.piece1
  25.8 0.0 collective-permute-done.1.piece2
  25.8 3.4 %collective-permute-done.2.piece3 = f32[16,128]{1,0:T(8,128)S(1)} collective-permute-done((f32[16,128]{1,0:T(8,128)S(1)}, f32[16,128]{1,0:T(8,128)S(1)}, u32[]{:S(2)}, u32[]{:S(2)}) %collective-permute-start.2) | collective-permute-done | bytes 8224 | tf_op jit(solution)/shard_map/ppermute | solution.py:266
  29.2 0.5 all-to-all-done.xy
  29.8 0.0 copy-done.3
  29.8 1.4 %shard_map.48 = (f32[16,40,128]{2,1,0:T(8,128)}, f32[64,128]{1,0:T(8,128)S(1)}) custom-call(s32[2]{0:T(128)S(1)} %copy-done.3, f32[16,96,128]{2,1,0:T(8,128)S(1)} %all-to-all-done.xy, f32[16,128]{1,0:T(8,128)S(1)} %get-tuple-element.21.piece0, f32[16,128]{1,0:T(8,128)S(1)} %collective-permute-done.piece1, f32[16,128]{1,0:T(8,128)S(1)} %collective-permute-done.1.piece2, ...), custom_call_target="tpu_custom_call" | custom-call | tf_op jit(solution)/shard_map/pallas_call | solution.py:272
  31.2 0.0 copy-start.1
  31.2 12.3 %all-to-all-start.1 = ((f32[16,40,128]{2,1,0:T(8,128)}), f32[16,40,128]{2,1,0:T(8,128)S(1)}, u32[]{:S(2)}, u32[]{:S(2)}) async-start(f32[16,40,128]{2,1,0:T(8,128)} %get-tuple-element.26), calls=%async_computation.1 | async-start | bytes 655360 | tf_op jit(solution)/shard_map/all_to_all | solution.py:273
  43.5 0.0 copy-done.1
  43.5 1.2 %shard_map.49 = (f32[3,16,128]{2,1,0:T(8,128)S(1)}, f32[24,10,8,128]{3,2,1,0:T(8,128)S(1)}) custom-call(s32[2]{0:T(128)S(1)} %copy-done.3, s32[10,4096]{1,0:T(8,128)S(1)} %copy-done.1), custom_call_target="tpu_custom_call" | custom-call | tf_op jit(solution)/shard_map/pallas_call | solution.py:268
  44.7 12.3 %all-to-all-done.1 = f32[16,40,128]{2,1,0:T(8,128)S(1)} async-done(((f32[16,40,128]{2,1,0:T(8,128)}), f32[16,40,128]{2,1,0:T(8,128)S(1)}, u32[]{:S(2)}, u32[]{:S(2)}) %all-to-all-start.1) | async-done | bytes 327712 | tf_op jit(solution)/shard_map/all_to_all | solution.py:273
  57.0 10.2 %all-gather.1 = f32[32,40,128]{2,1,0:T(8,128)S(1)} all-gather(f32[16,40,128]{2,1,0:T(8,128)S(1)} %all-to-all-done.1), channel_id=3, replica_groups=mesh['row'=16,'z'=16,'core'=2] {'core'}, dimensions={0}, use_global_device_ids=true | all-gather | bytes 983040 | tf_op jit(solution)/shard_map/all_gather | solution.py:274
  67.2 9.1 %shard_map.50 = f32[256,128]{1,0:T(8,128)} custom-call(s32[2]{0:T(128)S(1)} %copy-done.3, f32[128,256]{1,0:T(8,128)S(1)} %get-tuple-element.17.mt, f32[64,128]{1,0:T(8,128)S(1)} %get-tuple-element.25.rows, f32[2,16,40,128]{3,2,1,0:T(8,128)S(1)} %bitcast.3, f32[3,16,128]{2,1,0:T(8,128)S(1)} %get-tuple-element.27.lane_ids, ...), custom_call_target="tpu_custom_call" | custom-call | tf_op jit(solution)/shard_map/pallas_call | solution.py:275
Async XLA Ops:
  0.0 0.9 %copy-start = (f32[256,128]{1,0:T(8,128)S(1)}, f32[256,128]{1,0:T(8,128)}, u32[]{:S(2)}) copy-start(f32[256,128]{1,0:T(8,128)} %dist.3) | copy-start | bytes 393220
  0.9 0.7 copy-start.2
  10.6 0.7 copy-start.4
  12.9 16.9 %all-to-all-start = ((f32[16,96,128]{2,1,0:T(8,128)}), f32[16,96,128]{2,1,0:T(8,128)S(1)}, u32[]{:S(2)}, u32[]{:S(2)}) async-start(f32[16,96,128]{2,1,0:T(8,128)} %get-tuple-element.20), calls=%async_computation | async-start | bytes 1572864 | tf_op jit(solution)/shard_map/all_to_all | solution.py:271
  16.5 9.3 %collective-permute-start = (f32[16,128]{1,0:T(8,128)S(1)}, f32[16,128]{1,0:T(8,128)S(1)}, u32[]{:S(2)}, u32[]{:S(2)}) collective-permute-start(f32[16,128]{1,0:T(8,128)S(1)} %get-tuple-element.22), channel_id=1, source_target_pairs={{0,2},{2,0},{4,6},{6,4},{8,10},{10,8},{12,14},{14,12},{16,18},{18,... | collective-permute-start | bytes 24584 | tf_op jit(solution)/shard_map/ppermute | solution.py:266
  18.4 7.4 %collective-permute-start.1 = (f32[16,128]{1,0:T(8,128)S(1)}, f32[16,128]{1,0:T(8,128)S(1)}, u32[]{:S(2)}, u32[]{:S(2)}) collective-permute-start(f32[16,128]{1,0:T(8,128)S(1)} %get-tuple-element.23), channel_id=1, source_target_pairs={{0,4},{2,6},{4,0},{6,2},{8,12},{10,14},{12,8},{14,10},{16,20},{18,... | collective-permute-start | bytes 24584 | tf_op jit(solution)/shard_map/ppermute | solution.py:266
  22.7 7.0 %copy-start.3 = (s32[2]{0:T(128)S(1)}, s32[2]{0:T(128)}, u32[]{:S(2)}) copy-start(s32[2]{0:T(128)} %piv.9) | copy-start | bytes 28
  22.7 6.5 %collective-permute-start.2 = (f32[16,128]{1,0:T(8,128)S(1)}, f32[16,128]{1,0:T(8,128)S(1)}, u32[]{:S(2)}, u32[]{:S(2)}) collective-permute-start(f32[16,128]{1,0:T(8,128)S(1)} %get-tuple-element.24), channel_id=1, source_target_pairs={{0,6},{2,4},{4,2},{6,0},{8,14},{10,12},{12,10},{14,8},{16,22},{18,... | collective-permute-start | bytes 24584 | tf_op jit(solution)/shard_map/ppermute | solution.py:266
  31.2 12.3 %copy-start.1 = (s32[10,4096]{1,0:T(8,128)S(1)}, s32[10,4096]{1,0:T(8,128)}, u32[]{:S(2)}) copy-start(s32[10,4096]{1,0:T(8,128)} %ids.1) | copy-start | bytes 491524
  31.2 25.8 %all-to-all-start.1 = ((f32[16,40,128]{2,1,0:T(8,128)}), f32[16,40,128]{2,1,0:T(8,128)S(1)}, u32[]{:S(2)}, u32[]{:S(2)}) async-start(f32[16,40,128]{2,1,0:T(8,128)} %get-tuple-element.26), calls=%async_computation.1 | async-start | bytes 655360 | tf_op jit(solution)/shard_map/all_to_all | solution.py:273

commit v3 on v2

--- a/solution.py
+++ b/solution.py
@@ -106,7 +106,7 @@
         zchunk[d, Z_L:Z_ROWS] = jnp.where(group == 1, low, jnp.where(group == 5, high, fixed))
 
 
-def ids_kernel(piv, ids, lane_ids, sub_ids, held):
+def ids_kernel(piv, ids, lane_ids, sub_ids, onehot, held):
     p, q = piv[0], piv[1]
     row = lax.axis_index("row")
     col = 2 * lax.axis_index("z") + lax.axis_index("core")
@@ -130,9 +130,56 @@
         for k in range(NEIGHBORS):
             lane = 16 * (tile // 16) + k
             sub_ids[tile, k] = jnp.broadcast_to(turned[at : at + 8, lane : lane + 1], (8, 128))
-
-
-def final_kernel(piv, mt, rows, zed, lane_ids, sub_ids, out, lane_len, turned, ct, kt, rt, spread, new):
+    term = lax.broadcasted_iota(jnp.int32, (256, 128), 0)
+
+    def fill(t, carry):
+        picked = (lax.rem(term, 64) == t) & (term < 192)
+        onehot[:, pl.ds(pl.multiple_of(128 * t, 128), 128)] = jnp.where(picked, 1.0, 0.0).astype(jnp.bfloat16)
+        return carry
+
+    lax.fori_loop(0, 2 * PIVOT, fill, 0)
+
+
+def over_lanes(x, lane):
+    return jnp.broadcast_to(x[:, lane : lane + 1], (8, 128))
+
+
+def over_rows(x, row):
+    return jnp.broadcast_to(x[row : row + 1, :], (8, 128))
+
+
+def eliminate(state, b):
+    corner = state[2]
+    columns = [over_lanes(corner[b], 8 * b + j) for j in range(8)]
+    rows = [state[kind][b] for kind in range(3)]
+    for j in range(8):
+        for u in range(j + 1, 8):
+            columns[u] = jnp.minimum(columns[u], columns[j] + over_rows(columns[u], j))
+        rows = [jnp.minimum(r, columns[j] + over_rows(r, j)) for r in rows]
+    closed = [[over_rows(r, j) for j in range(8)] for r in rows]
+    for i in range(8):
+        if i == b:
+            continue
+        columns = [over_lanes(corner[i], 8 * b + j) for j in range(8)]
+        for kind in range(3):
+            paths = [columns[j] + closed[kind][j] for j in range(8)]
+            while len(paths) > 1:
+                paths = [jnp.minimum(paths[n], paths[n + 1]) for n in range(0, len(paths), 2)]
+            state[kind][i] = jnp.minimum(state[kind][i], paths[0])
+    for kind in range(3):
+        state[kind][b] = rows[kind]
+
+
+def thirds(x):
+    x = x[:, 0:64]
+    high = x.astype(jnp.bfloat16)
+    rest = x - high.astype(F32)
+    mid = rest.astype(jnp.bfloat16)
+    low = (rest - mid.astype(F32)).astype(jnp.bfloat16)
+    return jnp.concatenate([high, mid, low, low], 1)
+
+
+def final_kernel(piv, mt, rows, zed, lane_ids, sub_ids, onehot, out, lane_len, turned, ct, kt, rt, spread, new):
     p, q = piv[0], piv[1]
     row = lax.axis_index("row")
     z = lax.axis_index("z")
@@ -194,42 +241,43 @@
                 entries[n] = jnp.minimum(entries[n], jnp.minimum(there, back))
         return [jnp.where(own == vertex[kind], 0.0, e) for kind, e in zip(vertices, entries)]
 
-    left, right, corner = [], [], []
+    state = [[], [], []]
     for tile in range(8):
         at = 8 * tile
         base = (32 * p + at) if tile < 4 else (32 * q + at - 32)
-        a, b, c = relax(
+        done = relax(
             [ct[at : at + 8, 0:128], ct[at : at + 8, 128:256], kt[at : at + 8, :]], (0, 1, 2), 16 + tile, base
         )
-        left.append(a)
-        right.append(b)
-        corner.append(c)
-    left = jnp.concatenate(left, 0)
-    right = jnp.concatenate(right, 0)
-    corner = jnp.concatenate(corner, 0)
-    for tile in range(16):
-        for t in range(4 * tile, 4 * tile + 4):
-            step = corner[:, t : t + 1]
-            left = jnp.minimum(left, step + left[t : t + 1, :])
-            right = jnp.minimum(right, step + right[t : t + 1, :])
-            corner = jnp.minimum(corner, step + corner[t : t + 1, :])
+        for kind in range(3):
+            state[kind].append(done[kind])
+    for b in range(8):
+        eliminate(state, b)
+        if b < 4:
+            for tile in range(4 * b, 4 * b + 4):
+                at = 8 * tile
+                entries = [mt[at : at + 8, 0:128], mt[at : at + 8, 128:256], rt[at : at + 8, :]]
+                entries = relax(entries, (0, 1, 2), tile, 128 * col + at)
+                new[at : at + 8, 0:128] = entries[0]
+                new[at : at + 8, 128:256] = entries[1]
+                rt[at : at + 8, :] = entries[2]
+        else:
+            if b == 4:
+                parts = thirds(rt[...])
+            for c in range(4 * b - 16, 4 * b - 12):
+                spread[:, 512 * c : 512 * c + 512] = jnp.dot(
+                    parts, onehot[:, 512 * c : 512 * c + 512], preferred_element_type=F32
+                )
+    for tile in range(8):
         at = 8 * tile
-        a, b, c = relax(
-            [mt[at : at + 8, 0:128], mt[at : at + 8, 128:256], rt[at : at + 8, :]], (0, 1, 2), tile, 128 * col + at
-        )
-        new[at : at + 8, 0:128] = a
-        new[at : at + 8, 128:256] = b
-        for t in range(2 * PIVOT):
-            spread[t, at : at + 8, :] = jnp.broadcast_to(c[:, t : t + 1], (8, 128))
-    ct[:, 0:128] = left
-    ct[:, 128:256] = right
+        ct[at : at + 8, 0:128] = state[0][tile]
+        ct[at : at + 8, 128:256] = state[1][tile]
 
     def body(i, carry):
         at = pl.multiple_of(32 * i, 32)
         for half in (0, 128):
             here = new[pl.ds(at, 32), half : half + 128]
             for t in range(2 * PIVOT):
-                here = jnp.minimum(here, spread[t, pl.ds(at, 32), :] + ct[t : t + 1, half : half + 128])
+                here = jnp.minimum(here, spread[pl.ds(at, 32), 128 * t : 128 * t + 128] + ct[t : t + 1, half : half + 128])
             new[pl.ds(at, 32), half : half + 128] = here
         return carry
 
@@ -245,7 +293,7 @@
 def call(kernel, shapes, scratch, n_in):
     return pl.pallas_call(
         kernel,
-        out_shape=[jax.ShapeDtypeStruct(s, F32) for s in shapes],
+        out_shape=[s if isinstance(s, jax.ShapeDtypeStruct) else jax.ShapeDtypeStruct(s, F32) for s in shapes],
         in_specs=[SM] + [VM] * n_in,
         out_specs=[VM] * len(shapes),
         scratch_shapes=[pltpu.VMEM(s, F32) for s in scratch],
@@ -253,7 +301,8 @@
     )
 
 
-FINAL_SCRATCH = [(3, 16, 128), (128, 128), (64, 256), (64, 128), (128, 128), (64, 128, 128), (128, 256)]
+FINAL_SCRATCH = [(3, 16, 128), (128, 128), (64, 256), (64, 128), (128, 128), (128, 8192), (128, 256)]
+ONEHOT = jax.ShapeDtypeStruct((256, 2 * PIVOT * 128), jnp.bfloat16)
 
 
 def on_device(distances, neighbor_ids, edge_lengths, pivots):
@@ -265,14 +314,16 @@
     pieces = [pieces[0]] + [
         lax.ppermute(pieces[m], "z", [(i, i ^ m) for i in range(NZ)]) for m in range(1, 4)
     ]
-    lane_ids, sub_ids = call(ids_kernel, [(3, 16, 128), (24, NEIGHBORS, 8, 128)], [(128, 128)], 1)(
-        pivots, neighbor_ids
-    )
+    lane_ids, sub_ids, onehot = call(
+        ids_kernel, [(3, 16, 128), (24, NEIGHBORS, 8, 128), ONEHOT], [(128, 128)], 1
+    )(pivots, neighbor_ids)
     xy = lax.all_to_all(xy, "row", 0, 0)
     zed, rows = call(gather_kernel, [(NZ, Z_ROWS, 128), (64, 128)], [], 5)(pivots, xy, *pieces)
     zed = lax.all_to_all(zed, "z", 0, 0)
     zed = lax.all_gather(zed, "core")
-    (out,) = call(final_kernel, [(ROWS, COLS)], FINAL_SCRATCH, 5)(pivots, mt, rows, zed, lane_ids, sub_ids)
+    (out,) = call(final_kernel, [(ROWS, COLS)], FINAL_SCRATCH, 6)(
+        pivots, mt, rows, zed, lane_ids, sub_ids, onehot
+    )
     return out
 
 

time: 76.7 us -> 75.1 us (0.979)
  local copies, waits for them, and re-layouts: 2.25 us -> 8.64 us
  waiting for transfers between devices: 16.2 us -> 11.3 us
  Pallas kernels: 14 us -> 11 us
    unnamed x10 -> x18, local copies, waits for them, and re-layouts: 2.25 us -> 8.64 us
    all_to_all x1, waiting for transfers between devices: 12.3 us -> 7.29 us  [on_device(): zed = lax.all_to_all(zed, 'z', 0, 0)]
    pallas_call x2, Pallas kernels: 10.3 us -> 7.39 us  [the longest x1 4.75 us: on_device(): call(final_kernel, [(ROWS, COLS)], FINAL_SCRATCH, 6)]
  transfers between devices with their start and end apart: 5 -> 5, of which waited for: 3 -> 3; matrix products, arithmetic and copies ran while one was open for 0% -> 0% of each run, Pallas kernels for 2% -> 4%
where the time goes in v3:
time: 75.1 us; the launch traced here: 74.6 us
  starting transfers between devices  25 us (33%)
  blocking collectives  18.6 us (25%)
  waiting for transfers between devices  11.3 us (15%)
  Pallas kernels  11 us (15%)
  local copies, waits for them, and re-layouts  8.64 us (12%)
    all_to_all x1, starting transfers between devices, on_device(): zed = lax.all_to_all(zed, 'z', 0, 0)  12.1 us
    all_gather x1, blocking collectives, on_device(): zed = lax.all_gather(zed, 'core')  10.2 us
    ppermute x3, starting transfers between devices, on_device(): lax.ppermute(pieces[m], 'z', [(i, i ^ m) for i in range(NZ)])  9.27 us
    unnamed x18, local copies, waits for them, and re-layouts  8.64 us
    all_gather x1, blocking collectives, on_device(): got = lax.all_gather(send, 'core')  8.38 us
    all_to_all x1, waiting for transfers between devices, on_device(): zed = lax.all_to_all(zed, 'z', 0, 0)  7.29 us
    pallas_call x1, Pallas kernels, on_device(): call(final_kernel, [(ROWS, COLS)], FINAL_SCRATCH, 6)  4.75 us
    all_to_all x1, starting transfers between devices, on_device(): xy = lax.all_to_all(xy, 'row', 0, 0)  3.61 us
  transfers between devices with their start and end apart: 5, of which 3 were waited for; matrix products, arithmetic and copies ran while one was open for 0% of the time, Pallas kernels for 4%

profile of v3, /device:TPU:1, one launch (start us, length us, event | category | flops | bytes accessed | tf_op | source)
XLA Modules:
  0.0 74.6 jit_solution(10402912918381907487)
XLA Ops:
  0.0 0.0 copy-start.2
  0.0 0.9 %copy-done.2 = f32[256,128]{1,0:T(8,128)S(1)} copy-done((f32[256,128]{1,0:T(8,128)S(1)}, f32[256,128]{1,0:T(8,128)}, u32[]{:S(2)}) %copy-start.2) | copy-done | bytes 131096
  0.9 0.0 copy-start.4
  0.9 0.7 copy-done.4
  1.6 0.0 copy-start.7
  1.6 0.6 shard_map.46
  2.2 8.4 %all-gather = f32[128,128]{1,0:T(8,128)S(1)} all-gather(f32[64,128]{1,0:T(8,128)S(1)} %get-tuple-element.20), channel_id=2, replica_groups=mesh['row'=16,'z'=16,'core'=2] {'core'}, dimensions={0}, use_global_device_ids=true | all-gather | bytes 98304 | tf_op jit(solution)/shard_map/all_gather | solution.py:310
  10.6 0.0 copy-start.8
  10.6 0.7 copy-done.8
  11.3 1.6 %shard_map.47 = (f32[16,96,128]{2,1,0:T(8,128)}, f32[16,128]{1,0:T(8,128)S(1)}, f32[16,128]{1,0:T(8,128)S(1)}, f32[16,128]{1,0:T(8,128)S(1)}, f32[16,128]{1,0:T(8,128)S(1)}) custom-call(s32[2]{0:T(128)S(1)} %copy-done.4, f32[256,128]{1,0:T(8,128)S(1)} %copy-done.2, f32[64,128]{1,0:T(8,128)S(1)} %get-tuple-element.19.keep, f32[2,64,128]{2,1,0:T(8,128)S(1)} %bitcast.4, ...), custom_call_target="tpu_custom_call" | custom-call | tf_op jit(solution)/shard_map/pallas_call | solution.py:311
  12.9 3.6 %all-to-all-start = ((f32[16,96,128]{2,1,0:T(8,128)}), f32[16,96,128]{2,1,0:T(8,128)S(1)}, u32[]{:S(2)}, u32[]{:S(2)}) async-start(f32[16,96,128]{2,1,0:T(8,128)} %get-tuple-element.21), calls=%async_computation | async-start | bytes 1572864 | tf_op jit(solution)/shard_map/all_to_all | solution.py:320
  16.5 1.9 %collective-permute-start = (f32[16,128]{1,0:T(8,128)S(1)}, f32[16,128]{1,0:T(8,128)S(1)}, u32[]{:S(2)}, u32[]{:S(2)}) collective-permute-start(f32[16,128]{1,0:T(8,128)S(1)} %get-tuple-element.23), channel_id=1, source_target_pairs={{0,2},{2,0},{4,6},{6,4},{8,10},{10,8},{12,14},{14,12},{16,18},{18,... | collective-permute-start | bytes 24584 | tf_op jit(solution)/shard_map/ppermute | solution.py:315
  18.4 4.3 %collective-permute-start.1 = (f32[16,128]{1,0:T(8,128)S(1)}, f32[16,128]{1,0:T(8,128)S(1)}, u32[]{:S(2)}, u32[]{:S(2)}) collective-permute-start(f32[16,128]{1,0:T(8,128)S(1)} %get-tuple-element.24), channel_id=1, source_target_pairs={{0,4},{2,6},{4,0},{6,2},{8,12},{10,14},{12,8},{14,10},{16,20},{18,... | collective-permute-start | bytes 24584 | tf_op jit(solution)/shard_map/ppermute | solution.py:315
  22.7 3.1 %collective-permute-start.2 = (f32[16,128]{1,0:T(8,128)S(1)}, f32[16,128]{1,0:T(8,128)S(1)}, u32[]{:S(2)}, u32[]{:S(2)}) collective-permute-start(f32[16,128]{1,0:T(8,128)S(1)} %get-tuple-element.25), channel_id=1, source_target_pairs={{0,6},{2,4},{4,2},{6,0},{8,14},{10,12},{12,10},{14,8},{16,22},{18,... | collective-permute-start | bytes 24584 | tf_op jit(solution)/shard_map/ppermute | solution.py:315
  25.8 0.0 collective-permute-done.piece1
  25.8 0.0 collective-permute-done.1.piece2
  25.8 3.4 %collective-permute-done.2.piece3 = f32[16,128]{1,0:T(8,128)S(1)} collective-permute-done((f32[16,128]{1,0:T(8,128)S(1)}, f32[16,128]{1,0:T(8,128)S(1)}, u32[]{:S(2)}, u32[]{:S(2)}) %collective-permute-start.2) | collective-permute-done | bytes 8224 | tf_op jit(solution)/shard_map/ppermute | solution.py:315
  29.2 0.6 all-to-all-done.xy
  29.8 0.0 copy-start.5
  29.8 0.7 copy-done.5
  30.4 1.4 %shard_map.48 = (f32[16,40,128]{2,1,0:T(8,128)}, f32[64,128]{1,0:T(8,128)S(1)}) custom-call(s32[2]{0:T(128)S(1)} %copy-done.5, f32[16,96,128]{2,1,0:T(8,128)S(1)} %all-to-all-done.xy, f32[16,128]{1,0:T(8,128)S(1)} %get-tuple-element.22.piece0, f32[16,128]{1,0:T(8,128)S(1)} %collective-permute-done.piece1, f32[16,128]{1,0:T(8,128)S(1)} %collective-permute-done.1.piece2, ...), custom_call_target="tpu_custom_call" | custom-call | tf_op jit(solution)/shard_map/pallas_call | solution.py:321
  31.8 12.1 %all-to-all-start.1 = ((f32[16,40,128]{2,1,0:T(8,128)}), f32[16,40,128]{2,1,0:T(8,128)S(1)}, u32[]{:S(2)}, u32[]{:S(2)}) async-start(f32[16,40,128]{2,1,0:T(8,128)} %get-tuple-element.27), calls=%async_computation.1 | async-start | bytes 655360 | tf_op jit(solution)/shard_map/all_to_all | solution.py:322
  44.0 0.0 copy-start.3
  44.0 0.9 %copy-done.3 = s32[10,4096]{1,0:T(8,128)S(1)} copy-done((s32[10,4096]{1,0:T(8,128)S(1)}, s32[10,4096]{1,0:T(8,128)}, u32[]{:S(2)}) %copy-start.3) | copy-done | bytes 163864
  44.9 0.0 copy-start.6
  44.9 0.7 copy-done.6
  45.6 2.6 %shard_map.49 = (f32[3,16,128]{2,1,0:T(8,128)S(1)}, f32[24,10,8,128]{3,2,1,0:T(8,128)S(1)}, bf16[256,8192]{1,0:T(8,128)(2,1)S(1)}) custom-call(s32[2]{0:T(128)S(1)} %copy-done.6, s32[10,4096]{1,0:T(8,128)S(1)} %copy-done.3), custom_call_target="tpu_custom_call" | custom-call | tf_op jit(solution)/shard_map/pallas_call | solution.py:317
  48.3 0.0 copy-start
  48.3 1.9 %copy-done = bf16[256,8192]{1,0:T(8,128)(2,1)} copy-done((bf16[256,8192]{1,0:T(8,128)(2,1)}, bf16[256,8192]{1,0:T(8,128)(2,1)S(1)}, u32[]{:S(2)}) %copy-start) | copy-done | bytes 4194328
  50.2 7.3 %all-to-all-done.1 = f32[16,40,128]{2,1,0:T(8,128)S(1)} async-done(((f32[16,40,128]{2,1,0:T(8,128)}), f32[16,40,128]{2,1,0:T(8,128)S(1)}, u32[]{:S(2)}, u32[]{:S(2)}) %all-to-all-start.1) | async-done | bytes 327712 | tf_op jit(solution)/shard_map/all_to_all | solution.py:322
  57.5 10.2 %all-gather.1 = f32[32,40,128]{2,1,0:T(8,128)S(1)} all-gather(f32[16,40,128]{2,1,0:T(8,128)S(1)} %all-to-all-done.1), channel_id=3, replica_groups=mesh['row'=16,'z'=16,'core'=2] {'core'}, dimensions={0}, use_global_device_ids=true | all-gather | bytes 983040 | tf_op jit(solution)/shard_map/all_gather | solution.py:323
  67.7 0.0 copy-done.7
  67.7 0.0 copy-start.1
  67.7 2.2 %copy-done.1 = bf16[256,8192]{1,0:T(8,128)(2,1)S(1)} copy-done((bf16[256,8192]{1,0:T(8,128)(2,1)S(1)}, bf16[256,8192]{1,0:T(8,128)(2,1)}, u32[]{:S(2)}) %copy-start.1) | copy-done | bytes 4194328
  69.9 4.8 %shard_map.50 = f32[256,128]{1,0:T(8,128)} custom-call(s32[2]{0:T(128)S(1)} %copy-done.7, f32[128,256]{1,0:T(8,128)S(1)} %get-tuple-element.18.mt, f32[64,128]{1,0:T(8,128)S(1)} %get-tuple-element.26.rows, f32[2,16,40,128]{3,2,1,0:T(8,128)S(1)} %bitcast.3, f32[3,16,128]{2,1,0:T(8,128)S(1)} %get-tuple-element.28.lane_ids, ...), custom_call_target="tpu_custom_call" | custom-call | tf_op jit(solution)/shard_map/pallas_call | solution.py:324
Async XLA Ops:
  0.0 0.9 %copy-start.2 = (f32[256,128]{1,0:T(8,128)S(1)}, f32[256,128]{1,0:T(8,128)}, u32[]{:S(2)}) copy-start(f32[256,128]{1,0:T(8,128)} %dist.3) | copy-start | bytes 393220
  0.9 0.7 copy-start.4
  1.6 66.1 %copy-start.7 = (s32[2]{0:T(128)S(1)}, s32[2]{0:T(128)}, u32[]{:S(2)}) copy-start(s32[2]{0:T(128)} %piv.9) | copy-start | bytes 28
  10.6 0.7 copy-start.8
  12.9 16.9 %all-to-all-start = ((f32[16,96,128]{2,1,0:T(8,128)}), f32[16,96,128]{2,1,0:T(8,128)S(1)}, u32[]{:S(2)}, u32[]{:S(2)}) async-start(f32[16,96,128]{2,1,0:T(8,128)} %get-tuple-element.21), calls=%async_computation | async-start | bytes 1572864 | tf_op jit(solution)/shard_map/all_to_all | solution.py:320
  16.5 9.3 %collective-permute-start = (f32[16,128]{1,0:T(8,128)S(1)}, f32[16,128]{1,0:T(8,128)S(1)}, u32[]{:S(2)}, u32[]{:S(2)}) collective-permute-start(f32[16,128]{1,0:T(8,128)S(1)} %get-tuple-element.23), channel_id=1, source_target_pairs={{0,2},{2,0},{4,6},{6,4},{8,10},{10,8},{12,14},{14,12},{16,18},{18,... | collective-permute-start | bytes 24584 | tf_op jit(solution)/shard_map/ppermute | solution.py:315
  18.4 7.4 %collective-permute-start.1 = (f32[16,128]{1,0:T(8,128)S(1)}, f32[16,128]{1,0:T(8,128)S(1)}, u32[]{:S(2)}, u32[]{:S(2)}) collective-permute-start(f32[16,128]{1,0:T(8,128)S(1)} %get-tuple-element.24), channel_id=1, source_target_pairs={{0,4},{2,6},{4,0},{6,2},{8,12},{10,14},{12,8},{14,10},{16,20},{18,... | collective-permute-start | bytes 24584 | tf_op jit(solution)/shard_map/ppermute | solution.py:315
  22.7 6.5 %collective-permute-start.2 = (f32[16,128]{1,0:T(8,128)S(1)}, f32[16,128]{1,0:T(8,128)S(1)}, u32[]{:S(2)}, u32[]{:S(2)}) collective-permute-start(f32[16,128]{1,0:T(8,128)S(1)} %get-tuple-element.25), channel_id=1, source_target_pairs={{0,6},{2,4},{4,2},{6,0},{8,14},{10,12},{12,10},{14,8},{16,22},{18,... | collective-permute-start | bytes 24584 | tf_op jit(solution)/shard_map/ppermute | solution.py:315
  29.8 0.7 copy-start.5
  31.8 25.7 %all-to-all-start.1 = ((f32[16,40,128]{2,1,0:T(8,128)}), f32[16,40,128]{2,1,0:T(8,128)S(1)}, u32[]{:S(2)}, u32[]{:S(2)}) async-start(f32[16,40,128]{2,1,0:T(8,128)} %get-tuple-element.27), calls=%async_computation.1 | async-start | bytes 655360 | tf_op jit(solution)/shard_map/all_to_all | solution.py:322
  44.0 1.0 %copy-start.3 = (s32[10,4096]{1,0:T(8,128)S(1)}, s32[10,4096]{1,0:T(8,128)}, u32[]{:S(2)}) copy-start(s32[10,4096]{1,0:T(8,128)} %ids.1) | copy-start | bytes 491524
  44.9 0.7 copy-start.6
  48.3 2.0 %copy-start = (bf16[256,8192]{1,0:T(8,128)(2,1)}, bf16[256,8192]{1,0:T(8,128)(2,1)S(1)}, u32[]{:S(2)}) copy-start(bf16[256,8192]{1,0:T(8,128)(2,1)S(1)} %get-tuple-element.30.onehot) | copy-start | bytes 12582916
  67.7 2.2 %copy-start.1 = (bf16[256,8192]{1,0:T(8,128)(2,1)S(1)}, bf16[256,8192]{1,0:T(8,128)(2,1)}, u32[]{:S(2)}) copy-start(bf16[256,8192]{1,0:T(8,128)(2,1)} %copy-done) | copy-start | bytes 12582916

commit v4 on v3

--- a/solution.py
+++ b/solution.py
@@ -13,10 +13,10 @@
 NZ = 16
 F32 = jnp.float32
 INF = float("inf")
-VMEM_LIMIT = 48 * 1024 * 1024
-
-XY_RQ, XY_K, XY_L, XY_ROWS = 32, 64, 80, 96
-Z_K, Z_L, Z_ROWS = 16, 32, 40
+
+XY_K, XY_L, XY_ROWS = 4, 8, 16
+Z_L, Z_K, Z_ROWS = 16, 20, 24
+HOLDERS = 8
 
 
 def lanes(rows):
@@ -29,87 +29,86 @@
     return pltpu.roll(x, lax.rem(amount + 1024, 128), 1)
 
 
-def role(piv):
-    core = lax.axis_index("core")
+def place():
+    return lax.axis_index("row"), 4 * lax.axis_index("zh") + lax.axis_index("zl"), lax.axis_index("core")
+
+
+def pack_kernel(piv, dist, lengths, mt, scatter, panel, own_lengths, block, held, sems):
+    row, _, _ = place()
+    copies = [
+        pltpu.make_async_copy(dist, block, sems.at[0]),
+        pltpu.make_async_copy(lengths, held, sems.at[1]),
+    ]
+    for copy in copies:
+        copy.start()
+    for copy in copies:
+        copy.wait()
+    for h in range(2):
+        mt[:, 128 * h : 128 * h + 128] = block[128 * h : 128 * h + 128, :].T
+    for i in range(2):
+        off = lax.rem(piv[i], 4) * PIVOT
+        for n in range(0, HOLDERS, 2):
+            lines = mt[pl.ds(pl.multiple_of(off + 4 * n, 8), 8), :]
+            for m in range(2):
+                for h in range(2):
+                    at = 8 * i + 4 * h
+                    scatter[n + m, at : at + 4, :] = lines[4 * m : 4 * m + 4, 128 * h : 128 * h + 128]
+        panel[32 * i : 32 * i + 32, :] = block[pl.ds(pl.multiple_of(lax.rem(piv[i], 8) * PIVOT, 32), 32), :]
+    spaced = jnp.concatenate([held[...], jnp.zeros((8, 128 - NEIGHBORS), F32)], 1)
+    own_lengths[...] = shift_lanes(spaced, 16 * lax.rem(row, 8))
+
+
+def spread_kernel(piv, got, own_lengths, xy, piece):
     p, q = piv[0], piv[1]
-    first = core == 0
-    return core, p, q, jnp.where(first, p, q), jnp.where(first, q, p)
-
-
-def pack_kernel(piv, dist, keep, send, mt):
-    _, _, _, mine, other = role(piv)
-    for h in range(2):
-        mt[:, 128 * h : 128 * h + 128] = dist[128 * h : 128 * h + 128, :].T
-    for ref, pivot in ((keep, mine), (send, other)):
-        off = pl.multiple_of(lax.rem(pivot, 4) * PIVOT, 32)
-        for h in range(2):
-            ref[32 * h : 32 * h + 32, :] = mt[pl.ds(off, 32), 128 * h : 128 * h + 128]
-
-
-def spread_kernel(piv, dist, keep, got, lengths, xy, piece0, piece1, piece2, piece3, cols, held):
-    core, p, q, mine, _ = role(piv)
-    z = lax.axis_index("z")
-    row = lax.axis_index("row")
-    own = lax.rem(mine // 4, 2) == core
-    cols[...] = jnp.where(own, keep[...], got[1 - core])
-    for m, piece in enumerate((piece0, piece1, piece2, piece3)):
-        part = lax.rem(z, 4) ^ m
-        piece[...] = cols[pl.ds(pl.multiple_of(16 * part, 16), 16), :]
-    part_of = lanes(16) // PIVOT
     corner = None
     for i, pivot in enumerate((p, q)):
-        off = lax.rem(pivot, 8) * PIVOT
-        half = off // 128
-        for h in range(2):
-            part = cols[pl.ds(pl.multiple_of(32 * half + 16 * h, 16), 16), :]
-            part = shift_lanes(part, 64 * h + 32 * i - off)
-            corner = part if corner is None else jnp.where(part_of == 2 * h + i, part, corner)
-    held[...] = jnp.zeros_like(held)
-    held[0:8, 0:NEIGHBORS] = lengths[...]
-    own_lengths = shift_lanes(held[...].T[0:16], 8 * row)
-    rows_p = dist[pl.ds(pl.multiple_of(lax.rem(p, 8) * PIVOT, 32), 32), :]
-    rows_q = dist[pl.ds(pl.multiple_of(lax.rem(q, 8) * PIVOT, 32), 32), :]
+        holder = lax.rem(pivot // 8, 4) * 2 + lax.rem(pivot // 4, 2)
+        mine = got[holder, 8 * i : 8 * i + 8]
+        piece[8 * i : 8 * i + 8, :] = mine
+        for j, other in enumerate((p, q)):
+            half = jnp.where(lax.rem(other // 4, 2) == 0, mine, pltpu.roll(mine, 4, 0))
+            half = shift_lanes(half, 64 * i + 32 * j - lax.rem(other, 4) * PIVOT)
+            corner = half if corner is None else jnp.where(lanes(8) // PIVOT == 2 * i + j, half, corner)
+    corner = pltpu.roll(corner, 4, 0)
     for d in range(NXY):
-        xy[d, 0:XY_RQ] = rows_p
-        xy[d, XY_RQ:XY_K] = rows_q
-        xy[d, XY_K:XY_L] = corner
-        xy[d, XY_L:XY_ROWS] = own_lengths
-
-
-def gather_kernel(piv, xy, piece0, piece1, piece2, piece3, zchunk, rows):
-    _, p, q, mine, _ = role(piv)
-    z = lax.axis_index("z")
-    row = lax.axis_index("row")
+        xy[d, 0:XY_L] = corner
+        xy[d, XY_L:XY_ROWS] = own_lengths[...]
+
+
+def gather_kernel(piv, xy, piece, zchunk, turned):
+    p, q = piv[0], piv[1]
+    row, _, _ = place()
     row_p, row_q = p // 8, q // 8
-    rows[0:32] = xy[row_p, 0:XY_RQ]
-    rows[32:64] = xy[row_q, XY_RQ:XY_K]
-    m = (mine // 8) ^ z
-    piece = piece0[...]
-    for i, ref in ((1, piece1), (2, piece2), (3, piece3)):
-        piece = jnp.where(m == i, ref[...], piece)
-    corner = jnp.where(lax.rem(lanes(16), 64) < 32, xy[row_p, XY_K:XY_L], xy[row_q, XY_K:XY_L])
-    lengths = xy[0, XY_L:XY_ROWS]
-    for d in range(1, NXY):
-        lengths = jnp.maximum(lengths, xy[d, XY_L:XY_ROWS])
+    corner = jnp.where(lax.rem(lanes(8) // PIVOT, 2) == 0, xy[row_p, 0:XY_L], xy[row_q, 0:XY_L])
+    low = xy[0, XY_L:XY_ROWS]
+    high = xy[8, XY_L:XY_ROWS]
+    for d in range(1, 8):
+        low = jnp.maximum(low, xy[d, XY_L:XY_ROWS])
+        high = jnp.maximum(high, xy[8 + d, XY_L:XY_ROWS])
+    turned[...] = jnp.concatenate([low, high, jnp.zeros((112, 128), F32)], 0).T
     group = lanes(8) // 8
-    fixed = None
-    for h in range(2):
-        part = lengths[8 * h : 8 * h + 8]
-        for g, src in ((0, row), (2, row_p), (3, row_q)):
-            moved = shift_lanes(part, 32 * h + 8 * g - 8 * src)
-            fixed = moved if fixed is None else jnp.where(group == 4 * h + g, moved, fixed)
+
+    def take(device, at, lengths):
+        start = 16 * (device % 8)
+        from_lane = 8 * (device // 8)
+        first = turned[pl.ds(pl.multiple_of(start, 8), 8), :]
+        second = turned[pl.ds(pl.multiple_of(start + 8, 8), 8), :]
+        for g, part in ((0, first), (1, pltpu.roll(first, 4, 0)), (2, second)):
+            moved = shift_lanes(part, 32 * g + 8 * at - from_lane)
+            lengths = moved if lengths is None else jnp.where(group == 4 * g + at, moved, lengths)
+        return lengths
+
+    fixed = take(row_q, 3, take(row_p, 2, take(row, 0, None)))
+    upper = lax.broadcasted_iota(jnp.int32, (8, 128), 0) < 4
     for d in range(NZ):
-        low = shift_lanes(lengths[0:8], 8 - 8 * d)
-        high = shift_lanes(lengths[8:16], 40 - 8 * d)
-        zchunk[d, 0:Z_K] = piece
-        zchunk[d, Z_K:Z_L] = corner
-        zchunk[d, Z_L:Z_ROWS] = jnp.where(group == 1, low, jnp.where(group == 5, high, fixed))
+        zchunk[d, 0:Z_L] = piece[...]
+        zchunk[d, Z_L:Z_ROWS] = jnp.where(upper, take(d, 1, fixed), corner)
 
 
 def ids_kernel(piv, ids, lane_ids, sub_ids, onehot, held):
     p, q = piv[0], piv[1]
-    row = lax.axis_index("row")
-    col = 2 * lax.axis_index("z") + lax.axis_index("core")
+    row, z, core = place()
+    col = 2 * z + core
 
     def block(base):
         x = ids[:, pl.ds(pl.multiple_of(base, 128), 128)].astype(F32)
@@ -181,22 +180,21 @@
 
 def final_kernel(piv, mt, rows, zed, lane_ids, sub_ids, onehot, out, lane_len, turned, ct, kt, rt, spread, new):
     p, q = piv[0], piv[1]
-    row = lax.axis_index("row")
-    z = lax.axis_index("z")
-    core = lax.axis_index("core")
+    row, z, core = place()
     col = 2 * z + core
+    upper = lax.broadcasted_iota(jnp.int32, (8, 128), 0) < 4
 
     def lengths_at(first, count, group, at):
         parts = []
-        for h in range(2):
+        for g in range(3):
             out = None
             for u in range(count):
                 device = first + u
                 tile = zed[lax.rem(device, 2), device // 2, Z_L:Z_ROWS]
-                tile = shift_lanes(tile, at + 8 * u - 8 * group - 32 * h)
+                tile = shift_lanes(tile, at + 8 * u - 8 * group - 32 * g)
                 out = tile if out is None else jnp.where(lanes(8) // 8 >= at // 8 + u, tile, out)
             parts.append(out)
-        return jnp.concatenate(parts, 0)
+        return jnp.concatenate([jnp.where(upper, parts[0], pltpu.roll(parts[1], 4, 0)), parts[2]], 0)
 
     lane_len[0] = lengths_at(0, 16, 0, 0)
     lane_len[1] = lengths_at(16, 16, 0, 0)
@@ -209,15 +207,14 @@
     turned[...] = square.T
     rt[:, 0:64] = rows[...].T
 
-    group_p, group_q = p // 32 * 4, q // 32 * 4
-    for i, (pivot, group) in enumerate(((p, group_p), (q, group_q))):
-        for quarter in range(4):
-            at = 32 * i + 16 * (quarter % 2)
-            half = 128 * (quarter // 2)
-            ct[at : at + 16, half : half + 128] = zed[i, group + quarter, 0:Z_K]
-        corner = zed[i, pivot // 8, Z_K:Z_L]
-        kt[32 * i : 32 * i + 16, :] = corner
-        kt[32 * i + 16 : 32 * i + 32, :] = shift_lanes(corner, 64)
+    for i, pivot in enumerate((p, q)):
+        for n in range(HOLDERS):
+            holder = 4 * (pivot // 32) + n // 2
+            at = 32 * i + 4 * n
+            part = zed[n % 2, holder, 8 * i : 8 * i + 8]
+            ct[at : at + 4, 0:128] = part[0:4]
+            ct[at : at + 4, 128:256] = part[4:8]
+            kt[at : at + 4, :] = shift_lanes(zed[n % 2, holder, Z_L:Z_ROWS], 64 * i)[4:8]
 
     lane = lanes(8)
     sub = lax.broadcasted_iota(jnp.int32, (8, 128), 0)
@@ -288,16 +285,18 @@
 
 VM = pl.BlockSpec(memory_space=pltpu.VMEM)
 SM = pl.BlockSpec(memory_space=pltpu.SMEM)
-
-
-def call(kernel, shapes, scratch, n_in):
+ANY = pl.BlockSpec(memory_space=pl.ANY)
+MIB = 1024 * 1024
+
+
+def call(kernel, shapes, scratch, ins, mib):
     return pl.pallas_call(
         kernel,
         out_shape=[s if isinstance(s, jax.ShapeDtypeStruct) else jax.ShapeDtypeStruct(s, F32) for s in shapes],
-        in_specs=[SM] + [VM] * n_in,
+        in_specs=[SM] + ins,
         out_specs=[VM] * len(shapes),
-        scratch_shapes=[pltpu.VMEM(s, F32) for s in scratch],
-        compiler_params=pltpu.CompilerParams(vmem_limit_bytes=VMEM_LIMIT),
+        scratch_shapes=[pltpu.VMEM(s, F32) if isinstance(s, tuple) else s for s in scratch],
+        compiler_params=pltpu.CompilerParams(vmem_limit_bytes=mib * MIB),
     )
 
 
@@ -306,30 +305,36 @@
 
 
 def on_device(distances, neighbor_ids, edge_lengths, pivots):
-    keep, send, mt = call(pack_kernel, [(64, 128)] * 2 + [(COLS, ROWS)], [], 1)(pivots, distances)
-    got = lax.all_gather(send, "core")
-    xy, *pieces = call(
-        spread_kernel, [(NXY, XY_ROWS, 128)] + [(16, 128)] * 4, [(64, 128), (128, 128)], 4
-    )(pivots, distances, keep, got, edge_lengths.T)
-    pieces = [pieces[0]] + [
-        lax.ppermute(pieces[m], "z", [(i, i ^ m) for i in range(NZ)]) for m in range(1, 4)
-    ]
+    mt, scatter, panel, own_lengths = call(
+        pack_kernel,
+        [(COLS, ROWS), (HOLDERS, 16, 128), (64, 128), (8, 128)],
+        [(ROWS, COLS), (8, NEIGHBORS), pltpu.SemaphoreType.DMA((2,))],
+        [ANY, ANY],
+        8,
+    )(pivots, distances, edge_lengths.T)
+    home = jnp.repeat(pivots // 8, PIVOT)[:, None] ^ lax.axis_index("row")
+    for m in (1, 2, 4, 8):
+        other = lax.ppermute(panel, "row", [(i, i ^ m) for i in range(NXY)])
+        panel = jnp.where((home & m) != 0, other, panel)
+    scatter = lax.all_to_all(scatter, ("zl", "core"), 0, 0)
+    xy, piece = call(spread_kernel, [(NXY, XY_ROWS, 128), (16, 128)], [], [VM] * 2, 8)(
+        pivots, scatter, own_lengths
+    )
     lane_ids, sub_ids, onehot = call(
-        ids_kernel, [(3, 16, 128), (24, NEIGHBORS, 8, 128), ONEHOT], [(128, 128)], 1
+        ids_kernel, [(3, 16, 128), (24, NEIGHBORS, 8, 128), ONEHOT], [(128, 128)], [VM], 16
     )(pivots, neighbor_ids)
     xy = lax.all_to_all(xy, "row", 0, 0)
-    zed, rows = call(gather_kernel, [(NZ, Z_ROWS, 128), (64, 128)], [], 5)(pivots, xy, *pieces)
-    zed = lax.all_to_all(zed, "z", 0, 0)
+    (zed,) = call(gather_kernel, [(NZ, Z_ROWS, 128)], [(128, 128)], [VM] * 2, 8)(pivots, xy, piece)
+    zed = lax.all_to_all(zed, ("zh", "zl"), 0, 0)
     zed = lax.all_gather(zed, "core")
-    (out,) = call(final_kernel, [(ROWS, COLS)], FINAL_SCRATCH, 6)(
-        pivots, mt, rows, zed, lane_ids, sub_ids, onehot
+    (out,) = call(final_kernel, [(ROWS, COLS)], FINAL_SCRATCH, [VM] * 6, 24)(
+        pivots, mt, panel, zed, lane_ids, sub_ids, onehot
     )
     return out
 
 
 def solution(mesh):
-    fine = Mesh(mesh.devices.reshape(16, 16, 2), ("row", "z", "core"))
-    placed = (P("row", ("z", "core")), P(), P(None, ("row", "z", "core")), P())
-    return jax.shard_map(
-        on_device, mesh=fine, in_specs=placed, out_specs=P("row", ("z", "core")), check_vma=False
-    )
+    fine = Mesh(mesh.devices.reshape(16, 4, 4, 2), ("row", "zh", "zl", "core"))
+    cols = ("zh", "zl", "core")
+    placed = (P("row", cols), P(), P(None, ("row", *cols)), P())
+    return jax.shard_map(on_device, mesh=fine, in_specs=placed, out_specs=P("row", cols), check_vma=False)

time: 75.1 us -> 74.2 us (0.988)
  starting transfers between devices: 25 us -> 38.5 us
  blocking collectives: 18.6 us -> 5.49 us
  waiting for transfers between devices: 11.3 us -> 6.26 us
  local copies, waits for them, and re-layouts: 8.64 us -> 10.6 us
  other arithmetic: 0 us -> 0.98 us
    all_to_all x1 -> x2, starting transfers between devices: 12.1 us -> 22.4 us  [the longest x1 12.3 us: on_device(): zed = lax.all_to_all(zed, ('zh', 'zl'), 0, 0)]
    all_gather x1 -> x0, blocking collectives: 8.38 us -> none  [on_device(): got = lax.all_gather(send, 'core')]
    all_to_all x1 -> x2, waiting for transfers between devices: 7.29 us -> 2.34 us  [the longest x1 2.34 us: on_device(): scatter = lax.all_to_all(scatter, ('zl', 'core'), 0, 0)]
    all_gather x1, blocking collectives: 10.2 us -> 5.49 us  [on_device(): zed = lax.all_gather(zed, 'core')]
    ppermute x3 -> x4, starting transfers between devices: 9.27 us -> 12.1 us  [on_device(): other = lax.ppermute(panel, 'row', [(i, i ^ m) for i in range(NXY)])]
    unnamed x18 -> x20, local copies, waits for them, and re-layouts: 8.64 us -> 9.94 us
    ppermute x3 -> x4, waiting for transfers between devices: 3.41 us -> 2.25 us  [on_device(): other = lax.ppermute(panel, 'row', [(i, i ^ m) for i in range(NXY)])]
    all_to_all x1, waiting for transfers between devices: 0.56 us -> 1.67 us  [on_device(): xy = lax.all_to_all(xy, 'row', 0, 0)]
  transfers between devices with their start and end apart: 5 -> 7, of which waited for: 3 -> 3; matrix products, arithmetic and copies ran while one was open for 0% -> 2% of each run, Pallas kernels for 4% -> 7%
where the time goes in v4:
time: 74.2 us; the launch traced here: 73.6 us
  starting transfers between devices  38.5 us (52%)
  Pallas kernels  11.6 us (16%)
  local copies, waits for them, and re-layouts  10.6 us (14%)
  waiting for transfers between devices  6.26 us (8%)
  blocking collectives  5.49 us (7%)
  other arithmetic  0.98 us (1%)
    all_to_all x1, starting transfers between devices, on_device(): zed = lax.all_to_all(zed, ('zh', 'zl'), 0, 0)  12.3 us
    ppermute x4, starting transfers between devices, on_device(): other = lax.ppermute(panel, 'row', [(i, i ^ m) for i in range(NXY)])  12.1 us
    all_to_all x1, starting transfers between devices, on_device(): scatter = lax.all_to_all(scatter, ('zl', 'core'), 0, 0)  10.1 us
    unnamed x20, local copies, waits for them, and re-layouts  9.94 us
    all_gather x1, blocking collectives, on_device(): zed = lax.all_gather(zed, 'core')  5.49 us
    pallas_call x1, Pallas kernels, on_device(): call(final_kernel, [(ROWS, COLS)], FINAL_SCRATCH, [VM] * 6, 24)  4.72 us
    all_to_all x1, starting transfers between devices, on_device(): xy = lax.all_to_all(xy, 'row', 0, 0)  3.99 us
    pallas_call x1, Pallas kernels, on_device(): call(ids_kernel, [(3, 16, 128), (24, NEIGHBORS, 8, 128), ONEHOT], [(128,...  2.64 us
  transfers between devices with their start and end apart: 7, of which 3 were waited for; matrix products, arithmetic and copies ran while one was open for 2% of the time, Pallas kernels for 7%

profile of v4, /device:TPU:1, one launch (start us, length us, event | category | flops | bytes accessed | tf_op | source)
XLA Modules:
  0.0 73.6 jit_solution(7960345443086995586)
XLA Ops:
  0.0 0.0 copy-start.3
  0.0 0.9 %copy-done.3 = f32[256,128]{1,0:T(8,128)S(1)} copy-done((f32[256,128]{1,0:T(8,128)S(1)}, f32[256,128]{1,0:T(8,128)}, u32[]{:S(2)}) %copy-start.3) | copy-done | bytes 131096
  0.9 0.0 copy-start.4
  0.9 0.7 copy-done.4
  1.6 0.0 copy-start.9
  1.6 0.7 copy-done.9
  2.2 1.5 %shard_map.46 = (f32[128,256]{1,0:T(8,128)S(1)}, f32[8,16,128]{2,1,0:T(8,128)}, f32[64,128]{1,0:T(8,128)S(1)}, f32[8,128]{1,0:T(8,128)S(1)}) custom-call(s32[2]{0:T(128)S(1)} %copy-done.4, f32[256,128]{1,0:T(8,128)S(1)} %copy-done.3, f32[8,10]{1,0:T(8,128)S(1)} %bitcast.3), custom_call_target="tpu_custom_call" | custom-call | tf_op jit(solution)/shard_map/pallas_call | solution.py:308
  3.7 10.1 %all-to-all-start = ((f32[8,16,128]{2,1,0:T(8,128)}), f32[8,16,128]{2,1,0:T(8,128)S(1)}, u32[]{:S(2)}, u32[]{:S(2)}) async-start(f32[8,16,128]{2,1,0:T(8,128)} %get-tuple-element.16), calls=%async_computation | async-start | bytes 131072 | tf_op jit(solution)/shard_map/all_to_all | solution.py:319
  13.9 1.9 %collective-permute-start = (f32[64,128]{1,0:T(8,128)S(1)}, f32[64,128]{1,0:T(8,128)S(1)}, u32[]{:S(2)}, u32[]{:S(2)}) collective-permute-start(f32[64,128]{1,0:T(8,128)S(1)} %get-tuple-element.15), channel_id=1, source_target_pairs={{0,32},{32,0},{64,96},{96,64},{128,160},{160,128},{192,224},{224,1... | collective-permute-start | bytes 98312 | tf_op jit(solution)/shard_map/ppermute | solution.py:317
  15.8 0.7 and_compare_fusion.3
  16.5 0.1 broadcast_in_dim.38
  16.6 0.1 ne.70
  16.7 2.3 %all-to-all-done.got = f32[8,16,128]{2,1,0:T(8,128)S(1)} async-done(((f32[8,16,128]{2,1,0:T(8,128)}), f32[8,16,128]{2,1,0:T(8,128)S(1)}, u32[]{:S(2)}, u32[]{:S(2)}) %all-to-all-start) | async-done | bytes 65568 | tf_op jit(solution)/shard_map/all_to_all | solution.py:319
  19.0 0.0 copy-start.5
  19.0 0.7 copy-done.5
  19.6 1.3 %shard_map.47 = (f32[16,16,128]{2,1,0:T(8,128)}, f32[16,128]{1,0:T(8,128)S(1)}) custom-call(s32[2]{0:T(128)S(1)} %copy-done.5, f32[8,16,128]{2,1,0:T(8,128)S(1)} %all-to-all-done.got, f32[8,128]{1,0:T(8,128)S(1)} %get-tuple-element.17.own_lengths), custom_call_target="tpu_custom_call" | custom-call | tf_op jit(solution)/shard_map/pallas_call | solution.py:320
  20.9 4.0 %all-to-all-start.1 = ((f32[16,16,128]{2,1,0:T(8,128)}), f32[16,16,128]{2,1,0:T(8,128)S(1)}, u32[]{:S(2)}, u32[]{:S(2)}) async-start(f32[16,16,128]{2,1,0:T(8,128)} %get-tuple-element.18), calls=%async_computation.1 | async-start | bytes 262144 | tf_op jit(solution)/shard_map/all_to_all | solution.py:326
  25.0 0.0 collective-permute-done
  25.0 0.1 broadcast_select_fusion
  25.0 4.8 %collective-permute-start.1 = (f32[64,128]{1,0:T(8,128)S(1)}, f32[64,128]{1,0:T(8,128)S(1)}, u32[]{:S(2)}, u32[]{:S(2)}) collective-permute-start(f32[64,128]{1,0:T(8,128)S(1)} %broadcast_select_fusion), channel_id=1, source_target_pairs={{0,64},{32,96},{64,0},{96,32},{128,192},{160,224},{192,128},{224,1... | collective-permute-start | bytes 98312 | tf_op jit(solution)/shard_map/ppermute | solution.py:317
  29.8 0.1 broadcast_in_dim.36
  29.9 0.1 ne.68
  30.0 1.7 %all-to-all-done.1.xy = f32[16,16,128]{2,1,0:T(8,128)S(1)} async-done(((f32[16,16,128]{2,1,0:T(8,128)}), f32[16,16,128]{2,1,0:T(8,128)S(1)}, u32[]{:S(2)}, u32[]{:S(2)}) %all-to-all-start.1) | async-done | bytes 131104 | tf_op jit(solution)/shard_map/all_to_all | solution.py:326
  31.6 0.0 copy-start.6
  31.6 0.7 copy-done.6
  32.3 1.5 %shard_map.48 = f32[16,24,128]{2,1,0:T(8,128)} custom-call(s32[2]{0:T(128)S(1)} %copy-done.6, f32[16,16,128]{2,1,0:T(8,128)S(1)} %all-to-all-done.1.xy, f32[16,128]{1,0:T(8,128)S(1)} %get-tuple-element.19.piece), custom_call_target="tpu_custom_call" | custom-call | tf_op jit(solution)/shard_map/pallas_call | solution.py:327
  33.8 12.3 %all-to-all-start.2 = ((f32[16,24,128]{2,1,0:T(8,128)}), f32[16,24,128]{2,1,0:T(8,128)S(1)}, u32[]{:S(2)}, u32[]{:S(2)}) async-start(f32[16,24,128]{2,1,0:T(8,128)} %shard_map.48), calls=%async_computation.2 | async-start | bytes 393216 | tf_op jit(solution)/shard_map/all_to_all | solution.py:328
  46.1 0.0 collective-permute-done.1
  46.1 0.1 broadcast_select_fusion.1
  46.2 2.2 %collective-permute-start.2 = (f32[64,128]{1,0:T(8,128)S(1)}, f32[64,128]{1,0:T(8,128)S(1)}, u32[]{:S(2)}, u32[]{:S(2)}) collective-permute-start(f32[64,128]{1,0:T(8,128)S(1)} %broadcast_select_fusion.1), channel_id=1, source_target_pairs={{0,128},{32,160},{64,192},{96,224},{128,0},{160,32},{192,64},{224,... | collective-permute-start | bytes 98312 | tf_op jit(solution)/shard_map/ppermute | solution.py:317
  48.4 0.1 broadcast_in_dim.34
  48.5 0.1 ne.66
  48.6 2.2 %collective-permute-done.2 = f32[64,128]{1,0:T(8,128)S(1)} collective-permute-done((f32[64,128]{1,0:T(8,128)S(1)}, f32[64,128]{1,0:T(8,128)S(1)}, u32[]{:S(2)}, u32[]{:S(2)}) %collective-permute-start.2) | collective-permute-done | bytes 32800 | tf_op jit(solution)/shard_map/ppermute | solution.py:317
  50.8 0.1 broadcast_select_fusion.2
  50.9 3.1 %collective-permute-start.3 = (f32[64,128]{1,0:T(8,128)S(1)}, f32[64,128]{1,0:T(8,128)S(1)}, u32[]{:S(2)}, u32[]{:S(2)}) collective-permute-start(f32[64,128]{1,0:T(8,128)S(1)} %broadcast_select_fusion.2), channel_id=1, source_target_pairs={{0,256},{32,288},{64,320},{96,352},{128,384},{160,416},{192,448},{... | collective-permute-start | bytes 98312 | tf_op jit(solution)/shard_map/ppermute | solution.py:317
  54.0 0.1 broadcast_in_dim.32
  54.1 0.1 ne.64
  54.2 0.0 copy-start.2
  54.2 0.9 %copy-done.2 = s32[10,4096]{1,0:T(8,128)S(1)} copy-done((s32[10,4096]{1,0:T(8,128)S(1)}, s32[10,4096]{1,0:T(8,128)}, u32[]{:S(2)}) %copy-start.2) | copy-done | bytes 163864
  55.2 0.0 copy-start.7
  55.2 0.7 copy-done.7
  55.8 2.6 %shard_map.49 = (f32[3,16,128]{2,1,0:T(8,128)S(1)}, f32[24,10,8,128]{3,2,1,0:T(8,128)S(1)}, bf16[256,8192]{1,0:T(8,128)(2,1)S(1)}) custom-call(s32[2]{0:T(128)S(1)} %copy-done.7, s32[10,4096]{1,0:T(8,128)S(1)} %copy-done.2), custom_call_target="tpu_custom_call" | custom-call | tf_op jit(solution)/shard_map/pallas_call | solution.py:323
  58.5 0.0 copy-start
  58.5 1.9 %copy-done = bf16[256,8192]{1,0:T(8,128)(2,1)} copy-done((bf16[256,8192]{1,0:T(8,128)(2,1)}, bf16[256,8192]{1,0:T(8,128)(2,1)S(1)}, u32[]{:S(2)}) %copy-start) | copy-done | bytes 4194328
  60.4 0.0 collective-permute-done.3
  60.4 0.1 broadcast_select_fusion.3.rows
  60.5 0.0 all-to-all-done.2
  60.5 5.5 %all-gather = f32[32,24,128]{2,1,0:T(8,128)S(1)} all-gather(f32[16,24,128]{2,1,0:T(8,128)S(1)} %all-to-all-done.2), channel_id=2, replica_groups=mesh['row'=16,'zh'=4,'zl'=4,'core'=2] {'core'}, dimensions={0}, use_global_device_ids=true | all-gather | bytes 589824 | tf_op jit(solution)/shard_map/all_gather | solution.py:329
  66.0 0.0 copy-start.1
  66.0 2.2 %copy-done.1 = bf16[256,8192]{1,0:T(8,128)(2,1)S(1)} copy-done((bf16[256,8192]{1,0:T(8,128)(2,1)S(1)}, bf16[256,8192]{1,0:T(8,128)(2,1)}, u32[]{:S(2)}) %copy-start.1) | copy-done | bytes 4194328
  68.2 0.0 copy-start.8
  68.2 0.7 copy-done.8
  68.8 4.7 %shard_map.50 = f32[256,128]{1,0:T(8,128)} custom-call(s32[2]{0:T(128)S(1)} %copy-done.8, f32[128,256]{1,0:T(8,128)S(1)} %get-tuple-element.14.mt, f32[64,128]{1,0:T(8,128)S(1)} %broadcast_select_fusion.3.rows, f32[2,16,24,128]{3,2,1,0:T(8,128)S(1)} %bitcast.2, f32[3,16,128]{2,1,0:T(8,128)S(1)} %get-tuple-element.20.lane_ids, ...), custom_call_target="tpu_custom_call" | custom-call | tf_op jit(solution)/shard_map/pallas_call | solution.py:330
  (1 shorter events, 0.0 us)
Async XLA Ops:
  0.0 0.9 %copy-start.3 = (f32[256,128]{1,0:T(8,128)S(1)}, f32[256,128]{1,0:T(8,128)}, u32[]{:S(2)}) copy-start(f32[256,128]{1,0:T(8,128)} %dist.1) | copy-start | bytes 393220
  0.9 0.7 copy-start.4
  1.6 0.7 copy-start.9
  3.7 15.2 %all-to-all-start = ((f32[8,16,128]{2,1,0:T(8,128)}), f32[8,16,128]{2,1,0:T(8,128)S(1)}, u32[]{:S(2)}, u32[]{:S(2)}) async-start(f32[8,16,128]{2,1,0:T(8,128)} %get-tuple-element.16), calls=%async_computation | async-start | bytes 131072 | tf_op jit(solution)/shard_map/all_to_all | solution.py:319
  13.9 11.1 %collective-permute-start = (f32[64,128]{1,0:T(8,128)S(1)}, f32[64,128]{1,0:T(8,128)S(1)}, u32[]{:S(2)}, u32[]{:S(2)}) collective-permute-start(f32[64,128]{1,0:T(8,128)S(1)} %get-tuple-element.15), channel_id=1, source_target_pairs={{0,32},{32,0},{64,96},{96,64},{128,160},{160,128},{192,224},{224,1... | collective-permute-start | bytes 98312 | tf_op jit(solution)/shard_map/ppermute | solution.py:317
  19.0 0.7 copy-start.5
  20.9 10.7 %all-to-all-start.1 = ((f32[16,16,128]{2,1,0:T(8,128)}), f32[16,16,128]{2,1,0:T(8,128)S(1)}, u32[]{:S(2)}, u32[]{:S(2)}) async-start(f32[16,16,128]{2,1,0:T(8,128)} %get-tuple-element.18), calls=%async_computation.1 | async-start | bytes 262144 | tf_op jit(solution)/shard_map/all_to_all | solution.py:326
  25.0 21.0 %collective-permute-start.1 = (f32[64,128]{1,0:T(8,128)S(1)}, f32[64,128]{1,0:T(8,128)S(1)}, u32[]{:S(2)}, u32[]{:S(2)}) collective-permute-start(f32[64,128]{1,0:T(8,128)S(1)} %broadcast_select_fusion), channel_id=1, source_target_pairs={{0,64},{32,96},{64,0},{96,32},{128,192},{160,224},{192,128},{224,1... | collective-permute-start | bytes 98312 | tf_op jit(solution)/shard_map/ppermute | solution.py:317
  31.6 0.7 copy-start.6
  33.8 26.7 %all-to-all-start.2 = ((f32[16,24,128]{2,1,0:T(8,128)}), f32[16,24,128]{2,1,0:T(8,128)S(1)}, u32[]{:S(2)}, u32[]{:S(2)}) async-start(f32[16,24,128]{2,1,0:T(8,128)} %shard_map.48), calls=%async_computation.2 | async-start | bytes 393216 | tf_op jit(solution)/shard_map/all_to_all | solution.py:328
  46.2 4.7 %collective-permute-start.2 = (f32[64,128]{1,0:T(8,128)S(1)}, f32[64,128]{1,0:T(8,128)S(1)}, u32[]{:S(2)}, u32[]{:S(2)}) collective-permute-start(f32[64,128]{1,0:T(8,128)S(1)} %broadcast_select_fusion.1), channel_id=1, source_target_pairs={{0,128},{32,160},{64,192},{96,224},{128,0},{160,32},{192,64},{224,... | collective-permute-start | bytes 98312 | tf_op jit(solution)/shard_map/ppermute | solution.py:317
  50.9 9.5 %collective-permute-start.3 = (f32[64,128]{1,0:T(8,128)S(1)}, f32[64,128]{1,0:T(8,128)S(1)}, u32[]{:S(2)}, u32[]{:S(2)}) collective-permute-start(f32[64,128]{1,0:T(8,128)S(1)} %broadcast_select_fusion.2), channel_id=1, source_target_pairs={{0,256},{32,288},{64,320},{96,352},{128,384},{160,416},{192,448},{... | collective-permute-start | bytes 98312 | tf_op jit(solution)/shard_map/ppermute | solution.py:317
  54.2 1.0 %copy-start.2 = (s32[10,4096]{1,0:T(8,128)S(1)}, s32[10,4096]{1,0:T(8,128)}, u32[]{:S(2)}) copy-start(s32[10,4096]{1,0:T(8,128)} %ids.1) | copy-start | bytes 491524
  55.2 0.7 copy-start.7
  58.5 1.9 %copy-start = (bf16[256,8192]{1,0:T(8,128)(2,1)}, bf16[256,8192]{1,0:T(8,128)(2,1)S(1)}, u32[]{:S(2)}) copy-start(bf16[256,8192]{1,0:T(8,128)(2,1)S(1)} %get-tuple-element.22.onehot) | copy-start | bytes 12582916
  66.0 2.2 %copy-start.1 = (bf16[256,8192]{1,0:T(8,128)(2,1)S(1)}, bf16[256,8192]{1,0:T(8,128)(2,1)}, u32[]{:S(2)}) copy-start(bf16[256,8192]{1,0:T(8,128)(2,1)} %copy-done) | copy-start | bytes 12582916
  68.2 0.7 copy-start.8

commit v5 on v4

--- a/solution.py
+++ b/solution.py
@@ -33,11 +33,12 @@
     return lax.axis_index("row"), 4 * lax.axis_index("zh") + lax.axis_index("zl"), lax.axis_index("core")
 
 
-def pack_kernel(piv, dist, lengths, mt, scatter, panel, own_lengths, block, held, sems):
+def pack_kernel(pivots, dist, lengths, piv, mt, scatter, panel, home, own_lengths, block, held, sems):
     row, _, _ = place()
     copies = [
         pltpu.make_async_copy(dist, block, sems.at[0]),
         pltpu.make_async_copy(lengths, held, sems.at[1]),
+        pltpu.make_async_copy(pivots, piv, sems.at[2]),
     ]
     for copy in copies:
         copy.start()
@@ -53,6 +54,7 @@
                 for h in range(2):
                     at = 8 * i + 4 * h
                     scatter[n + m, at : at + 4, :] = lines[4 * m : 4 * m + 4, 128 * h : 128 * h + 128]
+        home[32 * i : 32 * i + 32, :] = jnp.full((32, 128), piv[i] // 8 ^ row)
         panel[32 * i : 32 * i + 32, :] = block[pl.ds(pl.multiple_of(lax.rem(piv[i], 8) * PIVOT, 32), 32), :]
     spaced = jnp.concatenate([held[...], jnp.zeros((8, 128 - NEIGHBORS), F32)], 1)
     own_lengths[...] = shift_lanes(spaced, 16 * lax.rem(row, 8))
@@ -129,14 +131,10 @@
         for k in range(NEIGHBORS):
             lane = 16 * (tile // 16) + k
             sub_ids[tile, k] = jnp.broadcast_to(turned[at : at + 8, lane : lane + 1], (8, 128))
-    term = lax.broadcasted_iota(jnp.int32, (256, 128), 0)
-
-    def fill(t, carry):
-        picked = (lax.rem(term, 64) == t) & (term < 192)
-        onehot[:, pl.ds(pl.multiple_of(128 * t, 128), 128)] = jnp.where(picked, 1.0, 0.0).astype(jnp.bfloat16)
-        return carry
-
-    lax.fori_loop(0, 2 * PIVOT, fill, 0)
+    term = lax.broadcasted_iota(jnp.int32, (64, 128), 0)
+    for t in range(16):
+        picked = (lax.rem(term, 16) == t) & (term < 48)
+        onehot[:, 128 * t : 128 * t + 128] = jnp.where(picked, 1.0, 0.0).astype(jnp.bfloat16)
 
 
 def over_lanes(x, lane):
@@ -170,12 +168,13 @@
 
 
 def thirds(x):
-    x = x[:, 0:64]
     high = x.astype(jnp.bfloat16)
     rest = x - high.astype(F32)
     mid = rest.astype(jnp.bfloat16)
     low = (rest - mid.astype(F32)).astype(jnp.bfloat16)
-    return jnp.concatenate([high, mid, low, low], 1)
+    return [
+        jnp.concatenate([term[:, 16 * n : 16 * n + 16] for term in (high, mid, low, low)], 1) for n in range(4)
+    ]
 
 
 def final_kernel(piv, mt, rows, zed, lane_ids, sub_ids, onehot, out, lane_len, turned, ct, kt, rt, spread, new):
@@ -260,9 +259,10 @@
         else:
             if b == 4:
                 parts = thirds(rt[...])
-            for c in range(4 * b - 16, 4 * b - 12):
-                spread[:, 512 * c : 512 * c + 512] = jnp.dot(
-                    parts, onehot[:, 512 * c : 512 * c + 512], preferred_element_type=F32
+            for c in range(4):
+                at = 2048 * (b - 4) + 512 * c
+                spread[:, at : at + 512] = jnp.dot(
+                    parts[b - 4], onehot[:, 512 * c : 512 * c + 512], preferred_element_type=F32
                 )
     for tile in range(8):
         at = 8 * tile
@@ -285,50 +285,52 @@
 
 VM = pl.BlockSpec(memory_space=pltpu.VMEM)
 SM = pl.BlockSpec(memory_space=pltpu.SMEM)
-ANY = pl.BlockSpec(memory_space=pl.ANY)
+HBM = pl.BlockSpec(memory_space=pltpu.HBM)
 MIB = 1024 * 1024
 
 
-def call(kernel, shapes, scratch, ins, mib):
+def call(kernel, shapes, scratch, ins, mib, outs=None):
     return pl.pallas_call(
         kernel,
         out_shape=[s if isinstance(s, jax.ShapeDtypeStruct) else jax.ShapeDtypeStruct(s, F32) for s in shapes],
-        in_specs=[SM] + ins,
-        out_specs=[VM] * len(shapes),
+        in_specs=ins,
+        out_specs=outs or [VM] * len(shapes),
         scratch_shapes=[pltpu.VMEM(s, F32) if isinstance(s, tuple) else s for s in scratch],
         compiler_params=pltpu.CompilerParams(vmem_limit_bytes=mib * MIB),
     )
 
 
 FINAL_SCRATCH = [(3, 16, 128), (128, 128), (64, 256), (64, 128), (128, 128), (128, 8192), (128, 256)]
-ONEHOT = jax.ShapeDtypeStruct((256, 2 * PIVOT * 128), jnp.bfloat16)
+ONEHOT = jax.ShapeDtypeStruct((64, 16 * 128), jnp.bfloat16)
+INTS = jax.ShapeDtypeStruct((64, 128), jnp.int32)
+PIVOTS = jax.ShapeDtypeStruct((2,), jnp.int32)
 
 
 def on_device(distances, neighbor_ids, edge_lengths, pivots):
-    mt, scatter, panel, own_lengths = call(
+    piv, mt, scatter, panel, home, own_lengths = call(
         pack_kernel,
-        [(COLS, ROWS), (HOLDERS, 16, 128), (64, 128), (8, 128)],
-        [(ROWS, COLS), (8, NEIGHBORS), pltpu.SemaphoreType.DMA((2,))],
-        [ANY, ANY],
+        [PIVOTS, (COLS, ROWS), (HOLDERS, 16, 128), (64, 128), INTS, (8, 128)],
+        [(ROWS, COLS), (8, NEIGHBORS), pltpu.SemaphoreType.DMA((3,))],
+        [HBM] * 3,
         8,
-    )(pivots, distances, edge_lengths.T)
-    home = jnp.repeat(pivots // 8, PIVOT)[:, None] ^ lax.axis_index("row")
+        [SM] + [VM] * 5,
+    )(*[pltpu.with_memory_space_constraint(x, pltpu.HBM) for x in (pivots, distances, edge_lengths.T)])
     for m in (1, 2, 4, 8):
         other = lax.ppermute(panel, "row", [(i, i ^ m) for i in range(NXY)])
         panel = jnp.where((home & m) != 0, other, panel)
     scatter = lax.all_to_all(scatter, ("zl", "core"), 0, 0)
-    xy, piece = call(spread_kernel, [(NXY, XY_ROWS, 128), (16, 128)], [], [VM] * 2, 8)(
-        pivots, scatter, own_lengths
+    xy, piece = call(spread_kernel, [(NXY, XY_ROWS, 128), (16, 128)], [], [SM] + [VM] * 2, 8)(
+        piv, scatter, own_lengths
     )
     lane_ids, sub_ids, onehot = call(
-        ids_kernel, [(3, 16, 128), (24, NEIGHBORS, 8, 128), ONEHOT], [(128, 128)], [VM], 16
-    )(pivots, neighbor_ids)
+        ids_kernel, [(3, 16, 128), (24, NEIGHBORS, 8, 128), ONEHOT], [(128, 128)], [SM, VM], 16
+    )(piv, neighbor_ids)
     xy = lax.all_to_all(xy, "row", 0, 0)
-    (zed,) = call(gather_kernel, [(NZ, Z_ROWS, 128)], [(128, 128)], [VM] * 2, 8)(pivots, xy, piece)
+    (zed,) = call(gather_kernel, [(NZ, Z_ROWS, 128)], [(128, 128)], [SM] + [VM] * 2, 8)(piv, xy, piece)
     zed = lax.all_to_all(zed, ("zh", "zl"), 0, 0)
     zed = lax.all_gather(zed, "core")
-    (out,) = call(final_kernel, [(ROWS, COLS)], FINAL_SCRATCH, [VM] * 6, 24)(
-        pivots, mt, panel, zed, lane_ids, sub_ids, onehot
+    (out,) = call(final_kernel, [(ROWS, COLS)], FINAL_SCRATCH, [SM] + [VM] * 6, 24)(
+        piv, mt, panel, zed, lane_ids, sub_ids, onehot
     )
     return out
 

time: 74.2 us -> 67.5 us (0.910)
  local copies, waits for them, and re-layouts: 10.6 us -> 0.01 us
  waiting for transfers between devices: 6.26 us -> 10.8 us
  blocking collectives: 5.49 us -> 7.15 us
  Pallas kernels: 11.6 us -> 10.3 us
  other arithmetic: 0.98 us -> 0.03 us
    unnamed x20 -> x2, local copies, waits for them, and re-layouts: 9.94 us -> 0.01 us
    ppermute x4, waiting for transfers between devices: 2.25 us -> 4.49 us  [on_device(): other = lax.ppermute(panel, 'row', [(i, i ^ m) for i in range(NXY)])]
    all_gather x1, blocking collectives: 5.49 us -> 7.15 us  [on_device(): zed = lax.all_gather(zed, 'core')]
    pallas_call x1, Pallas kernels: 2.64 us -> 1.2 us  [on_device(): call(ids_kernel, [(3, 16, 128), (24, NEIGHBORS, 8, 128), ONEHOT], [(128,...]
    all_to_all x1, waiting for transfers between devices: 0.01 us -> 1.2 us  [on_device(): zed = lax.all_to_all(zed, ('zh', 'zl'), 0, 0)]
    all_to_all x1, waiting for transfers between devices: 2.34 us -> 3.19 us  [on_device(): scatter = lax.all_to_all(scatter, ('zl', 'core'), 0, 0)]
  transfers between devices with their start and end apart: 7 -> 7, of which waited for: 3 -> 5; matrix products, arithmetic and copies ran while one was open for 2% -> 0% of each run, Pallas kernels for 7% -> 6%
where the time goes in v5:
time: 67.5 us; the launch traced here: 67 us
  starting transfers between devices  38.7 us (57%)
  waiting for transfers between devices  10.8 us (16%)
  Pallas kernels  10.3 us (15%)
  blocking collectives  7.15 us (11%)
    all_to_all x1, starting transfers between devices, on_device(): zed = lax.all_to_all(zed, ('zh', 'zl'), 0, 0)  12.4 us
    ppermute x4, starting transfers between devices, on_device(): other = lax.ppermute(panel, 'row', [(i, i ^ m) for i in range(NXY)])  12.1 us
    all_to_all x1, starting transfers between devices, on_device(): scatter = lax.all_to_all(scatter, ('zl', 'core'), 0, 0)  10.1 us
    all_gather x1, blocking collectives, on_device(): zed = lax.all_gather(zed, 'core')  7.15 us
    pallas_call x1, Pallas kernels, on_device(): call(final_kernel, [(ROWS, COLS)], FINAL_SCRATCH, [SM] + [VM] * 6, 24)  4.65 us
    ppermute x4, waiting for transfers between devices, on_device(): other = lax.ppermute(panel, 'row', [(i, i ^ m) for i in range(NXY)])  4.49 us
    all_to_all x1, starting transfers between devices, on_device(): xy = lax.all_to_all(xy, 'row', 0, 0)  3.99 us
    all_to_all x1, waiting for transfers between devices, on_device(): scatter = lax.all_to_all(scatter, ('zl', 'core'), 0, 0)  3.19 us
  transfers between devices with their start and end apart: 7, of which 5 were waited for; matrix products, arithmetic and copies ran while one was open for 0% of the time, Pallas kernels for 6%

profile of v5, /device:TPU:1, one launch (start us, length us, event | category | flops | bytes accessed | tf_op | source)
XLA Modules:
  0.0 67.0 jit_solution(7635482153184896476)
XLA Ops:
  0.0 1.7 %shard_map.46 = (s32[2]{0:T(128)S(1)}, f32[128,256]{1,0:T(8,128)S(1)}, f32[8,16,128]{2,1,0:T(8,128)}, f32[64,128]{1,0:T(8,128)S(1)}, s32[64,128]{1,0:T(8,128)S(1)}, /*index=5*/f32[8,128]{1,0:T(8,128)S(1)}) custom-call(s32[2]{0:T(128)} %pivots.1, f32[256,128]{1,0:T(8,128)} %dist.1, f32[8,10]{1,0:T(8,128)} %bitcast.3), custom_call_target="tpu_custom_call" | custom-call | tf_op jit(solution)/shard_map/pallas_call | solution.py:310
  1.7 10.1 %all-to-all-start = ((f32[8,16,128]{2,1,0:T(8,128)}), f32[8,16,128]{2,1,0:T(8,128)S(1)}, u32[]{:S(2)}, u32[]{:S(2)}) async-start(f32[8,16,128]{2,1,0:T(8,128)} %get-tuple-element.20), calls=%async_computation | async-start | bytes 131072 | tf_op jit(solution)/shard_map/all_to_all | solution.py:321
  11.8 1.9 %collective-permute-start = (f32[64,128]{1,0:T(8,128)S(1)}, f32[64,128]{1,0:T(8,128)S(1)}, u32[]{:S(2)}, u32[]{:S(2)}) collective-permute-start(f32[64,128]{1,0:T(8,128)S(1)} %get-tuple-element.19), channel_id=1, source_target_pairs={{0,32},{32,0},{64,96},{96,64},{128,160},{160,128},{192,224},{224,1... | collective-permute-start | bytes 98312 | tf_op jit(solution)/shard_map/ppermute | solution.py:319
  13.8 3.2 %all-to-all-done.got = f32[8,16,128]{2,1,0:T(8,128)S(1)} async-done(((f32[8,16,128]{2,1,0:T(8,128)}), f32[8,16,128]{2,1,0:T(8,128)S(1)}, u32[]{:S(2)}, u32[]{:S(2)}) %all-to-all-start) | async-done | bytes 65568 | tf_op jit(solution)/shard_map/all_to_all | solution.py:321
  16.9 1.3 %shard_map.47 = (f32[16,16,128]{2,1,0:T(8,128)}, f32[16,128]{1,0:T(8,128)S(1)}) custom-call(s32[2]{0:T(128)S(1)} %get-tuple-element.16.piv, f32[8,16,128]{2,1,0:T(8,128)S(1)} %all-to-all-done.got, f32[8,128]{1,0:T(8,128)S(1)} %get-tuple-element.21.own_lengths), custom_call_target="tpu_custom_call" | custom-call | tf_op jit(solution)/shard_map/pallas_call | solution.py:322
  18.3 4.0 %all-to-all-start.1 = ((f32[16,16,128]{2,1,0:T(8,128)}), f32[16,16,128]{2,1,0:T(8,128)S(1)}, u32[]{:S(2)}, u32[]{:S(2)}) async-start(f32[16,16,128]{2,1,0:T(8,128)} %get-tuple-element.22), calls=%async_computation.1 | async-start | bytes 262144 | tf_op jit(solution)/shard_map/all_to_all | solution.py:328
  22.3 0.0 collective-permute-done
  22.3 4.8 %collective-permute-start.1 = (f32[64,128]{1,0:T(8,128)S(1)}, f32[64,128]{1,0:T(8,128)S(1)}, u32[]{:S(2)}, u32[]{:S(2)}) collective-permute-start(f32[64,128]{1,0:T(8,128)S(1)} %fusion.3), channel_id=1, source_target_pairs={{0,64},{32,96},{64,0},{96,32},{128,192},{160,224},{192,128},{224,1... | collective-permute-start | bytes 98312 | tf_op jit(solution)/shard_map/ppermute | solution.py:319
  27.1 1.9 %all-to-all-done.1.xy = f32[16,16,128]{2,1,0:T(8,128)S(1)} async-done(((f32[16,16,128]{2,1,0:T(8,128)}), f32[16,16,128]{2,1,0:T(8,128)S(1)}, u32[]{:S(2)}, u32[]{:S(2)}) %all-to-all-start.1) | async-done | bytes 131104 | tf_op jit(solution)/shard_map/all_to_all | solution.py:328
  28.9 1.4 %shard_map.48 = f32[16,24,128]{2,1,0:T(8,128)} custom-call(s32[2]{0:T(128)S(1)} %get-tuple-element.16.piv, f32[16,16,128]{2,1,0:T(8,128)S(1)} %all-to-all-done.1.xy, f32[16,128]{1,0:T(8,128)S(1)} %get-tuple-element.23.piece), custom_call_target="tpu_custom_call" | custom-call | tf_op jit(solution)/shard_map/pallas_call | solution.py:329
  30.4 0.0 copy-start
  30.4 12.4 %all-to-all-start.2 = ((f32[16,24,128]{2,1,0:T(8,128)}), f32[16,24,128]{2,1,0:T(8,128)S(1)}, u32[]{:S(2)}, u32[]{:S(2)}) async-start(f32[16,24,128]{2,1,0:T(8,128)} %shard_map.48), calls=%async_computation.2 | async-start | bytes 393216 | tf_op jit(solution)/shard_map/all_to_all | solution.py:330
  42.8 0.0 collective-permute-done.1
  42.9 2.2 %collective-permute-start.2 = (f32[64,128]{1,0:T(8,128)S(1)}, f32[64,128]{1,0:T(8,128)S(1)}, u32[]{:S(2)}, u32[]{:S(2)}) collective-permute-start(f32[64,128]{1,0:T(8,128)S(1)} %fusion.2), channel_id=1, source_target_pairs={{0,128},{32,160},{64,192},{96,224},{128,0},{160,32},{192,64},{224,... | collective-permute-start | bytes 98312 | tf_op jit(solution)/shard_map/ppermute | solution.py:319
  45.1 2.4 %collective-permute-done.2 = f32[64,128]{1,0:T(8,128)S(1)} collective-permute-done((f32[64,128]{1,0:T(8,128)S(1)}, f32[64,128]{1,0:T(8,128)S(1)}, u32[]{:S(2)}, u32[]{:S(2)}) %collective-permute-start.2) | collective-permute-done | bytes 32800 | tf_op jit(solution)/shard_map/ppermute | solution.py:319
  47.5 3.2 %collective-permute-start.3 = (f32[64,128]{1,0:T(8,128)S(1)}, f32[64,128]{1,0:T(8,128)S(1)}, u32[]{:S(2)}, u32[]{:S(2)}) collective-permute-start(f32[64,128]{1,0:T(8,128)S(1)} %fusion.1), channel_id=1, source_target_pairs={{0,256},{32,288},{64,320},{96,352},{128,384},{160,416},{192,448},{... | collective-permute-start | bytes 98312 | tf_op jit(solution)/shard_map/ppermute | solution.py:319
  50.7 0.0 copy-done
  50.7 1.2 %shard_map.49 = (f32[3,16,128]{2,1,0:T(8,128)S(1)}, f32[24,10,8,128]{3,2,1,0:T(8,128)S(1)}, bf16[64,2048]{1,0:T(8,128)(2,1)S(1)}) custom-call(s32[2]{0:T(128)S(1)} %get-tuple-element.16.piv, s32[10,4096]{1,0:T(8,128)S(1)} %copy-done), custom_call_target="tpu_custom_call" | custom-call | tf_op jit(solution)/shard_map/pallas_call | solution.py:325
  51.9 2.1 %collective-permute-done.3 = f32[64,128]{1,0:T(8,128)S(1)} collective-permute-done((f32[64,128]{1,0:T(8,128)S(1)}, f32[64,128]{1,0:T(8,128)S(1)}, u32[]{:S(2)}, u32[]{:S(2)}) %collective-permute-start.3) | collective-permute-done | bytes 32800 | tf_op jit(solution)/shard_map/ppermute | solution.py:319
  54.0 1.2 %all-to-all-done.2 = f32[16,24,128]{2,1,0:T(8,128)S(1)} async-done(((f32[16,24,128]{2,1,0:T(8,128)}), f32[16,24,128]{2,1,0:T(8,128)S(1)}, u32[]{:S(2)}, u32[]{:S(2)}) %all-to-all-start.2) | async-done | bytes 196640 | tf_op jit(solution)/shard_map/all_to_all | solution.py:330
  55.2 7.1 %all-gather = f32[32,24,128]{2,1,0:T(8,128)S(1)} all-gather(f32[16,24,128]{2,1,0:T(8,128)S(1)} %all-to-all-done.2), channel_id=2, replica_groups=mesh['row'=16,'zh'=4,'zl'=4,'core'=2] {'core'}, dimensions={0}, use_global_device_ids=true | all-gather | bytes 589824 | tf_op jit(solution)/shard_map/all_gather | solution.py:331
  62.3 4.7 %shard_map.50 = f32[256,128]{1,0:T(8,128)} custom-call(s32[2]{0:T(128)S(1)} %get-tuple-element.16.piv, f32[128,256]{1,0:T(8,128)S(1)} %get-tuple-element.17.mt, f32[64,128]{1,0:T(8,128)S(1)} %fusion.rows, f32[2,16,24,128]{3,2,1,0:T(8,128)S(1)} %bitcast.2, f32[3,16,128]{2,1,0:T(8,128)S(1)} %get-tuple-element.24.lane_ids, ...), custom_call_target="tpu_custom_call" | custom-call | tf_op jit(solution)/shard_map/pallas_call | solution.py:332
  (4 shorter events, 0.0 us)
Async XLA Ops:
  1.7 15.2 %all-to-all-start = ((f32[8,16,128]{2,1,0:T(8,128)}), f32[8,16,128]{2,1,0:T(8,128)S(1)}, u32[]{:S(2)}, u32[]{:S(2)}) async-start(f32[8,16,128]{2,1,0:T(8,128)} %get-tuple-element.20), calls=%async_computation | async-start | bytes 131072 | tf_op jit(solution)/shard_map/all_to_all | solution.py:321
  11.8 10.4 %collective-permute-start = (f32[64,128]{1,0:T(8,128)S(1)}, f32[64,128]{1,0:T(8,128)S(1)}, u32[]{:S(2)}, u32[]{:S(2)}) collective-permute-start(f32[64,128]{1,0:T(8,128)S(1)} %get-tuple-element.19), channel_id=1, source_target_pairs={{0,32},{32,0},{64,96},{96,64},{128,160},{160,128},{192,224},{224,1... | collective-permute-start | bytes 98312 | tf_op jit(solution)/shard_map/ppermute | solution.py:319
  18.3 10.7 %all-to-all-start.1 = ((f32[16,16,128]{2,1,0:T(8,128)}), f32[16,16,128]{2,1,0:T(8,128)S(1)}, u32[]{:S(2)}, u32[]{:S(2)}) async-start(f32[16,16,128]{2,1,0:T(8,128)} %get-tuple-element.22), calls=%async_computation.1 | async-start | bytes 262144 | tf_op jit(solution)/shard_map/all_to_all | solution.py:328
  22.3 20.6 %collective-permute-start.1 = (f32[64,128]{1,0:T(8,128)S(1)}, f32[64,128]{1,0:T(8,128)S(1)}, u32[]{:S(2)}, u32[]{:S(2)}) collective-permute-start(f32[64,128]{1,0:T(8,128)S(1)} %fusion.3), channel_id=1, source_target_pairs={{0,64},{32,96},{64,0},{96,32},{128,192},{160,224},{192,128},{224,1... | collective-permute-start | bytes 98312 | tf_op jit(solution)/shard_map/ppermute | solution.py:319
  30.4 20.3 %copy-start = (s32[10,4096]{1,0:T(8,128)S(1)}, s32[10,4096]{1,0:T(8,128)}, u32[]{:S(2)}) copy-start(s32[10,4096]{1,0:T(8,128)} %ids.1) | copy-start | bytes 491524
  30.4 24.8 %all-to-all-start.2 = ((f32[16,24,128]{2,1,0:T(8,128)}), f32[16,24,128]{2,1,0:T(8,128)S(1)}, u32[]{:S(2)}, u32[]{:S(2)}) async-start(f32[16,24,128]{2,1,0:T(8,128)} %shard_map.48), calls=%async_computation.2 | async-start | bytes 393216 | tf_op jit(solution)/shard_map/all_to_all | solution.py:330
  42.9 4.7 %collective-permute-start.2 = (f32[64,128]{1,0:T(8,128)S(1)}, f32[64,128]{1,0:T(8,128)S(1)}, u32[]{:S(2)}, u32[]{:S(2)}) collective-permute-start(f32[64,128]{1,0:T(8,128)S(1)} %fusion.2), channel_id=1, source_target_pairs={{0,128},{32,160},{64,192},{96,224},{128,0},{160,32},{192,64},{224,... | collective-permute-start | bytes 98312 | tf_op jit(solution)/shard_map/ppermute | solution.py:319
  47.5 6.5 %collective-permute-start.3 = (f32[64,128]{1,0:T(8,128)S(1)}, f32[64,128]{1,0:T(8,128)S(1)}, u32[]{:S(2)}, u32[]{:S(2)}) collective-permute-start(f32[64,128]{1,0:T(8,128)S(1)} %fusion.1), channel_id=1, source_target_pairs={{0,256},{32,288},{64,320},{96,352},{128,384},{160,416},{192,448},{... | collective-permute-start | bytes 98312 | tf_op jit(solution)/shard_map/ppermute | solution.py:319

commit v6 on v5

--- a/solution.py
+++ b/solution.py
@@ -14,7 +14,7 @@
 F32 = jnp.float32
 INF = float("inf")
 
-XY_K, XY_L, XY_ROWS = 4, 8, 16
+XY_L, XY_R, XY_ROWS = 8, 16, 80
 Z_L, Z_K, Z_ROWS = 16, 20, 24
 HOLDERS = 8
 
@@ -33,7 +33,7 @@
     return lax.axis_index("row"), 4 * lax.axis_index("zh") + lax.axis_index("zl"), lax.axis_index("core")
 
 
-def pack_kernel(pivots, dist, lengths, piv, mt, scatter, panel, home, own_lengths, block, held, sems):
+def pack_kernel(pivots, dist, lengths, piv, mt, scatter, panel, own_lengths, block, held, sems):
     row, _, _ = place()
     copies = [
         pltpu.make_async_copy(dist, block, sems.at[0]),
@@ -54,13 +54,12 @@
                 for h in range(2):
                     at = 8 * i + 4 * h
                     scatter[n + m, at : at + 4, :] = lines[4 * m : 4 * m + 4, 128 * h : 128 * h + 128]
-        home[32 * i : 32 * i + 32, :] = jnp.full((32, 128), piv[i] // 8 ^ row)
         panel[32 * i : 32 * i + 32, :] = block[pl.ds(pl.multiple_of(lax.rem(piv[i], 8) * PIVOT, 32), 32), :]
     spaced = jnp.concatenate([held[...], jnp.zeros((8, 128 - NEIGHBORS), F32)], 1)
     own_lengths[...] = shift_lanes(spaced, 16 * lax.rem(row, 8))
 
 
-def spread_kernel(piv, got, own_lengths, xy, piece):
+def spread_kernel(piv, got, own_lengths, panel, xy, piece):
     p, q = piv[0], piv[1]
     corner = None
     for i, pivot in enumerate((p, q)):
@@ -74,19 +73,22 @@
     corner = pltpu.roll(corner, 4, 0)
     for d in range(NXY):
         xy[d, 0:XY_L] = corner
-        xy[d, XY_L:XY_ROWS] = own_lengths[...]
-
-
-def gather_kernel(piv, xy, piece, zchunk, turned):
+        xy[d, XY_L:XY_R] = own_lengths[...]
+        xy[d, XY_R:XY_ROWS] = panel[...]
+
+
+def gather_kernel(piv, xy, piece, zchunk, rows, turned):
     p, q = piv[0], piv[1]
     row, _, _ = place()
     row_p, row_q = p // 8, q // 8
+    rows[0:32] = xy[row_p, XY_R : XY_R + 32]
+    rows[32:64] = xy[row_q, XY_R + 32 : XY_ROWS]
     corner = jnp.where(lax.rem(lanes(8) // PIVOT, 2) == 0, xy[row_p, 0:XY_L], xy[row_q, 0:XY_L])
-    low = xy[0, XY_L:XY_ROWS]
-    high = xy[8, XY_L:XY_ROWS]
+    low = xy[0, XY_L:XY_R]
+    high = xy[8, XY_L:XY_R]
     for d in range(1, 8):
-        low = jnp.maximum(low, xy[d, XY_L:XY_ROWS])
-        high = jnp.maximum(high, xy[8 + d, XY_L:XY_ROWS])
+        low = jnp.maximum(low, xy[d, XY_L:XY_R])
+        high = jnp.maximum(high, xy[8 + d, XY_L:XY_R])
     turned[...] = jnp.concatenate([low, high, jnp.zeros((112, 128), F32)], 0).T
     group = lanes(8) // 8
 
@@ -302,35 +304,31 @@
 
 FINAL_SCRATCH = [(3, 16, 128), (128, 128), (64, 256), (64, 128), (128, 128), (128, 8192), (128, 256)]
 ONEHOT = jax.ShapeDtypeStruct((64, 16 * 128), jnp.bfloat16)
-INTS = jax.ShapeDtypeStruct((64, 128), jnp.int32)
 PIVOTS = jax.ShapeDtypeStruct((2,), jnp.int32)
 
 
 def on_device(distances, neighbor_ids, edge_lengths, pivots):
-    piv, mt, scatter, panel, home, own_lengths = call(
+    piv, mt, scatter, panel, own_lengths = call(
         pack_kernel,
-        [PIVOTS, (COLS, ROWS), (HOLDERS, 16, 128), (64, 128), INTS, (8, 128)],
+        [PIVOTS, (COLS, ROWS), (HOLDERS, 16, 128), (64, 128), (8, 128)],
         [(ROWS, COLS), (8, NEIGHBORS), pltpu.SemaphoreType.DMA((3,))],
         [HBM] * 3,
         8,
-        [SM] + [VM] * 5,
+        [SM] + [VM] * 4,
     )(*[pltpu.with_memory_space_constraint(x, pltpu.HBM) for x in (pivots, distances, edge_lengths.T)])
-    for m in (1, 2, 4, 8):
-        other = lax.ppermute(panel, "row", [(i, i ^ m) for i in range(NXY)])
-        panel = jnp.where((home & m) != 0, other, panel)
     scatter = lax.all_to_all(scatter, ("zl", "core"), 0, 0)
-    xy, piece = call(spread_kernel, [(NXY, XY_ROWS, 128), (16, 128)], [], [SM] + [VM] * 2, 8)(
-        piv, scatter, own_lengths
+    xy, piece = call(spread_kernel, [(NXY, XY_ROWS, 128), (16, 128)], [], [SM] + [VM] * 3, 8)(
+        piv, scatter, own_lengths, panel
     )
     lane_ids, sub_ids, onehot = call(
         ids_kernel, [(3, 16, 128), (24, NEIGHBORS, 8, 128), ONEHOT], [(128, 128)], [SM, VM], 16
     )(piv, neighbor_ids)
     xy = lax.all_to_all(xy, "row", 0, 0)
-    (zed,) = call(gather_kernel, [(NZ, Z_ROWS, 128)], [(128, 128)], [SM] + [VM] * 2, 8)(piv, xy, piece)
+    zed, rows = call(gather_kernel, [(NZ, Z_ROWS, 128), (64, 128)], [(128, 128)], [SM] + [VM] * 2, 8)(piv, xy, piece)
     zed = lax.all_to_all(zed, ("zh", "zl"), 0, 0)
     zed = lax.all_gather(zed, "core")
     (out,) = call(final_kernel, [(ROWS, COLS)], FINAL_SCRATCH, [SM] + [VM] * 6, 24)(
-        piv, mt, panel, zed, lane_ids, sub_ids, onehot
+        piv, mt, rows, zed, lane_ids, sub_ids, onehot
     )
     return out
 

time: 67.5 us -> 70.5 us (1.044)
  blocking collectives: 7.15 us -> 37.3 us
  starting transfers between devices: 38.7 us -> 12.3 us
  Pallas kernels: 10.3 us -> 9.47 us
    all_to_all x0 -> x2, blocking collectives: none -> 30 us  [the longest x1 15.7 us: on_device(): xy = lax.all_to_all(xy, 'row', 0, 0)]
    all_to_all x2 -> x0, starting transfers between devices: 14.1 us -> none  [the longest x1 10.1 us: on_device(): scatter = lax.all_to_all(scatter, ('zl', 'core'), 0, 0)]
    ppermute x4 -> x0, starting transfers between devices: 12.1 us -> none  [on_device(): other = lax.ppermute(panel, 'row', [(i, i ^ m) for i in range(NXY)])]
    all_to_all x1, waiting for transfers between devices: 1.2 us -> 11.1 us  [on_device(): zed = lax.all_to_all(zed, ('zh', 'zl'), 0, 0)]
    all_to_all x2 -> x0, waiting for transfers between devices: 5.07 us -> none  [the longest x1 3.19 us: on_device(): scatter = lax.all_to_all(scatter, ('zl', 'core'), 0, 0)]
    ppermute x4 -> x0, waiting for transfers between devices: 4.49 us -> none  [on_device(): other = lax.ppermute(panel, 'row', [(i, i ^ m) for i in range(NXY)])]
    pallas_call x3, Pallas kernels: 4.44 us -> 3.61 us  [the longest x1 1.54 us: on_device(): call(pack_kernel, [PIVOTS, (COLS, ROWS), (HOLDERS, 16, 128), (64, 128), (...]
  transfers between devices with their start and end apart: 7 -> 1, of which waited for: 5 -> 1; matrix products, arithmetic and copies ran while one was open for 0% -> 0% of each run, Pallas kernels for 6% -> 2%
where the time goes in v6:
time: 70.5 us; the launch traced here: 70.3 us
  blocking collectives  37.3 us (53%)
  starting transfers between devices  12.3 us (17%)
  waiting for transfers between devices  11.1 us (16%)
  Pallas kernels  9.47 us (13%)
    all_to_all x1, blocking collectives, on_device(): xy = lax.all_to_all(xy, 'row', 0, 0)  15.7 us
    all_to_all x1, blocking collectives, on_device(): scatter = lax.all_to_all(scatter, ('zl', 'core'), 0, 0)  14.3 us
    all_to_all x1, starting transfers between devices, on_device(): zed = lax.all_to_all(zed, ('zh', 'zl'), 0, 0)  12.3 us
    all_to_all x1, waiting for transfers between devices, on_device(): zed = lax.all_to_all(zed, ('zh', 'zl'), 0, 0)  11.1 us
    all_gather x1, blocking collectives, on_device(): zed = lax.all_gather(zed, 'core')  7.31 us
    pallas_call x1, Pallas kernels, on_device(): call(final_kernel, [(ROWS, COLS)], FINAL_SCRATCH, [SM] + [VM] * 6, 24)  4.65 us
    pallas_call x1, Pallas kernels, on_device(): call(pack_kernel, [PIVOTS, (COLS, ROWS), (HOLDERS, 16, 128), (64, 128), (...  1.54 us
    pallas_call x1, Pallas kernels, on_device(): call(gather_kernel, [(NZ, Z_ROWS, 128), (64, 128)], [(128, 128)], [SM] +...  1.44 us
  transfers between devices with their start and end apart: 1, of which 1 were waited for; matrix products, arithmetic and copies ran while one was open for 0% of the time, Pallas kernels for 2%

profile of v6, /device:TPU:1, one launch (start us, length us, event | category | flops | bytes accessed | tf_op | source)
XLA Modules:
  0.0 70.3 jit_solution(15494510137267021634)
XLA Ops:
  0.0 1.5 %shard_map.46 = (s32[2]{0:T(128)S(1)}, f32[128,256]{1,0:T(8,128)S(1)}, f32[8,16,128]{2,1,0:T(8,128)S(1)}, f32[64,128]{1,0:T(8,128)S(1)}, f32[8,128]{1,0:T(8,128)S(1)}) custom-call(s32[2]{0:T(128)} %pivots.1, f32[256,128]{1,0:T(8,128)} %dist.1, f32[8,10]{1,0:T(8,128)} %bitcast.3), custom_call_target="tpu_custom_call" | custom-call | tf_op jit(solution)/shard_map/pallas_call | solution.py:311
  1.6 14.3 %all_to_all.15.got = f32[8,16,128]{2,1,0:T(8,128)S(1)} all-to-all(f32[8,16,128]{2,1,0:T(8,128)S(1)} %get-tuple-element.19), channel_id=1, replica_groups=mesh['row'=16,'zh'=4,'zl'=4,'core'=2] {'zl','core'}, dimensions={0} | all-to-all | bytes 131072 | tf_op jit(solution)/shard_map/all_to_all | solution.py:319
  15.9 0.6 shard_map.47
  16.5 15.7 %all_to_all.16.xy = f32[16,80,128]{2,1,0:T(8,128)S(1)} all-to-all(f32[16,80,128]{2,1,0:T(8,128)S(1)} %get-tuple-element.22), channel_id=1, replica_groups=mesh['row'=16,'zh'=4,'zl'=4,'core'=2] {'row'}, dimensions={0} | all-to-all | bytes 1310720 | tf_op jit(solution)/shard_map/all_to_all | solution.py:326
  32.2 1.4 %shard_map.48 = (f32[16,24,128]{2,1,0:T(8,128)}, f32[64,128]{1,0:T(8,128)S(1)}) custom-call(s32[2]{0:T(128)S(1)} %get-tuple-element.17.piv, f32[16,80,128]{2,1,0:T(8,128)S(1)} %all_to_all.16.xy, f32[16,128]{1,0:T(8,128)S(1)} %get-tuple-element.23.piece), custom_call_target="tpu_custom_call" | custom-call | tf_op jit(solution)/shard_map/pallas_call | solution.py:327
  33.6 0.0 copy-start
  33.6 12.3 %all-to-all-start.2 = ((f32[16,24,128]{2,1,0:T(8,128)}), f32[16,24,128]{2,1,0:T(8,128)S(1)}, u32[]{:S(2)}, u32[]{:S(2)}) async-start(f32[16,24,128]{2,1,0:T(8,128)} %get-tuple-element.25), calls=%async_computation.2 | async-start | bytes 393216 | tf_op jit(solution)/shard_map/all_to_all | solution.py:328
  46.0 0.0 copy-done
  46.0 1.2 %shard_map.49 = (f32[3,16,128]{2,1,0:T(8,128)S(1)}, f32[24,10,8,128]{3,2,1,0:T(8,128)S(1)}, bf16[64,2048]{1,0:T(8,128)(2,1)S(1)}) custom-call(s32[2]{0:T(128)S(1)} %get-tuple-element.17.piv, s32[10,4096]{1,0:T(8,128)S(1)} %copy-done), custom_call_target="tpu_custom_call" | custom-call | tf_op jit(solution)/shard_map/pallas_call | solution.py:323
  47.2 11.1 %all-to-all-done.2 = f32[16,24,128]{2,1,0:T(8,128)S(1)} async-done(((f32[16,24,128]{2,1,0:T(8,128)}), f32[16,24,128]{2,1,0:T(8,128)S(1)}, u32[]{:S(2)}, u32[]{:S(2)}) %all-to-all-start.2) | async-done | bytes 196640 | tf_op jit(solution)/shard_map/all_to_all | solution.py:328
  58.3 7.3 %all-gather = f32[32,24,128]{2,1,0:T(8,128)S(1)} all-gather(f32[16,24,128]{2,1,0:T(8,128)S(1)} %all-to-all-done.2), channel_id=2, replica_groups=mesh['row'=16,'zh'=4,'zl'=4,'core'=2] {'core'}, dimensions={0}, use_global_device_ids=true | all-gather | bytes 589824 | tf_op jit(solution)/shard_map/all_gather | solution.py:329
  65.6 4.7 %shard_map.50 = f32[256,128]{1,0:T(8,128)} custom-call(s32[2]{0:T(128)S(1)} %get-tuple-element.17.piv, f32[128,256]{1,0:T(8,128)S(1)} %get-tuple-element.18.mt, f32[64,128]{1,0:T(8,128)S(1)} %get-tuple-element.24.rows, f32[2,16,24,128]{3,2,1,0:T(8,128)S(1)} %bitcast.2, f32[3,16,128]{2,1,0:T(8,128)S(1)} %get-tuple-element.26.lane_ids, ...), custom_call_target="tpu_custom_call" | custom-call | tf_op jit(solution)/shard_map/pallas_call | solution.py:330
Async XLA Ops:
  33.6 12.4 %copy-start = (s32[10,4096]{1,0:T(8,128)S(1)}, s32[10,4096]{1,0:T(8,128)}, u32[]{:S(2)}) copy-start(s32[10,4096]{1,0:T(8,128)} %ids.1) | copy-start | bytes 491524
  33.6 24.7 %all-to-all-start.2 = ((f32[16,24,128]{2,1,0:T(8,128)}), f32[16,24,128]{2,1,0:T(8,128)S(1)}, u32[]{:S(2)}, u32[]{:S(2)}) async-start(f32[16,24,128]{2,1,0:T(8,128)} %get-tuple-element.25), calls=%async_computation.2 | async-start | bytes 393216 | tf_op jit(solution)/shard_map/all_to_all | solution.py:328

commit v7 on v6

--- a/solution.py
+++ b/solution.py
@@ -14,8 +14,8 @@
 F32 = jnp.float32
 INF = float("inf")
 
-XY_L, XY_R, XY_ROWS = 8, 16, 80
-Z_L, Z_K, Z_ROWS = 16, 20, 24
+XY_L, XY_P, XY_Q, XY_ROWS = 8, 16, 32, 48
+Z_L, Z_ROWS = 8, 16
 HOLDERS = 8
 
 
@@ -59,36 +59,59 @@
     own_lengths[...] = shift_lanes(spaced, 16 * lax.rem(row, 8))
 
 
-def spread_kernel(piv, got, own_lengths, panel, xy, piece):
+def spread_kernel(piv, got, own_lengths, panel, other_panel, xy, keep, send):
     p, q = piv[0], piv[1]
-    corner = None
+    row, z, _ = place()
+    corner, halves = None, [[], []]
     for i, pivot in enumerate((p, q)):
         holder = lax.rem(pivot // 8, 4) * 2 + lax.rem(pivot // 4, 2)
         mine = got[holder, 8 * i : 8 * i + 8]
-        piece[8 * i : 8 * i + 8, :] = mine
+        for b in range(2):
+            halves[b] += [mine[2 * b : 2 * b + 2], mine[4 + 2 * b : 6 + 2 * b]]
         for j, other in enumerate((p, q)):
             half = jnp.where(lax.rem(other // 4, 2) == 0, mine, pltpu.roll(mine, 4, 0))
             half = shift_lanes(half, 64 * i + 32 * j - lax.rem(other, 4) * PIVOT)
             corner = half if corner is None else jnp.where(lanes(8) // PIVOT == 2 * i + j, half, corner)
+    first, second = [jnp.concatenate(parts, 0) for parts in halves]
+    even = lax.rem(z // 4, 2) == 0
+    keep[...] = jnp.where(even, first, second)
+    send[...] = jnp.where(even, second, first)
     corner = pltpu.roll(corner, 4, 0)
+    part = pl.multiple_of(16 * lax.rem(row, 2), 16)
+    lines = [
+        jnp.where(
+            lax.rem(pivot // 8 + row, 2) == 0,
+            panel[pl.ds(32 * i + part, 16), :],
+            other_panel[pl.ds(32 * i + part, 16), :],
+        )
+        for i, pivot in enumerate((p, q))
+    ]
     for d in range(NXY):
         xy[d, 0:XY_L] = corner
-        xy[d, XY_L:XY_R] = own_lengths[...]
-        xy[d, XY_R:XY_ROWS] = panel[...]
-
-
-def gather_kernel(piv, xy, piece, zchunk, rows, turned):
+        xy[d, XY_L:XY_P] = own_lengths[...]
+        xy[d, XY_P:XY_Q] = lines[0]
+        xy[d, XY_Q:XY_ROWS] = lines[1]
+
+
+def gather_kernel(piv, xy, keep, other, zchunk, rows, turned):
     p, q = piv[0], piv[1]
-    row, _, _ = place()
+    row, z, _ = place()
     row_p, row_q = p // 8, q // 8
-    rows[0:32] = xy[row_p, XY_R : XY_R + 32]
-    rows[32:64] = xy[row_q, XY_R + 32 : XY_ROWS]
+    for b in range(2):
+        rows[16 * b : 16 * b + 16] = xy[row_p // 2 * 2 + b, XY_P:XY_Q]
+        rows[32 + 16 * b : 48 + 16 * b] = xy[row_q // 2 * 2 + b, XY_Q:XY_ROWS]
+    upper = lax.broadcasted_iota(jnp.int32, (8, 128), 0) < 4
+    piece = jnp.where(
+        upper,
+        jnp.where(p // 32 == z // 4, keep[...], other[...]),
+        jnp.where(q // 32 == z // 4, keep[...], other[...]),
+    )
     corner = jnp.where(lax.rem(lanes(8) // PIVOT, 2) == 0, xy[row_p, 0:XY_L], xy[row_q, 0:XY_L])
-    low = xy[0, XY_L:XY_R]
-    high = xy[8, XY_L:XY_R]
+    low = xy[0, XY_L:XY_P]
+    high = xy[8, XY_L:XY_P]
     for d in range(1, 8):
-        low = jnp.maximum(low, xy[d, XY_L:XY_R])
-        high = jnp.maximum(high, xy[8 + d, XY_L:XY_R])
+        low = jnp.maximum(low, xy[d, XY_L:XY_P])
+        high = jnp.maximum(high, xy[8 + d, XY_L:XY_P])
     turned[...] = jnp.concatenate([low, high, jnp.zeros((112, 128), F32)], 0).T
     group = lanes(8) // 8
 
@@ -103,9 +126,8 @@
         return lengths
 
     fixed = take(row_q, 3, take(row_p, 2, take(row, 0, None)))
-    upper = lax.broadcasted_iota(jnp.int32, (8, 128), 0) < 4
     for d in range(NZ):
-        zchunk[d, 0:Z_L] = piece[...]
+        zchunk[d, 0:Z_L] = piece
         zchunk[d, Z_L:Z_ROWS] = jnp.where(upper, take(d, 1, fixed), corner)
 
 
@@ -210,12 +232,13 @@
 
     for i, pivot in enumerate((p, q)):
         for n in range(HOLDERS):
-            holder = 4 * (pivot // 32) + n // 2
             at = 32 * i + 4 * n
-            part = zed[n % 2, holder, 8 * i : 8 * i + 8]
-            ct[at : at + 4, 0:128] = part[0:4]
-            ct[at : at + 4, 128:256] = part[4:8]
-            kt[at : at + 4, :] = shift_lanes(zed[n % 2, holder, Z_L:Z_ROWS], 64 * i)[4:8]
+            group = pivot // 32
+            for b in range(2):
+                part = zed[n % 2, 4 * (group // 2 * 2 + b) + n // 2, 0:Z_L]
+                ct[at + 2 * b : at + 2 * b + 2, 0:128] = part[4 * i : 4 * i + 2]
+                ct[at + 2 * b : at + 2 * b + 2, 128:256] = part[4 * i + 2 : 4 * i + 4]
+            kt[at : at + 4, :] = shift_lanes(zed[n % 2, 4 * group + n // 2, Z_L:Z_ROWS], 64 * i)[4:8]
 
     lane = lanes(8)
     sub = lax.broadcasted_iota(jnp.int32, (8, 128), 0)
@@ -316,15 +339,19 @@
         8,
         [SM] + [VM] * 4,
     )(*[pltpu.with_memory_space_constraint(x, pltpu.HBM) for x in (pivots, distances, edge_lengths.T)])
+    other_panel = lax.ppermute(panel, "row", [(i, i ^ 1) for i in range(NXY)])
     scatter = lax.all_to_all(scatter, ("zl", "core"), 0, 0)
-    xy, piece = call(spread_kernel, [(NXY, XY_ROWS, 128), (16, 128)], [], [SM] + [VM] * 3, 8)(
-        piv, scatter, own_lengths, panel
-    )
+    xy, keep, send = call(spread_kernel, [(NXY, XY_ROWS, 128), (8, 128), (8, 128)], [], [SM] + [VM] * 4, 8)(
+        piv, scatter, own_lengths, panel, other_panel
+    )
+    other_half = lax.ppermute(send, "zh", [(i, i ^ 1) for i in range(4)])
     lane_ids, sub_ids, onehot = call(
         ids_kernel, [(3, 16, 128), (24, NEIGHBORS, 8, 128), ONEHOT], [(128, 128)], [SM, VM], 16
     )(piv, neighbor_ids)
     xy = lax.all_to_all(xy, "row", 0, 0)
-    zed, rows = call(gather_kernel, [(NZ, Z_ROWS, 128), (64, 128)], [(128, 128)], [SM] + [VM] * 2, 8)(piv, xy, piece)
+    zed, rows = call(gather_kernel, [(NZ, Z_ROWS, 128), (64, 128)], [(128, 128)], [SM] + [VM] * 3, 8)(
+        piv, xy, keep, other_half
+    )
     zed = lax.all_to_all(zed, ("zh", "zl"), 0, 0)
     zed = lax.all_gather(zed, "core")
     (out,) = call(final_kernel, [(ROWS, COLS)], FINAL_SCRATCH, [SM] + [VM] * 6, 24)(

time: 70.5 us -> 67.3 us (0.955)
  blocking collectives: 37.3 us -> 5.91 us
  starting transfers between devices: 12.3 us -> 35.3 us
  waiting for transfers between devices: 11.1 us -> 15.2 us
  Pallas kernels: 9.47 us -> 10.4 us
    all_to_all x2 -> x0, blocking collectives: 30 us -> none  [the longest x1 15.7 us: on_device(): xy = lax.all_to_all(xy, 'row', 0, 0)]
    all_to_all x0 -> x2, starting transfers between devices: none -> 14.1 us  [the longest x1 10.1 us: on_device(): scatter = lax.all_to_all(scatter, ('zl', 'core'), 0, 0)]
    ppermute x0 -> x2, starting transfers between devices: none -> 10.7 us  [the longest x1 8.82 us: on_device(): other_half = lax.ppermute(send, 'zh', [(i, i ^ 1) for i in range(4)])]
    ppermute x0 -> x2, waiting for transfers between devices: none -> 4.3 us  [the longest x1 3.03 us: on_device(): other_panel = lax.ppermute(panel, 'row', [(i, i ^ 1) for i in range(NXY)])]
    all_to_all x1, starting transfers between devices: 12.3 us -> 10.5 us  [on_device(): zed = lax.all_to_all(zed, ('zh', 'zl'), 0, 0)]
    all_gather x1, blocking collectives: 7.31 us -> 5.91 us  [on_device(): zed = lax.all_gather(zed, 'core')]
    pallas_call x1, Pallas kernels: 0.63 us -> 1.41 us  [on_device(): call(spread_kernel, [(NXY, XY_ROWS, 128), (8, 128), (8, 128)], [], [SM] +...]
  transfers between devices with their start and end apart: 1 -> 5, of which waited for: 1 -> 4; matrix products, arithmetic and copies ran while one was open for 0% -> 0% of each run, Pallas kernels for 2% -> 2%
where the time goes in v7:
time: 67.3 us; the launch traced here: 66.9 us
  starting transfers between devices  35.3 us (52%)
  waiting for transfers between devices  15.2 us (23%)
  Pallas kernels  10.4 us (15%)
  blocking collectives  5.91 us (9%)
    all_to_all x1, waiting for transfers between devices, on_device(): zed = lax.all_to_all(zed, ('zh', 'zl'), 0, 0)  10.8 us
    all_to_all x1, starting transfers between devices, on_device(): zed = lax.all_to_all(zed, ('zh', 'zl'), 0, 0)  10.5 us
    all_to_all x1, starting transfers between devices, on_device(): scatter = lax.all_to_all(scatter, ('zl', 'core'), 0, 0)  10.1 us
    ppermute x1, starting transfers between devices, on_device(): other_half = lax.ppermute(send, 'zh', [(i, i ^ 1) for i in range(4)])  8.82 us
    all_gather x1, blocking collectives, on_device(): zed = lax.all_gather(zed, 'core')  5.91 us
    pallas_call x1, Pallas kernels, on_device(): call(final_kernel, [(ROWS, COLS)], FINAL_SCRATCH, [SM] + [VM] * 6, 24)  4.68 us
    all_to_all x1, starting transfers between devices, on_device(): xy = lax.all_to_all(xy, 'row', 0, 0)  3.99 us
    ppermute x1, waiting for transfers between devices, on_device(): other_panel = lax.ppermute(panel, 'row', [(i, i ^ 1) for i in range(NXY)])  3.03 us
  transfers between devices with their start and end apart: 5, of which 4 were waited for; matrix products, arithmetic and copies ran while one was open for 0% of the time, Pallas kernels for 2%

profile of v7, /device:TPU:1, one launch (start us, length us, event | category | flops | bytes accessed | tf_op | source)
XLA Modules:
  0.0 66.9 jit_solution(8489696251706786562)
XLA Ops:
  0.0 1.7 %shard_map.46 = (s32[2]{0:T(128)S(1)}, f32[128,256]{1,0:T(8,128)S(1)}, f32[8,16,128]{2,1,0:T(8,128)}, f32[64,128]{1,0:T(8,128)S(1)}, f32[8,128]{1,0:T(8,128)S(1)}) custom-call(s32[2]{0:T(128)} %pivots.1, f32[256,128]{1,0:T(8,128)} %dist.1, f32[8,10]{1,0:T(8,128)} %bitcast.3), custom_call_target="tpu_custom_call" | custom-call | tf_op jit(solution)/shard_map/pallas_call | solution.py:334
  1.7 10.1 %all-to-all-start = ((f32[8,16,128]{2,1,0:T(8,128)}), f32[8,16,128]{2,1,0:T(8,128)S(1)}, u32[]{:S(2)}, u32[]{:S(2)}) async-start(f32[8,16,128]{2,1,0:T(8,128)} %get-tuple-element.20), calls=%async_computation | async-start | bytes 131072 | tf_op jit(solution)/shard_map/all_to_all | solution.py:343
  11.8 1.9 %collective-permute-start = (f32[64,128]{1,0:T(8,128)S(1)}, f32[64,128]{1,0:T(8,128)S(1)}, u32[]{:S(2)}, u32[]{:S(2)}) collective-permute-start(f32[64,128]{1,0:T(8,128)S(1)} %get-tuple-element.22.panel), channel_id=1, source_target_pairs={{0,32},{32,0},{64,96},{96,64},{128,160},{160,128},{192,224},{224,1... | collective-permute-start | bytes 98312 | tf_op jit(solution)/shard_map/ppermute | solution.py:342
  13.8 3.0 %collective-permute-done.other_panel = f32[64,128]{1,0:T(8,128)S(1)} collective-permute-done((f32[64,128]{1,0:T(8,128)S(1)}, f32[64,128]{1,0:T(8,128)S(1)}, u32[]{:S(2)}, u32[]{:S(2)}) %collective-permute-start) | collective-permute-done | bytes 32800 | tf_op jit(solution)/shard_map/ppermute | solution.py:342
  16.8 0.2 all-to-all-done.got
  16.9 1.4 %shard_map.47 = (f32[16,48,128]{2,1,0:T(8,128)}, f32[8,128]{1,0:T(8,128)S(1)}, f32[8,128]{1,0:T(8,128)S(1)}) custom-call(s32[2]{0:T(128)S(1)} %get-tuple-element.18.piv, f32[8,16,128]{2,1,0:T(8,128)S(1)} %all-to-all-done.got, f32[8,128]{1,0:T(8,128)S(1)} %get-tuple-element.21.own_lengths, f32[64,128]{1,0:T(8,128)S(1)} %get-tuple-element.22.panel, ...), custom_call_target="tpu_custom_call" | custom-call | tf_op jit(solution)/shard_map/pallas_call | solution.py:344
  18.4 4.0 %all-to-all-start.1 = ((f32[16,48,128]{2,1,0:T(8,128)}), f32[16,48,128]{2,1,0:T(8,128)S(1)}, u32[]{:S(2)}, u32[]{:S(2)}) async-start(f32[16,48,128]{2,1,0:T(8,128)} %get-tuple-element.23), calls=%async_computation.1 | async-start | bytes 786432 | tf_op jit(solution)/shard_map/all_to_all | solution.py:351
  22.4 8.8 %collective-permute-start.1 = (f32[8,128]{1,0:T(8,128)S(1)}, f32[8,128]{1,0:T(8,128)S(1)}, u32[]{:S(2)}, u32[]{:S(2)}) collective-permute-start(f32[8,128]{1,0:T(8,128)S(1)} %get-tuple-element.25), channel_id=1, source_target_pairs={{0,8},{8,0},{16,24},{24,16},{1,9},{9,1},{17,25},{25,17},{2,10},{10... | collective-permute-start | bytes 12296 | tf_op jit(solution)/shard_map/ppermute | solution.py:347
  31.2 1.3 %collective-permute-done.1.other = f32[8,128]{1,0:T(8,128)S(1)} collective-permute-done((f32[8,128]{1,0:T(8,128)S(1)}, f32[8,128]{1,0:T(8,128)S(1)}, u32[]{:S(2)}, u32[]{:S(2)}) %collective-permute-start.1) | collective-permute-done | bytes 4128 | tf_op jit(solution)/shard_map/ppermute | solution.py:347
  32.5 0.0 all-to-all-done.1.xy
  32.5 0.0 copy-start
  32.5 1.4 %shard_map.48 = (f32[16,16,128]{2,1,0:T(8,128)}, f32[64,128]{1,0:T(8,128)S(1)}) custom-call(s32[2]{0:T(128)S(1)} %get-tuple-element.18.piv, f32[16,48,128]{2,1,0:T(8,128)S(1)} %all-to-all-done.1.xy, f32[8,128]{1,0:T(8,128)S(1)} %get-tuple-element.24.keep, f32[8,128]{1,0:T(8,128)S(1)} %collective-permute-done.1.other), custom_call_target="tpu_custom_call" | custom-call | tf_op jit(solution)/shard_map/pallas_call | solution.py:352
  33.9 10.5 %all-to-all-start.2 = ((f32[16,16,128]{2,1,0:T(8,128)}), f32[16,16,128]{2,1,0:T(8,128)S(1)}, u32[]{:S(2)}, u32[]{:S(2)}) async-start(f32[16,16,128]{2,1,0:T(8,128)} %get-tuple-element.27), calls=%async_computation.2 | async-start | bytes 262144 | tf_op jit(solution)/shard_map/all_to_all | solution.py:355
  44.4 0.0 copy-done
  44.4 1.2 %shard_map.49 = (f32[3,16,128]{2,1,0:T(8,128)S(1)}, f32[24,10,8,128]{3,2,1,0:T(8,128)S(1)}, bf16[64,2048]{1,0:T(8,128)(2,1)S(1)}) custom-call(s32[2]{0:T(128)S(1)} %get-tuple-element.18.piv, s32[10,4096]{1,0:T(8,128)S(1)} %copy-done), custom_call_target="tpu_custom_call" | custom-call | tf_op jit(solution)/shard_map/pallas_call | solution.py:348
  45.6 10.8 %all-to-all-done.2 = f32[16,16,128]{2,1,0:T(8,128)S(1)} async-done(((f32[16,16,128]{2,1,0:T(8,128)}), f32[16,16,128]{2,1,0:T(8,128)S(1)}, u32[]{:S(2)}, u32[]{:S(2)}) %all-to-all-start.2) | async-done | bytes 131104 | tf_op jit(solution)/shard_map/all_to_all | solution.py:355
  56.3 5.9 %all-gather = f32[32,16,128]{2,1,0:T(8,128)S(1)} all-gather(f32[16,16,128]{2,1,0:T(8,128)S(1)} %all-to-all-done.2), channel_id=2, replica_groups=mesh['row'=16,'zh'=4,'zl'=4,'core'=2] {'core'}, dimensions={0}, use_global_device_ids=true | all-gather | bytes 393216 | tf_op jit(solution)/shard_map/all_gather | solution.py:356
  62.2 4.7 %shard_map.50 = f32[256,128]{1,0:T(8,128)} custom-call(s32[2]{0:T(128)S(1)} %get-tuple-element.18.piv, f32[128,256]{1,0:T(8,128)S(1)} %get-tuple-element.19.mt, f32[64,128]{1,0:T(8,128)S(1)} %get-tuple-element.26.rows, f32[2,16,16,128]{3,2,1,0:T(8,128)S(1)} %bitcast.2, f32[3,16,128]{2,1,0:T(8,128)S(1)} %get-tuple-element.28.lane_ids, ...), custom_call_target="tpu_custom_call" | custom-call | tf_op jit(solution)/shard_map/pallas_call | solution.py:357
Async XLA Ops:
  1.7 15.2 %all-to-all-start = ((f32[8,16,128]{2,1,0:T(8,128)}), f32[8,16,128]{2,1,0:T(8,128)S(1)}, u32[]{:S(2)}, u32[]{:S(2)}) async-start(f32[8,16,128]{2,1,0:T(8,128)} %get-tuple-element.20), calls=%async_computation | async-start | bytes 131072 | tf_op jit(solution)/shard_map/all_to_all | solution.py:343
  11.8 4.9 %collective-permute-start = (f32[64,128]{1,0:T(8,128)S(1)}, f32[64,128]{1,0:T(8,128)S(1)}, u32[]{:S(2)}, u32[]{:S(2)}) collective-permute-start(f32[64,128]{1,0:T(8,128)S(1)} %get-tuple-element.22.panel), channel_id=1, source_target_pairs={{0,32},{32,0},{64,96},{96,64},{128,160},{160,128},{192,224},{224,1... | collective-permute-start | bytes 98312 | tf_op jit(solution)/shard_map/ppermute | solution.py:342
  18.4 14.1 %all-to-all-start.1 = ((f32[16,48,128]{2,1,0:T(8,128)}), f32[16,48,128]{2,1,0:T(8,128)S(1)}, u32[]{:S(2)}, u32[]{:S(2)}) async-start(f32[16,48,128]{2,1,0:T(8,128)} %get-tuple-element.23), calls=%async_computation.1 | async-start | bytes 786432 | tf_op jit(solution)/shard_map/all_to_all | solution.py:351
  22.4 10.1 %collective-permute-start.1 = (f32[8,128]{1,0:T(8,128)S(1)}, f32[8,128]{1,0:T(8,128)S(1)}, u32[]{:S(2)}, u32[]{:S(2)}) collective-permute-start(f32[8,128]{1,0:T(8,128)S(1)} %get-tuple-element.25), channel_id=1, source_target_pairs={{0,8},{8,0},{16,24},{24,16},{1,9},{9,1},{17,25},{25,17},{2,10},{10... | collective-permute-start | bytes 12296 | tf_op jit(solution)/shard_map/ppermute | solution.py:347
  32.5 11.9 %copy-start = (s32[10,4096]{1,0:T(8,128)S(1)}, s32[10,4096]{1,0:T(8,128)}, u32[]{:S(2)}) copy-start(s32[10,4096]{1,0:T(8,128)} %ids.1) | copy-start | bytes 491524
  33.9 22.4 %all-to-all-start.2 = ((f32[16,16,128]{2,1,0:T(8,128)}), f32[16,16,128]{2,1,0:T(8,128)S(1)}, u32[]{:S(2)}, u32[]{:S(2)}) async-start(f32[16,16,128]{2,1,0:T(8,128)} %get-tuple-element.27), calls=%async_computation.2 | async-start | bytes 262144 | tf_op jit(solution)/shard_map/all_to_all | solution.py:355

commit v8 on v7

--- a/solution.py
+++ b/solution.py
@@ -14,7 +14,7 @@
 F32 = jnp.float32
 INF = float("inf")
 
-XY_L, XY_P, XY_Q, XY_ROWS = 8, 16, 32, 48
+XY_P, XY_Q, XY_ROWS = 8, 24, 40
 Z_L, Z_ROWS = 8, 16
 HOLDERS = 8
 
@@ -30,11 +30,17 @@
 
 
 def place():
-    return lax.axis_index("row"), 4 * lax.axis_index("zh") + lax.axis_index("zl"), lax.axis_index("core")
+    z = 0
+    for bit in ("z3", "z2", "z1", "z0"):
+        z = 2 * z + lax.axis_index(bit)
+    return lax.axis_index("row"), z, lax.axis_index("core")
+
+
+def upper_half():
+    return lax.broadcasted_iota(jnp.int32, (8, 128), 0) < 4
 
 
 def pack_kernel(pivots, dist, lengths, piv, mt, scatter, panel, own_lengths, block, held, sems):
-    row, _, _ = place()
     copies = [
         pltpu.make_async_copy(dist, block, sems.at[0]),
         pltpu.make_async_copy(lengths, held, sems.at[1]),
@@ -56,7 +62,9 @@
                     scatter[n + m, at : at + 4, :] = lines[4 * m : 4 * m + 4, 128 * h : 128 * h + 128]
         panel[32 * i : 32 * i + 32, :] = block[pl.ds(pl.multiple_of(lax.rem(piv[i], 8) * PIVOT, 32), 32), :]
     spaced = jnp.concatenate([held[...], jnp.zeros((8, 128 - NEIGHBORS), F32)], 1)
-    own_lengths[...] = shift_lanes(spaced, 16 * lax.rem(row, 8))
+    lines = jnp.concatenate([spaced, jnp.zeros((120, 128), F32)], 0).T
+    low, high = lines[0:8], lines[8:16]
+    own_lengths[...] = low + shift_lanes(pltpu.roll(low, 4, 0), 32) + shift_lanes(high, 64)
 
 
 def spread_kernel(piv, got, own_lengths, panel, other_panel, xy, keep, send):
@@ -64,7 +72,7 @@
     row, z, _ = place()
     corner, halves = None, [[], []]
     for i, pivot in enumerate((p, q)):
-        holder = lax.rem(pivot // 8, 4) * 2 + lax.rem(pivot // 4, 2)
+        holder = lax.rem(pivot // 32, 2) * 4 + lax.rem(pivot // 8, 2) * 2 + lax.rem(pivot // 4, 2)
         mine = got[holder, 8 * i : 8 * i + 8]
         for b in range(2):
             halves[b] += [mine[2 * b : 2 * b + 2], mine[4 + 2 * b : 6 + 2 * b]]
@@ -73,10 +81,10 @@
             half = shift_lanes(half, 64 * i + 32 * j - lax.rem(other, 4) * PIVOT)
             corner = half if corner is None else jnp.where(lanes(8) // PIVOT == 2 * i + j, half, corner)
     first, second = [jnp.concatenate(parts, 0) for parts in halves]
-    even = lax.rem(z // 4, 2) == 0
+    even = lax.rem(z // 2, 2) == 0
     keep[...] = jnp.where(even, first, second)
     send[...] = jnp.where(even, second, first)
-    corner = pltpu.roll(corner, 4, 0)
+    small = jnp.where(upper_half(), own_lengths[...], pltpu.roll(corner, 4, 0))
     part = pl.multiple_of(16 * lax.rem(row, 2), 16)
     lines = [
         jnp.where(
@@ -87,48 +95,35 @@
         for i, pivot in enumerate((p, q))
     ]
     for d in range(NXY):
-        xy[d, 0:XY_L] = corner
-        xy[d, XY_L:XY_P] = own_lengths[...]
+        xy[d, 0:XY_P] = small
         xy[d, XY_P:XY_Q] = lines[0]
         xy[d, XY_Q:XY_ROWS] = lines[1]
 
 
-def gather_kernel(piv, xy, keep, other, zchunk, rows, turned):
+def gather_kernel(piv, xy, keep, other, zchunk, rows):
     p, q = piv[0], piv[1]
-    row, z, _ = place()
+    row, z, core = place()
     row_p, row_q = p // 8, q // 8
     for b in range(2):
         rows[16 * b : 16 * b + 16] = xy[row_p // 2 * 2 + b, XY_P:XY_Q]
         rows[32 + 16 * b : 48 + 16 * b] = xy[row_q // 2 * 2 + b, XY_Q:XY_ROWS]
-    upper = lax.broadcasted_iota(jnp.int32, (8, 128), 0) < 4
+    upper = upper_half()
+    bit = lax.rem(z // 2, 2)
     piece = jnp.where(
         upper,
-        jnp.where(p // 32 == z // 4, keep[...], other[...]),
-        jnp.where(q // 32 == z // 4, keep[...], other[...]),
-    )
-    corner = jnp.where(lax.rem(lanes(8) // PIVOT, 2) == 0, xy[row_p, 0:XY_L], xy[row_q, 0:XY_L])
-    low = xy[0, XY_L:XY_P]
-    high = xy[8, XY_L:XY_P]
-    for d in range(1, 8):
-        low = jnp.maximum(low, xy[d, XY_L:XY_P])
-        high = jnp.maximum(high, xy[8 + d, XY_L:XY_P])
-    turned[...] = jnp.concatenate([low, high, jnp.zeros((112, 128), F32)], 0).T
-    group = lanes(8) // 8
-
-    def take(device, at, lengths):
-        start = 16 * (device % 8)
-        from_lane = 8 * (device // 8)
-        first = turned[pl.ds(pl.multiple_of(start, 8), 8), :]
-        second = turned[pl.ds(pl.multiple_of(start + 8, 8), 8), :]
-        for g, part in ((0, first), (1, pltpu.roll(first, 4, 0)), (2, second)):
-            moved = shift_lanes(part, 32 * g + 8 * at - from_lane)
-            lengths = moved if lengths is None else jnp.where(group == 4 * g + at, moved, lengths)
-        return lengths
-
-    fixed = take(row_q, 3, take(row_p, 2, take(row, 0, None)))
+        jnp.where(lax.rem(p // 16, 2) == bit, keep[...], other[...]),
+        jnp.where(lax.rem(q // 16, 2) == bit, keep[...], other[...]),
+    )
+    corner = jnp.where(lax.rem(lanes(8) // PIVOT, 2) == 0, xy[row_p, 0:XY_P], xy[row_q, 0:XY_P])
+    turn = 2 * lax.rem(z, 2) + core
+
+    def take(device, at):
+        return shift_lanes(xy[device, 0:XY_P], 8 * lax.rem(turn + at, 4))
+
+    fixed = take(row, 0) + take(row_p, 2) + take(row_q, 3)
     for d in range(NZ):
         zchunk[d, 0:Z_L] = piece
-        zchunk[d, Z_L:Z_ROWS] = jnp.where(upper, take(d, 1, fixed), corner)
+        zchunk[d, Z_L:Z_ROWS] = jnp.where(upper, fixed + take(d, 1), corner)
 
 
 def ids_kernel(piv, ids, lane_ids, sub_ids, onehot, held):
@@ -205,40 +200,48 @@
     p, q = piv[0], piv[1]
     row, z, core = place()
     col = 2 * z + core
-    upper = lax.broadcasted_iota(jnp.int32, (8, 128), 0) < 4
-
-    def lengths_at(first, count, group, at):
-        parts = []
-        for g in range(3):
-            out = None
-            for u in range(count):
-                device = first + u
-                tile = zed[lax.rem(device, 2), device // 2, Z_L:Z_ROWS]
-                tile = shift_lanes(tile, at + 8 * u - 8 * group - 32 * g)
-                out = tile if out is None else jnp.where(lanes(8) // 8 >= at // 8 + u, tile, out)
-            parts.append(out)
-        return jnp.concatenate([jnp.where(upper, parts[0], pltpu.roll(parts[1], 4, 0)), parts[2]], 0)
-
-    lane_len[0] = lengths_at(0, 16, 0, 0)
-    lane_len[1] = lengths_at(16, 16, 0, 0)
+    slot = lax.rem(lanes(8) // 8, 4)
+
+    def lengths_at(first, count, at):
+        parts = [None] * 3
+        for v in range(count):
+            merged = None
+            for w in range(4):
+                device = first + 4 * v + w
+                tile = zed[w % 2, device // 2, Z_L:Z_ROWS]
+                merged = tile if w == 0 else jnp.where(slot == (at + w) % 4, tile, merged)
+            for g in range(3):
+                moved = shift_lanes(merged, 32 * (v - g))
+                parts[g] = moved if v == 0 else jnp.where(lanes(8) // 32 >= v, moved, parts[g])
+        both = [jnp.where(upper_half(), parts[0], pltpu.roll(parts[1], 4, 0)), parts[2]]
+        if at:
+            both = [
+                jnp.where(slot < 4 - at, shift_lanes(part, -8 * at), shift_lanes(part, 32 - 8 * at)) for part in both
+            ]
+        return jnp.concatenate(both, 0)
+
+    lane_len[0] = lengths_at(0, 4, 0)
+    lane_len[1] = lengths_at(16, 4, 0)
     lane_len[2] = jnp.where(
         lanes(16) < 32,
-        lengths_at(lax.rem(p, 8) * 4, 4, 2, 0),
-        lengths_at(lax.rem(q, 8) * 4, 4, 3, 32),
-    )
-    square = jnp.concatenate([lengths_at(16 * core, 16, 1, 0), lane_len[2], jnp.zeros((96, 128), F32)], 0)
+        lengths_at(lax.rem(p, 8) * 4, 1, 2),
+        shift_lanes(lengths_at(lax.rem(q, 8) * 4, 1, 3), 32),
+    )
+    square = jnp.concatenate([lengths_at(16 * core, 4, 1), lane_len[2], jnp.zeros((96, 128), F32)], 0)
     turned[...] = square.T
     rt[:, 0:64] = rows[...].T
 
     for i, pivot in enumerate((p, q)):
+        home = pivot // 64 * 8
         for n in range(HOLDERS):
             at = 32 * i + 4 * n
-            group = pivot // 32
+            base = home + 4 * (n // 4) + n // 2 % 2
             for b in range(2):
-                part = zed[n % 2, 4 * (group // 2 * 2 + b) + n // 2, 0:Z_L]
+                part = zed[n % 2, base + 2 * b, 0:Z_L]
                 ct[at + 2 * b : at + 2 * b + 2, 0:128] = part[4 * i : 4 * i + 2]
                 ct[at + 2 * b : at + 2 * b + 2, 128:256] = part[4 * i + 2 : 4 * i + 4]
-            kt[at : at + 4, :] = shift_lanes(zed[n % 2, 4 * group + n // 2, Z_L:Z_ROWS], 64 * i)[4:8]
+            corner = zed[n % 2, base + 2 * lax.rem(pivot // 16, 2), Z_L:Z_ROWS]
+            kt[at : at + 4, :] = shift_lanes(corner, 64 * i)[4:8]
 
     lane = lanes(8)
     sub = lax.broadcasted_iota(jnp.int32, (8, 128), 0)
@@ -340,19 +343,20 @@
         [SM] + [VM] * 4,
     )(*[pltpu.with_memory_space_constraint(x, pltpu.HBM) for x in (pivots, distances, edge_lengths.T)])
     other_panel = lax.ppermute(panel, "row", [(i, i ^ 1) for i in range(NXY)])
-    scatter = lax.all_to_all(scatter, ("zl", "core"), 0, 0)
+    scatter = lax.all_to_all(scatter, ("z2", "z0", "core"), 0, 0)
     xy, keep, send = call(spread_kernel, [(NXY, XY_ROWS, 128), (8, 128), (8, 128)], [], [SM] + [VM] * 4, 8)(
         piv, scatter, own_lengths, panel, other_panel
     )
-    other_half = lax.ppermute(send, "zh", [(i, i ^ 1) for i in range(4)])
+    other_half = lax.ppermute(send, "z1", [(0, 1), (1, 0)])
     lane_ids, sub_ids, onehot = call(
         ids_kernel, [(3, 16, 128), (24, NEIGHBORS, 8, 128), ONEHOT], [(128, 128)], [SM, VM], 16
     )(piv, neighbor_ids)
     xy = lax.all_to_all(xy, "row", 0, 0)
-    zed, rows = call(gather_kernel, [(NZ, Z_ROWS, 128), (64, 128)], [(128, 128)], [SM] + [VM] * 3, 8)(
+    xy, lane_ids, sub_ids, onehot = lax.optimization_barrier((xy, lane_ids, sub_ids, onehot))
+    zed, rows = call(gather_kernel, [(NZ, Z_ROWS, 128), (64, 128)], [], [SM] + [VM] * 3, 8)(
         piv, xy, keep, other_half
     )
-    zed = lax.all_to_all(zed, ("zh", "zl"), 0, 0)
+    zed = lax.all_to_all(zed, ("z3", "z2", "z1", "z0"), 0, 0)
     zed = lax.all_gather(zed, "core")
     (out,) = call(final_kernel, [(ROWS, COLS)], FINAL_SCRATCH, [SM] + [VM] * 6, 24)(
         piv, mt, rows, zed, lane_ids, sub_ids, onehot
@@ -361,7 +365,7 @@
 
 
 def solution(mesh):
-    fine = Mesh(mesh.devices.reshape(16, 4, 4, 2), ("row", "zh", "zl", "core"))
-    cols = ("zh", "zl", "core")
+    fine = Mesh(mesh.devices.reshape(16, 2, 2, 2, 2, 2), ("row", "z3", "z2", "z1", "z0", "core"))
+    cols = ("z3", "z2", "z1", "z0", "core")
     placed = (P("row", cols), P(), P(None, ("row", *cols)), P())
     return jax.shard_map(on_device, mesh=fine, in_specs=placed, out_specs=P("row", cols), check_vma=False)

time: 67.3 us -> 70.9 us (1.053)
  blocking collectives: 5.91 us -> 27.9 us
  starting transfers between devices: 35.3 us -> 26.3 us
  waiting for transfers between devices: 15.2 us -> 6.56 us
  Pallas kernels: 10.4 us -> 9.64 us
    all_to_all x0 -> x1, blocking collectives: none -> 22.2 us  [on_device(): zed = lax.all_to_all(zed, ('z3', 'z2', 'z1', 'z0'), 0, 0)]
    all_to_all x2 -> x1, starting transfers between devices: 20.6 us -> 11.3 us  [on_device(): scatter = lax.all_to_all(scatter, ('z2', 'z0', 'core'), 0, 0)]
    all_to_all x2 -> x1, waiting for transfers between devices: 10.9 us -> 3.14 us  [on_device(): scatter = lax.all_to_all(scatter, ('z2', 'z0', 'core'), 0, 0)]
    ppermute x1, starting transfers between devices: 8.82 us -> 4.9 us  [on_device(): other_half = lax.ppermute(send, 'z1', [(0, 1), (1, 0)])]
    all_to_all x1, starting transfers between devices: 3.99 us -> 6.89 us  [on_device(): xy = lax.all_to_all(xy, 'row', 0, 0)]
    all_to_all x1, waiting for transfers between devices: 0.01 us -> 1.68 us  [on_device(): xy = lax.all_to_all(xy, 'row', 0, 0)]
    ppermute x1, starting transfers between devices: 1.91 us -> 3.19 us  [on_device(): other_panel = lax.ppermute(panel, 'row', [(i, i ^ 1) for i in range(NXY)])]
    ppermute x1, waiting for transfers between devices: 3.03 us -> 1.74 us  [on_device(): other_panel = lax.ppermute(panel, 'row', [(i, i ^ 1) for i in range(NXY)])]
  transfers between devices with their start and end apart: 5 -> 4, of which waited for: 4 -> 3; matrix products, arithmetic and copies ran while one was open for 0% -> 0% of each run, Pallas kernels for 2% -> 2%
where the time goes in v8:
time: 70.9 us; the launch traced here: 70.5 us
  blocking collectives  27.9 us (39%)
  starting transfers between devices  26.3 us (37%)
  Pallas kernels  9.64 us (14%)
  waiting for transfers between devices  6.56 us (9%)
    all_to_all x1, blocking collectives, on_device(): zed = lax.all_to_all(zed, ('z3', 'z2', 'z1', 'z0'), 0, 0)  22.2 us
    all_to_all x1, starting transfers between devices, on_device(): scatter = lax.all_to_all(scatter, ('z2', 'z0', 'core'), 0, 0)  11.3 us
    all_to_all x1, starting transfers between devices, on_device(): xy = lax.all_to_all(xy, 'row', 0, 0)  6.89 us
    all_gather x1, blocking collectives, on_device(): zed = lax.all_gather(zed, 'core')  5.69 us
    ppermute x1, starting transfers between devices, on_device(): other_half = lax.ppermute(send, 'z1', [(0, 1), (1, 0)])  4.9 us
    pallas_call x1, Pallas kernels, on_device(): call(final_kernel, [(ROWS, COLS)], FINAL_SCRATCH, [SM] + [VM] * 6, 24)  4.64 us
    ppermute x1, starting transfers between devices, on_device(): other_panel = lax.ppermute(panel, 'row', [(i, i ^ 1) for i in range(NXY)])  3.19 us
    all_to_all x1, waiting for transfers between devices, on_device(): scatter = lax.all_to_all(scatter, ('z2', 'z0', 'core'), 0, 0)  3.14 us
  transfers between devices with their start and end apart: 4, of which 3 were waited for; matrix products, arithmetic and copies ran while one was open for 0% of the time, Pallas kernels for 2%

profile of v8, /device:TPU:1, one launch (start us, length us, event | category | flops | bytes accessed | tf_op | source)
XLA Modules:
  0.0 70.5 jit_solution(18168400830577510725)
XLA Ops:
  0.0 1.7 %shard_map.46 = (s32[2]{0:T(128)S(1)}, f32[128,256]{1,0:T(8,128)S(1)}, f32[8,16,128]{2,1,0:T(8,128)}, f32[64,128]{1,0:T(8,128)S(1)}, f32[8,128]{1,0:T(8,128)S(1)}) custom-call(s32[2]{0:T(128)} %pivots.1, f32[256,128]{1,0:T(8,128)} %dist.1, f32[8,10]{1,0:T(8,128)} %bitcast.3), custom_call_target="tpu_custom_call" | custom-call | tf_op jit(solution)/shard_map/pallas_call | solution.py:337
  1.7 11.3 %all-to-all-start = ((f32[8,16,128]{2,1,0:T(8,128)}), f32[8,16,128]{2,1,0:T(8,128)S(1)}, u32[]{:S(2)}, u32[]{:S(2)}) async-start(f32[8,16,128]{2,1,0:T(8,128)} %get-tuple-element.24), calls=%async_computation | async-start | bytes 131072 | tf_op jit(solution)/shard_map/all_to_all | solution.py:346
  13.0 3.2 %collective-permute-start = (f32[64,128]{1,0:T(8,128)S(1)}, f32[64,128]{1,0:T(8,128)S(1)}, u32[]{:S(2)}, u32[]{:S(2)}) collective-permute-start(f32[64,128]{1,0:T(8,128)S(1)} %get-tuple-element.26.panel), channel_id=1, source_target_pairs={{0,32},{32,0},{64,96},{96,64},{128,160},{160,128},{192,224},{224,1... | collective-permute-start | bytes 98312 | tf_op jit(solution)/shard_map/ppermute | solution.py:345
  16.2 1.7 %collective-permute-done.other_panel = f32[64,128]{1,0:T(8,128)S(1)} collective-permute-done((f32[64,128]{1,0:T(8,128)S(1)}, f32[64,128]{1,0:T(8,128)S(1)}, u32[]{:S(2)}, u32[]{:S(2)}) %collective-permute-start) | collective-permute-done | bytes 32800 | tf_op jit(solution)/shard_map/ppermute | solution.py:345
  18.0 3.1 %all-to-all-done.got = f32[8,16,128]{2,1,0:T(8,128)S(1)} async-done(((f32[8,16,128]{2,1,0:T(8,128)}), f32[8,16,128]{2,1,0:T(8,128)S(1)}, u32[]{:S(2)}, u32[]{:S(2)}) %all-to-all-start) | async-done | bytes 65568 | tf_op jit(solution)/shard_map/all_to_all | solution.py:346
  21.1 1.4 %shard_map.47 = (f32[16,40,128]{2,1,0:T(8,128)}, f32[8,128]{1,0:T(8,128)S(1)}, f32[8,128]{1,0:T(8,128)S(1)}) custom-call(s32[2]{0:T(128)S(1)} %get-tuple-element.22.piv, f32[8,16,128]{2,1,0:T(8,128)S(1)} %all-to-all-done.got, f32[8,128]{1,0:T(8,128)S(1)} %get-tuple-element.25.own_lengths, f32[64,128]{1,0:T(8,128)S(1)} %get-tuple-element.26.panel, ...), custom_call_target="tpu_custom_call" | custom-call | tf_op jit(solution)/shard_map/pallas_call | solution.py:347
  22.5 0.0 copy-start
  22.5 6.9 %all-to-all-start.1 = ((f32[16,40,128]{2,1,0:T(8,128)}), f32[16,40,128]{2,1,0:T(8,128)S(1)}, u32[]{:S(2)}, u32[]{:S(2)}) async-start(f32[16,40,128]{2,1,0:T(8,128)} %get-tuple-element.27), calls=%async_computation.1 | async-start | bytes 655360 | tf_op jit(solution)/shard_map/all_to_all | solution.py:354
  29.4 4.9 %collective-permute-start.1 = (f32[8,128]{1,0:T(8,128)S(1)}, f32[8,128]{1,0:T(8,128)S(1)}, u32[]{:S(2)}, u32[]{:S(2)}) collective-permute-start(f32[8,128]{1,0:T(8,128)S(1)} %get-tuple-element.33), channel_id=1, source_target_pairs={{0,4},{4,0},{1,5},{5,1},{2,6},{6,2},{3,7},{7,3},{8,12},{12,8},{9,1... | collective-permute-start | bytes 12296 | tf_op jit(solution)/shard_map/ppermute | solution.py:350
  34.3 0.0 copy-done
  34.4 1.2 %shard_map.48 = (f32[3,16,128]{2,1,0:T(8,128)S(1)}, f32[24,10,8,128]{3,2,1,0:T(8,128)S(1)}, bf16[64,2048]{1,0:T(8,128)(2,1)S(1)}) custom-call(s32[2]{0:T(128)S(1)} %get-tuple-element.22.piv, s32[10,4096]{1,0:T(8,128)S(1)} %copy-done), custom_call_target="tpu_custom_call" | custom-call | tf_op jit(solution)/shard_map/pallas_call | solution.py:351
  35.6 1.7 %all-to-all-done.1.xy = f32[16,40,128]{2,1,0:T(8,128)S(1)} async-done(((f32[16,40,128]{2,1,0:T(8,128)}), f32[16,40,128]{2,1,0:T(8,128)S(1)}, u32[]{:S(2)}, u32[]{:S(2)}) %all-to-all-start.1) | async-done | bytes 327712 | tf_op jit(solution)/shard_map/all_to_all | solution.py:354
  37.2 0.0 collective-permute-done.1.other
  37.2 0.7 shard_map.49
  37.9 22.2 %all_to_all.15 = f32[16,16,128]{2,1,0:T(8,128)S(1)} all-to-all(f32[16,16,128]{2,1,0:T(8,128)S(1)} %get-tuple-element.35), channel_id=1, replica_groups=mesh['row'=16,'z3'=2,'z2'=2,'z1'=2,'z0'=2,'core'=2] {'z3','z2','z1','z0'}, dimensions={0} | all-to-all | bytes 262144 | tf_op jit(solution)/shard_map/all_to_all | solution.py:359
  60.2 5.7 %all-gather = f32[32,16,128]{2,1,0:T(8,128)S(1)} all-gather(f32[16,16,128]{2,1,0:T(8,128)S(1)} %all_to_all.15), channel_id=2, replica_groups=mesh['row'=16,'z3'=2,'z2'=2,'z1'=2,'z0'=2,'core'=2] {'core'}, dimensions={0}, use_global_device_ids=true | all-gather | bytes 393216 | tf_op jit(solution)/shard_map/all_gather | solution.py:360
  65.9 4.6 %shard_map.50 = f32[256,128]{1,0:T(8,128)} custom-call(s32[2]{0:T(128)S(1)} %get-tuple-element.22.piv, f32[128,256]{1,0:T(8,128)S(1)} %get-tuple-element.23.mt, f32[64,128]{1,0:T(8,128)S(1)} %get-tuple-element.34.rows, f32[2,16,16,128]{3,2,1,0:T(8,128)S(1)} %bitcast.2, f32[3,16,128]{2,1,0:T(8,128)S(1)} %get-tuple-element.36.lane_ids, ...), custom_call_target="tpu_custom_call" | custom-call | tf_op jit(solution)/shard_map/pallas_call | solution.py:361
Async XLA Ops:
  1.7 19.4 %all-to-all-start = ((f32[8,16,128]{2,1,0:T(8,128)}), f32[8,16,128]{2,1,0:T(8,128)S(1)}, u32[]{:S(2)}, u32[]{:S(2)}) async-start(f32[8,16,128]{2,1,0:T(8,128)} %get-tuple-element.24), calls=%async_computation | async-start | bytes 131072 | tf_op jit(solution)/shard_map/all_to_all | solution.py:346
  13.0 4.9 %collective-permute-start = (f32[64,128]{1,0:T(8,128)S(1)}, f32[64,128]{1,0:T(8,128)S(1)}, u32[]{:S(2)}, u32[]{:S(2)}) collective-permute-start(f32[64,128]{1,0:T(8,128)S(1)} %get-tuple-element.26.panel), channel_id=1, source_target_pairs={{0,32},{32,0},{64,96},{96,64},{128,160},{160,128},{192,224},{224,1... | collective-permute-start | bytes 98312 | tf_op jit(solution)/shard_map/ppermute | solution.py:345
  22.5 11.8 %copy-start = (s32[10,4096]{1,0:T(8,128)S(1)}, s32[10,4096]{1,0:T(8,128)}, u32[]{:S(2)}) copy-start(s32[10,4096]{1,0:T(8,128)} %ids.1) | copy-start | bytes 491524
  22.5 14.7 %all-to-all-start.1 = ((f32[16,40,128]{2,1,0:T(8,128)}), f32[16,40,128]{2,1,0:T(8,128)S(1)}, u32[]{:S(2)}, u32[]{:S(2)}) async-start(f32[16,40,128]{2,1,0:T(8,128)} %get-tuple-element.27), calls=%async_computation.1 | async-start | bytes 655360 | tf_op jit(solution)/shard_map/all_to_all | solution.py:354
  29.4 7.8 %collective-permute-start.1 = (f32[8,128]{1,0:T(8,128)S(1)}, f32[8,128]{1,0:T(8,128)S(1)}, u32[]{:S(2)}, u32[]{:S(2)}) collective-permute-start(f32[8,128]{1,0:T(8,128)S(1)} %get-tuple-element.33), channel_id=1, source_target_pairs={{0,4},{4,0},{1,5},{5,1},{2,6},{6,2},{3,7},{7,3},{8,12},{12,8},{9,1... | collective-permute-start | bytes 12296 | tf_op jit(solution)/shard_map/ppermute | solution.py:350

commit v9 on v8

--- a/solution.py
+++ b/solution.py
@@ -14,7 +14,7 @@
 F32 = jnp.float32
 INF = float("inf")
 
-XY_P, XY_Q, XY_ROWS = 8, 24, 40
+XY_P, XY_Q, XY_ROWS = 8, 40, 72
 Z_L, Z_ROWS = 8, 16
 HOLDERS = 8
 
@@ -67,12 +67,12 @@
     own_lengths[...] = low + shift_lanes(pltpu.roll(low, 4, 0), 32) + shift_lanes(high, 64)
 
 
-def spread_kernel(piv, got, own_lengths, panel, other_panel, xy, keep, send):
+def spread_kernel(piv, got, own_lengths, panel, xy, keep, send):
     p, q = piv[0], piv[1]
-    row, z, _ = place()
+    _, z, _ = place()
     corner, halves = None, [[], []]
     for i, pivot in enumerate((p, q)):
-        holder = lax.rem(pivot // 32, 2) * 4 + lax.rem(pivot // 8, 2) * 2 + lax.rem(pivot // 4, 2)
+        holder = lax.rem(pivot // 4, HOLDERS)
         mine = got[holder, 8 * i : 8 * i + 8]
         for b in range(2):
             halves[b] += [mine[2 * b : 2 * b + 2], mine[4 + 2 * b : 6 + 2 * b]]
@@ -81,38 +81,27 @@
             half = shift_lanes(half, 64 * i + 32 * j - lax.rem(other, 4) * PIVOT)
             corner = half if corner is None else jnp.where(lanes(8) // PIVOT == 2 * i + j, half, corner)
     first, second = [jnp.concatenate(parts, 0) for parts in halves]
-    even = lax.rem(z // 2, 2) == 0
+    even = lax.rem(z // 4, 2) == 0
     keep[...] = jnp.where(even, first, second)
     send[...] = jnp.where(even, second, first)
     small = jnp.where(upper_half(), own_lengths[...], pltpu.roll(corner, 4, 0))
-    part = pl.multiple_of(16 * lax.rem(row, 2), 16)
-    lines = [
-        jnp.where(
-            lax.rem(pivot // 8 + row, 2) == 0,
-            panel[pl.ds(32 * i + part, 16), :],
-            other_panel[pl.ds(32 * i + part, 16), :],
-        )
-        for i, pivot in enumerate((p, q))
-    ]
     for d in range(NXY):
         xy[d, 0:XY_P] = small
-        xy[d, XY_P:XY_Q] = lines[0]
-        xy[d, XY_Q:XY_ROWS] = lines[1]
+        xy[d, XY_P:XY_ROWS] = panel[...]
 
 
 def gather_kernel(piv, xy, keep, other, zchunk, rows):
     p, q = piv[0], piv[1]
     row, z, core = place()
     row_p, row_q = p // 8, q // 8
-    for b in range(2):
-        rows[16 * b : 16 * b + 16] = xy[row_p // 2 * 2 + b, XY_P:XY_Q]
-        rows[32 + 16 * b : 48 + 16 * b] = xy[row_q // 2 * 2 + b, XY_Q:XY_ROWS]
+    rows[0:32] = xy[row_p, XY_P:XY_Q]
+    rows[32:64] = xy[row_q, XY_Q:XY_ROWS]
     upper = upper_half()
-    bit = lax.rem(z // 2, 2)
+    bit = lax.rem(z // 4, 2)
     piece = jnp.where(
         upper,
-        jnp.where(lax.rem(p // 16, 2) == bit, keep[...], other[...]),
-        jnp.where(lax.rem(q // 16, 2) == bit, keep[...], other[...]),
+        jnp.where(lax.rem(p // 32, 2) == bit, keep[...], other[...]),
+        jnp.where(lax.rem(q // 32, 2) == bit, keep[...], other[...]),
     )
     corner = jnp.where(lax.rem(lanes(8) // PIVOT, 2) == 0, xy[row_p, 0:XY_P], xy[row_q, 0:XY_P])
     turn = 2 * lax.rem(z, 2) + core
@@ -235,12 +224,12 @@
         home = pivot // 64 * 8
         for n in range(HOLDERS):
             at = 32 * i + 4 * n
-            base = home + 4 * (n // 4) + n // 2 % 2
+            base = home + n // 2
             for b in range(2):
-                part = zed[n % 2, base + 2 * b, 0:Z_L]
+                part = zed[n % 2, base + 4 * b, 0:Z_L]
                 ct[at + 2 * b : at + 2 * b + 2, 0:128] = part[4 * i : 4 * i + 2]
                 ct[at + 2 * b : at + 2 * b + 2, 128:256] = part[4 * i + 2 : 4 * i + 4]
-            corner = zed[n % 2, base + 2 * lax.rem(pivot // 16, 2), Z_L:Z_ROWS]
+            corner = zed[n % 2, base + 4 * lax.rem(pivot // 32, 2), Z_L:Z_ROWS]
             kt[at : at + 4, :] = shift_lanes(corner, 64 * i)[4:8]
 
     lane = lanes(8)
@@ -342,12 +331,11 @@
         8,
         [SM] + [VM] * 4,
     )(*[pltpu.with_memory_space_constraint(x, pltpu.HBM) for x in (pivots, distances, edge_lengths.T)])
-    other_panel = lax.ppermute(panel, "row", [(i, i ^ 1) for i in range(NXY)])
-    scatter = lax.all_to_all(scatter, ("z2", "z0", "core"), 0, 0)
-    xy, keep, send = call(spread_kernel, [(NXY, XY_ROWS, 128), (8, 128), (8, 128)], [], [SM] + [VM] * 4, 8)(
-        piv, scatter, own_lengths, panel, other_panel
-    )
-    other_half = lax.ppermute(send, "z1", [(0, 1), (1, 0)])
+    scatter = lax.all_to_all(scatter, ("z1", "z0", "core"), 0, 0)
+    xy, keep, send = call(spread_kernel, [(NXY, XY_ROWS, 128), (8, 128), (8, 128)], [], [SM] + [VM] * 3, 8)(
+        piv, scatter, own_lengths, panel
+    )
+    other_half = lax.ppermute(send, "z2", [(0, 1), (1, 0)])
     lane_ids, sub_ids, onehot = call(
         ids_kernel, [(3, 16, 128), (24, NEIGHBORS, 8, 128), ONEHOT], [(128, 128)], [SM, VM], 16
     )(piv, neighbor_ids)

time: 70.9 us -> 68.6 us (0.968)
  blocking collectives: 27.9 us -> 44.1 us
  starting transfers between devices: 26.3 us -> 13.6 us
  waiting for transfers between devices: 6.56 us -> 0.98 us
    all_to_all x0 -> x1, blocking collectives: none -> 14.3 us  [on_device(): scatter = lax.all_to_all(scatter, ('z1', 'z0', 'core'), 0, 0)]
    all_to_all x1 -> x0, starting transfers between devices: 11.3 us -> none  [on_device(): scatter = lax.all_to_all(scatter, ('z2', 'z0', 'core'), 0, 0)]
    all_to_all x1 -> x0, waiting for transfers between devices: 3.14 us -> none  [on_device(): scatter = lax.all_to_all(scatter, ('z2', 'z0', 'core'), 0, 0)]
    all_to_all x1, starting transfers between devices: 6.89 us -> 4.83 us  [on_device(): xy = lax.all_to_all(xy, 'row', 0, 0)]
    all_to_all x1, blocking collectives: 22.2 us -> 24 us  [on_device(): zed = lax.all_to_all(zed, ('z3', 'z2', 'z1', 'z0'), 0, 0)]
    ppermute x2 -> x1, waiting for transfers between devices: 1.74 us -> 0.01 us  [on_device(): other_half = lax.ppermute(send, 'z2', [(0, 1), (1, 0)])]
    ppermute x2 -> x1, starting transfers between devices: 8.09 us -> 8.82 us  [on_device(): other_half = lax.ppermute(send, 'z2', [(0, 1), (1, 0)])]
  transfers between devices with their start and end apart: 4 -> 2, of which waited for: 3 -> 1; matrix products, arithmetic and copies ran while one was open for 0% -> 0% of each run, Pallas kernels for 2% -> 2%
where the time goes in v9:
time: 68.6 us; the launch traced here: 68.2 us
  blocking collectives  44.1 us (64%)
  starting transfers between devices  13.6 us (20%)
  Pallas kernels  9.52 us (14%)
  waiting for transfers between devices  0.98 us (1%)
    all_to_all x1, blocking collectives, on_device(): zed = lax.all_to_all(zed, ('z3', 'z2', 'z1', 'z0'), 0, 0)  24 us
    all_to_all x1, blocking collectives, on_device(): scatter = lax.all_to_all(scatter, ('z1', 'z0', 'core'), 0, 0)  14.3 us
    ppermute x1, starting transfers between devices, on_device(): other_half = lax.ppermute(send, 'z2', [(0, 1), (1, 0)])  8.82 us
    all_gather x1, blocking collectives, on_device(): zed = lax.all_gather(zed, 'core')  5.72 us
    all_to_all x1, starting transfers between devices, on_device(): xy = lax.all_to_all(xy, 'row', 0, 0)  4.83 us
    pallas_call x1, Pallas kernels, on_device(): call(final_kernel, [(ROWS, COLS)], FINAL_SCRATCH, [SM] + [VM] * 6, 24)  4.64 us
    pallas_call x1, Pallas kernels, on_device(): call(pack_kernel, [PIVOTS, (COLS, ROWS), (HOLDERS, 16, 128), (64, 128), (...  1.53 us
    pallas_call x1, Pallas kernels, on_device(): call(spread_kernel, [(NXY, XY_ROWS, 128), (8, 128), (8, 128)], [], [SM] +...  1.46 us
  transfers between devices with their start and end apart: 2, of which 1 were waited for; matrix products, arithmetic and copies ran while one was open for 0% of the time, Pallas kernels for 2%

profile of v9, /device:TPU:1, one launch (start us, length us, event | category | flops | bytes accessed | tf_op | source)
XLA Modules:
  0.0 68.2 jit_solution(13460545866543017817)
XLA Ops:
  0.0 1.5 %shard_map.46 = (s32[2]{0:T(128)S(1)}, f32[128,256]{1,0:T(8,128)S(1)}, f32[8,16,128]{2,1,0:T(8,128)S(1)}, f32[64,128]{1,0:T(8,128)S(1)}, f32[8,128]{1,0:T(8,128)S(1)}) custom-call(s32[2]{0:T(128)} %pivots.1, f32[256,128]{1,0:T(8,128)} %dist.1, f32[8,10]{1,0:T(8,128)} %bitcast.3), custom_call_target="tpu_custom_call" | custom-call | tf_op jit(solution)/shard_map/pallas_call | solution.py:326
  1.5 14.3 %all_to_all.15.got = f32[8,16,128]{2,1,0:T(8,128)S(1)} all-to-all(f32[8,16,128]{2,1,0:T(8,128)S(1)} %get-tuple-element.24), channel_id=1, replica_groups=mesh['row'=16,'z3'=2,'z2'=2,'z1'=2,'z0'=2,'core'=2] {'z1','z0','core'}, dimensions={0} | all-to-all | bytes 131072 | tf_op jit(solution)/shard_map/all_to_all | solution.py:334
  15.9 1.5 %shard_map.47 = (f32[16,72,128]{2,1,0:T(8,128)}, f32[8,128]{1,0:T(8,128)S(1)}, f32[8,128]{1,0:T(8,128)S(1)}) custom-call(s32[2]{0:T(128)S(1)} %get-tuple-element.22.piv, f32[8,16,128]{2,1,0:T(8,128)S(1)} %all_to_all.15.got, f32[8,128]{1,0:T(8,128)S(1)} %get-tuple-element.25.own_lengths, f32[64,128]{1,0:T(8,128)S(1)} %get-tuple-element.26.panel), custom_call_target="tpu_custom_call" | custom-call | tf_op jit(solution)/shard_map/pallas_call | solution.py:335
  17.3 0.0 copy-start
  17.3 4.8 %all-to-all-start.1 = ((f32[16,72,128]{2,1,0:T(8,128)}), f32[16,72,128]{2,1,0:T(8,128)S(1)}, u32[]{:S(2)}, u32[]{:S(2)}) async-start(f32[16,72,128]{2,1,0:T(8,128)} %get-tuple-element.27), calls=%async_computation.1 | async-start | bytes 1179648 | tf_op jit(solution)/shard_map/all_to_all | solution.py:342
  22.2 8.8 %collective-permute-start = (f32[8,128]{1,0:T(8,128)S(1)}, f32[8,128]{1,0:T(8,128)S(1)}, u32[]{:S(2)}, u32[]{:S(2)}) collective-permute-start(f32[8,128]{1,0:T(8,128)S(1)} %get-tuple-element.33), channel_id=1, source_target_pairs={{0,8},{8,0},{1,9},{9,1},{2,10},{10,2},{3,11},{11,3},{4,12},{12,4},... | collective-permute-start | bytes 12296 | tf_op jit(solution)/shard_map/ppermute | solution.py:338
  31.0 0.0 copy-done
  31.0 1.2 %shard_map.48 = (f32[3,16,128]{2,1,0:T(8,128)S(1)}, f32[24,10,8,128]{3,2,1,0:T(8,128)S(1)}, bf16[64,2048]{1,0:T(8,128)(2,1)S(1)}) custom-call(s32[2]{0:T(128)S(1)} %get-tuple-element.22.piv, s32[10,4096]{1,0:T(8,128)S(1)} %copy-done), custom_call_target="tpu_custom_call" | custom-call | tf_op jit(solution)/shard_map/pallas_call | solution.py:339
  32.2 1.0 %all-to-all-done.1.xy = f32[16,72,128]{2,1,0:T(8,128)S(1)} async-done(((f32[16,72,128]{2,1,0:T(8,128)}), f32[16,72,128]{2,1,0:T(8,128)S(1)}, u32[]{:S(2)}, u32[]{:S(2)}) %all-to-all-start.1) | async-done | bytes 589856 | tf_op jit(solution)/shard_map/all_to_all | solution.py:342
  33.2 0.0 collective-permute-done.other
  33.2 0.7 shard_map.49
  33.9 24.0 %all_to_all.16 = f32[16,16,128]{2,1,0:T(8,128)S(1)} all-to-all(f32[16,16,128]{2,1,0:T(8,128)S(1)} %get-tuple-element.35), channel_id=1, replica_groups=mesh['row'=16,'z3'=2,'z2'=2,'z1'=2,'z0'=2,'core'=2] {'z3','z2','z1','z0'}, dimensions={0} | all-to-all | bytes 262144 | tf_op jit(solution)/shard_map/all_to_all | solution.py:347
  57.9 5.7 %all-gather = f32[32,16,128]{2,1,0:T(8,128)S(1)} all-gather(f32[16,16,128]{2,1,0:T(8,128)S(1)} %all_to_all.16), channel_id=2, replica_groups=mesh['row'=16,'z3'=2,'z2'=2,'z1'=2,'z0'=2,'core'=2] {'core'}, dimensions={0}, use_global_device_ids=true | all-gather | bytes 393216 | tf_op jit(solution)/shard_map/all_gather | solution.py:348
  63.6 4.6 %shard_map.50 = f32[256,128]{1,0:T(8,128)} custom-call(s32[2]{0:T(128)S(1)} %get-tuple-element.22.piv, f32[128,256]{1,0:T(8,128)S(1)} %get-tuple-element.23.mt, f32[64,128]{1,0:T(8,128)S(1)} %get-tuple-element.34.rows, f32[2,16,16,128]{3,2,1,0:T(8,128)S(1)} %bitcast.2, f32[3,16,128]{2,1,0:T(8,128)S(1)} %get-tuple-element.36.lane_ids, ...), custom_call_target="tpu_custom_call" | custom-call | tf_op jit(solution)/shard_map/pallas_call | solution.py:349
Async XLA Ops:
  17.3 13.7 %copy-start = (s32[10,4096]{1,0:T(8,128)S(1)}, s32[10,4096]{1,0:T(8,128)}, u32[]{:S(2)}) copy-start(s32[10,4096]{1,0:T(8,128)} %ids.1) | copy-start | bytes 491524
  17.3 15.8 %all-to-all-start.1 = ((f32[16,72,128]{2,1,0:T(8,128)}), f32[16,72,128]{2,1,0:T(8,128)S(1)}, u32[]{:S(2)}, u32[]{:S(2)}) async-start(f32[16,72,128]{2,1,0:T(8,128)} %get-tuple-element.27), calls=%async_computation.1 | async-start | bytes 1179648 | tf_op jit(solution)/shard_map/all_to_all | solution.py:342
  22.2 11.0 %collective-permute-start = (f32[8,128]{1,0:T(8,128)S(1)}, f32[8,128]{1,0:T(8,128)S(1)}, u32[]{:S(2)}, u32[]{:S(2)}) collective-permute-start(f32[8,128]{1,0:T(8,128)S(1)} %get-tuple-element.33), channel_id=1, source_target_pairs={{0,8},{8,0},{1,9},{9,1},{2,10},{10,2},{3,11},{11,3},{4,12},{12,4},... | collective-permute-start | bytes 12296 | tf_op jit(solution)/shard_map/ppermute | solution.py:338

commit v10 on v8

--- a/solution.py
+++ b/solution.py
@@ -15,7 +15,7 @@
 INF = float("inf")
 
 XY_P, XY_Q, XY_ROWS = 8, 24, 40
-Z_L, Z_ROWS = 8, 16
+Z_L, Z_ROWS = 16, 24
 HOLDERS = 8
 
 
@@ -67,23 +67,18 @@
     own_lengths[...] = low + shift_lanes(pltpu.roll(low, 4, 0), 32) + shift_lanes(high, 64)
 
 
-def spread_kernel(piv, got, own_lengths, panel, other_panel, xy, keep, send):
+def spread_kernel(piv, got, own_lengths, panel, other_panel, xy, piece):
     p, q = piv[0], piv[1]
-    row, z, _ = place()
-    corner, halves = None, [[], []]
+    row, _, _ = place()
+    corner = None
     for i, pivot in enumerate((p, q)):
-        holder = lax.rem(pivot // 32, 2) * 4 + lax.rem(pivot // 8, 2) * 2 + lax.rem(pivot // 4, 2)
+        holder = lax.rem(pivot // 4, HOLDERS)
         mine = got[holder, 8 * i : 8 * i + 8]
-        for b in range(2):
-            halves[b] += [mine[2 * b : 2 * b + 2], mine[4 + 2 * b : 6 + 2 * b]]
+        piece[8 * i : 8 * i + 8, :] = mine
         for j, other in enumerate((p, q)):
             half = jnp.where(lax.rem(other // 4, 2) == 0, mine, pltpu.roll(mine, 4, 0))
             half = shift_lanes(half, 64 * i + 32 * j - lax.rem(other, 4) * PIVOT)
             corner = half if corner is None else jnp.where(lanes(8) // PIVOT == 2 * i + j, half, corner)
-    first, second = [jnp.concatenate(parts, 0) for parts in halves]
-    even = lax.rem(z // 2, 2) == 0
-    keep[...] = jnp.where(even, first, second)
-    send[...] = jnp.where(even, second, first)
     small = jnp.where(upper_half(), own_lengths[...], pltpu.roll(corner, 4, 0))
     part = pl.multiple_of(16 * lax.rem(row, 2), 16)
     lines = [
@@ -100,7 +95,7 @@
         xy[d, XY_Q:XY_ROWS] = lines[1]
 
 
-def gather_kernel(piv, xy, keep, other, zchunk, rows):
+def gather_kernel(piv, xy, piece, zchunk, rows):
     p, q = piv[0], piv[1]
     row, z, core = place()
     row_p, row_q = p // 8, q // 8
@@ -108,12 +103,6 @@
         rows[16 * b : 16 * b + 16] = xy[row_p // 2 * 2 + b, XY_P:XY_Q]
         rows[32 + 16 * b : 48 + 16 * b] = xy[row_q // 2 * 2 + b, XY_Q:XY_ROWS]
     upper = upper_half()
-    bit = lax.rem(z // 2, 2)
-    piece = jnp.where(
-        upper,
-        jnp.where(lax.rem(p // 16, 2) == bit, keep[...], other[...]),
-        jnp.where(lax.rem(q // 16, 2) == bit, keep[...], other[...]),
-    )
     corner = jnp.where(lax.rem(lanes(8) // PIVOT, 2) == 0, xy[row_p, 0:XY_P], xy[row_q, 0:XY_P])
     turn = 2 * lax.rem(z, 2) + core
 
@@ -122,7 +111,7 @@
 
     fixed = take(row, 0) + take(row_p, 2) + take(row_q, 3)
     for d in range(NZ):
-        zchunk[d, 0:Z_L] = piece
+        zchunk[d, 0:Z_L] = piece[...]
         zchunk[d, Z_L:Z_ROWS] = jnp.where(upper, fixed + take(d, 1), corner)
 
 
@@ -232,15 +221,13 @@
     rt[:, 0:64] = rows[...].T
 
     for i, pivot in enumerate((p, q)):
-        home = pivot // 64 * 8
         for n in range(HOLDERS):
             at = 32 * i + 4 * n
-            base = home + 4 * (n // 4) + n // 2 % 2
-            for b in range(2):
-                part = zed[n % 2, base + 2 * b, 0:Z_L]
-                ct[at + 2 * b : at + 2 * b + 2, 0:128] = part[4 * i : 4 * i + 2]
-                ct[at + 2 * b : at + 2 * b + 2, 128:256] = part[4 * i + 2 : 4 * i + 4]
-            corner = zed[n % 2, base + 2 * lax.rem(pivot // 16, 2), Z_L:Z_ROWS]
+            holder = pivot // 32 * 4 + n // 2
+            part = zed[n % 2, holder, 8 * i : 8 * i + 8]
+            ct[at : at + 4, 0:128] = part[0:4]
+            ct[at : at + 4, 128:256] = part[4:8]
+            corner = zed[n % 2, holder, Z_L:Z_ROWS]
             kt[at : at + 4, :] = shift_lanes(corner, 64 * i)[4:8]
 
     lane = lanes(8)
@@ -342,20 +329,17 @@
         8,
         [SM] + [VM] * 4,
     )(*[pltpu.with_memory_space_constraint(x, pltpu.HBM) for x in (pivots, distances, edge_lengths.T)])
-    other_panel = lax.ppermute(panel, "row", [(i, i ^ 1) for i in range(NXY)])
-    scatter = lax.all_to_all(scatter, ("z2", "z0", "core"), 0, 0)
-    xy, keep, send = call(spread_kernel, [(NXY, XY_ROWS, 128), (8, 128), (8, 128)], [], [SM] + [VM] * 4, 8)(
-        piv, scatter, own_lengths, panel, other_panel
-    )
-    other_half = lax.ppermute(send, "z1", [(0, 1), (1, 0)])
     lane_ids, sub_ids, onehot = call(
         ids_kernel, [(3, 16, 128), (24, NEIGHBORS, 8, 128), ONEHOT], [(128, 128)], [SM, VM], 16
     )(piv, neighbor_ids)
+    other_panel = lax.ppermute(panel, "row", [(i, i ^ 1) for i in range(NXY)])
+    scatter = lax.all_to_all(scatter, ("z1", "z0", "core"), 0, 0)
+    scatter, lane_ids, sub_ids, onehot = lax.optimization_barrier((scatter, lane_ids, sub_ids, onehot))
+    xy, piece = call(spread_kernel, [(NXY, XY_ROWS, 128), (16, 128)], [], [SM] + [VM] * 4, 8)(
+        piv, scatter, own_lengths, panel, other_panel
+    )
     xy = lax.all_to_all(xy, "row", 0, 0)
-    xy, lane_ids, sub_ids, onehot = lax.optimization_barrier((xy, lane_ids, sub_ids, onehot))
-    zed, rows = call(gather_kernel, [(NZ, Z_ROWS, 128), (64, 128)], [], [SM] + [VM] * 3, 8)(
-        piv, xy, keep, other_half
-    )
+    zed, rows = call(gather_kernel, [(NZ, Z_ROWS, 128), (64, 128)], [], [SM] + [VM] * 2, 8)(piv, xy, piece)
     zed = lax.all_to_all(zed, ("z3", "z2", "z1", "z0"), 0, 0)
     zed = lax.all_gather(zed, "core")
     (out,) = call(final_kernel, [(ROWS, COLS)], FINAL_SCRATCH, [SM] + [VM] * 6, 24)(

time: 70.9 us -> 66.6 us (0.939)
  blocking collectives: 27.9 us -> 43.3 us
  starting transfers between devices: 26.3 us -> 12.1 us
  waiting for transfers between devices: 6.56 us -> 1.98 us
  Pallas kernels: 9.64 us -> 8.89 us
    all_to_all x0 -> x1, blocking collectives: none -> 11.6 us  [on_device(): xy = lax.all_to_all(xy, 'row', 0, 0)]
    all_to_all x2 -> x1, starting transfers between devices: 18.2 us -> 10.1 us  [on_device(): scatter = lax.all_to_all(scatter, ('z1', 'z0', 'core'), 0, 0)]
    ppermute x1 -> x0, starting transfers between devices: 4.9 us -> none  [on_device(): other_half = lax.ppermute(send, 'z1', [(0, 1), (1, 0)])]
    all_to_all x2 -> x1, waiting for transfers between devices: 4.82 us -> 1.98 us  [on_device(): scatter = lax.all_to_all(scatter, ('z1', 'z0', 'core'), 0, 0)]
    all_to_all x1, blocking collectives: 22.2 us -> 24.4 us  [on_device(): zed = lax.all_to_all(zed, ('z3', 'z2', 'z1', 'z0'), 0, 0)]
    ppermute x1, waiting for transfers between devices: 1.74 us -> 0.01 us  [on_device(): other_panel = lax.ppermute(panel, 'row', [(i, i ^ 1) for i in range(NXY)])]
    all_gather x1, blocking collectives: 5.69 us -> 7.27 us  [on_device(): zed = lax.all_gather(zed, 'core')]
    ppermute x1, starting transfers between devices: 3.19 us -> 1.91 us  [on_device(): other_panel = lax.ppermute(panel, 'row', [(i, i ^ 1) for i in range(NXY)])]
  transfers between devices with their start and end apart: 4 -> 2, of which waited for: 3 -> 1; matrix products, arithmetic and copies ran while one was open for 0% -> 0% of each run, Pallas kernels for 2% -> 2%
where the time goes in v10:
time: 66.6 us; the launch traced here: 66.3 us
  blocking collectives  43.3 us (65%)
  starting transfers between devices  12.1 us (18%)
  Pallas kernels  8.89 us (13%)
  waiting for transfers between devices  1.98 us (3%)
    all_to_all x1, blocking collectives, on_device(): zed = lax.all_to_all(zed, ('z3', 'z2', 'z1', 'z0'), 0, 0)  24.4 us
    all_to_all x1, blocking collectives, on_device(): xy = lax.all_to_all(xy, 'row', 0, 0)  11.6 us
    all_to_all x1, starting transfers between devices, on_device(): scatter = lax.all_to_all(scatter, ('z1', 'z0', 'core'), 0, 0)  10.1 us
    all_gather x1, blocking collectives, on_device(): zed = lax.all_gather(zed, 'core')  7.27 us
    pallas_call x1, Pallas kernels, on_device(): call(final_kernel, [(ROWS, COLS)], FINAL_SCRATCH, [SM] + [VM] * 6, 24)  4.65 us
    all_to_all x1, waiting for transfers between devices, on_device(): scatter = lax.all_to_all(scatter, ('z1', 'z0', 'core'), 0, 0)  1.98 us
    ppermute x1, starting transfers between devices, on_device(): other_panel = lax.ppermute(panel, 'row', [(i, i ^ 1) for i in range(NXY)])  1.91 us
    pallas_call x1, Pallas kernels, on_device(): call(pack_kernel, [PIVOTS, (COLS, ROWS), (HOLDERS, 16, 128), (64, 128), (...  1.74 us
  transfers between devices with their start and end apart: 2, of which 1 were waited for; matrix products, arithmetic and copies ran while one was open for 0% of the time, Pallas kernels for 2%

profile of v10, /device:TPU:1, one launch (start us, length us, event | category | flops | bytes accessed | tf_op | source)
XLA Modules:
  0.0 66.3 jit_solution(14420709760888903866)
XLA Ops:
  0.0 0.0 copy-start
  0.0 1.7 %shard_map.46 = (s32[2]{0:T(128)S(1)}, f32[128,256]{1,0:T(8,128)S(1)}, f32[8,16,128]{2,1,0:T(8,128)}, f32[64,128]{1,0:T(8,128)S(1)}, f32[8,128]{1,0:T(8,128)S(1)}) custom-call(s32[2]{0:T(128)} %pivots.1, f32[256,128]{1,0:T(8,128)} %dist.1, f32[8,10]{1,0:T(8,128)} %bitcast.3), custom_call_target="tpu_custom_call" | custom-call | tf_op jit(solution)/shard_map/pallas_call | solution.py:324
  1.7 10.1 %all-to-all-start = ((f32[8,16,128]{2,1,0:T(8,128)}), f32[8,16,128]{2,1,0:T(8,128)S(1)}, u32[]{:S(2)}, u32[]{:S(2)}) async-start(f32[8,16,128]{2,1,0:T(8,128)} %get-tuple-element.23), calls=%async_computation | async-start | bytes 131072 | tf_op jit(solution)/shard_map/all_to_all | solution.py:336
  11.9 1.9 %collective-permute-start = (f32[64,128]{1,0:T(8,128)S(1)}, f32[64,128]{1,0:T(8,128)S(1)}, u32[]{:S(2)}, u32[]{:S(2)}) collective-permute-start(f32[64,128]{1,0:T(8,128)S(1)} %get-tuple-element.29.panel), channel_id=1, source_target_pairs={{0,32},{32,0},{64,96},{96,64},{128,160},{160,128},{192,224},{224,1... | collective-permute-start | bytes 98312 | tf_op jit(solution)/shard_map/ppermute | solution.py:335
  13.8 0.0 copy-done
  13.8 1.2 %shard_map.47 = (f32[3,16,128]{2,1,0:T(8,128)S(1)}, f32[24,10,8,128]{3,2,1,0:T(8,128)S(1)}, bf16[64,2048]{1,0:T(8,128)(2,1)S(1)}) custom-call(s32[2]{0:T(128)S(1)} %get-tuple-element.21.piv, s32[10,4096]{1,0:T(8,128)S(1)} %copy-done), custom_call_target="tpu_custom_call" | custom-call | tf_op jit(solution)/shard_map/pallas_call | solution.py:332
  15.0 2.0 %all-to-all-done.got = f32[8,16,128]{2,1,0:T(8,128)S(1)} async-done(((f32[8,16,128]{2,1,0:T(8,128)}), f32[8,16,128]{2,1,0:T(8,128)S(1)}, u32[]{:S(2)}, u32[]{:S(2)}) %all-to-all-start) | async-done | bytes 65568 | tf_op jit(solution)/shard_map/all_to_all | solution.py:336
  17.0 0.0 collective-permute-done.other_panel
  17.0 0.6 shard_map.48
  17.6 11.6 %all_to_all.15.xy = f32[16,40,128]{2,1,0:T(8,128)S(1)} all-to-all(f32[16,40,128]{2,1,0:T(8,128)S(1)} %get-tuple-element.30), channel_id=1, replica_groups=mesh['row'=16,'z3'=2,'z2'=2,'z1'=2,'z0'=2,'core'=2] {'row'}, dimensions={0} | all-to-all | bytes 655360 | tf_op jit(solution)/shard_map/all_to_all | solution.py:341
  29.2 0.7 %shard_map.49 = (f32[16,24,128]{2,1,0:T(8,128)S(1)}, f32[64,128]{1,0:T(8,128)S(1)}) custom-call(s32[2]{0:T(128)S(1)} %get-tuple-element.21.piv, f32[16,40,128]{2,1,0:T(8,128)S(1)} %all_to_all.15.xy, f32[16,128]{1,0:T(8,128)S(1)} %get-tuple-element.31.piece), custom_call_target="tpu_custom_call" | custom-call | tf_op jit(solution)/shard_map/pallas_call | solution.py:342
  29.9 24.4 %all_to_all.16 = f32[16,24,128]{2,1,0:T(8,128)S(1)} all-to-all(f32[16,24,128]{2,1,0:T(8,128)S(1)} %get-tuple-element.33), channel_id=1, replica_groups=mesh['row'=16,'z3'=2,'z2'=2,'z1'=2,'z0'=2,'core'=2] {'z3','z2','z1','z0'}, dimensions={0} | all-to-all | bytes 393216 | tf_op jit(solution)/shard_map/all_to_all | solution.py:343
  54.4 7.3 %all-gather = f32[32,24,128]{2,1,0:T(8,128)S(1)} all-gather(f32[16,24,128]{2,1,0:T(8,128)S(1)} %all_to_all.16), channel_id=2, replica_groups=mesh['row'=16,'z3'=2,'z2'=2,'z1'=2,'z0'=2,'core'=2] {'core'}, dimensions={0}, use_global_device_ids=true | all-gather | bytes 589824 | tf_op jit(solution)/shard_map/all_gather | solution.py:344
  61.6 4.6 %shard_map.50 = f32[256,128]{1,0:T(8,128)} custom-call(s32[2]{0:T(128)S(1)} %get-tuple-element.21.piv, f32[128,256]{1,0:T(8,128)S(1)} %get-tuple-element.22.mt, f32[64,128]{1,0:T(8,128)S(1)} %get-tuple-element.32.rows, f32[2,16,24,128]{3,2,1,0:T(8,128)S(1)} %bitcast.2, f32[3,16,128]{2,1,0:T(8,128)S(1)} %get-tuple-element.34.lane_ids, ...), custom_call_target="tpu_custom_call" | custom-call | tf_op jit(solution)/shard_map/pallas_call | solution.py:345
Async XLA Ops:
  0.0 13.8 %copy-start = (s32[10,4096]{1,0:T(8,128)S(1)}, s32[10,4096]{1,0:T(8,128)}, u32[]{:S(2)}) copy-start(s32[10,4096]{1,0:T(8,128)} %ids.1) | copy-start | bytes 491524
  1.7 15.2 %all-to-all-start = ((f32[8,16,128]{2,1,0:T(8,128)}), f32[8,16,128]{2,1,0:T(8,128)S(1)}, u32[]{:S(2)}, u32[]{:S(2)}) async-start(f32[8,16,128]{2,1,0:T(8,128)} %get-tuple-element.23), calls=%async_computation | async-start | bytes 131072 | tf_op jit(solution)/shard_map/all_to_all | solution.py:336
  11.9 5.1 %collective-permute-start = (f32[64,128]{1,0:T(8,128)S(1)}, f32[64,128]{1,0:T(8,128)S(1)}, u32[]{:S(2)}, u32[]{:S(2)}) collective-permute-start(f32[64,128]{1,0:T(8,128)S(1)} %get-tuple-element.29.panel), channel_id=1, source_target_pairs={{0,32},{32,0},{64,96},{96,64},{128,160},{160,128},{192,224},{224,1... | collective-permute-start | bytes 98312 | tf_op jit(solution)/shard_map/ppermute | solution.py:335

commit v11 on v8

--- a/solution.py
+++ b/solution.py
@@ -72,7 +72,7 @@
     row, z, _ = place()
     corner, halves = None, [[], []]
     for i, pivot in enumerate((p, q)):
-        holder = lax.rem(pivot // 32, 2) * 4 + lax.rem(pivot // 8, 2) * 2 + lax.rem(pivot // 4, 2)
+        holder = lax.rem(pivot // 4, HOLDERS)
         mine = got[holder, 8 * i : 8 * i + 8]
         for b in range(2):
             halves[b] += [mine[2 * b : 2 * b + 2], mine[4 + 2 * b : 6 + 2 * b]]
@@ -81,7 +81,7 @@
             half = shift_lanes(half, 64 * i + 32 * j - lax.rem(other, 4) * PIVOT)
             corner = half if corner is None else jnp.where(lanes(8) // PIVOT == 2 * i + j, half, corner)
     first, second = [jnp.concatenate(parts, 0) for parts in halves]
-    even = lax.rem(z // 2, 2) == 0
+    even = lax.rem(z // 4, 2) == 0
     keep[...] = jnp.where(even, first, second)
     send[...] = jnp.where(even, second, first)
     small = jnp.where(upper_half(), own_lengths[...], pltpu.roll(corner, 4, 0))
@@ -108,11 +108,11 @@
         rows[16 * b : 16 * b + 16] = xy[row_p // 2 * 2 + b, XY_P:XY_Q]
         rows[32 + 16 * b : 48 + 16 * b] = xy[row_q // 2 * 2 + b, XY_Q:XY_ROWS]
     upper = upper_half()
-    bit = lax.rem(z // 2, 2)
+    bit = lax.rem(z // 4, 2)
     piece = jnp.where(
         upper,
-        jnp.where(lax.rem(p // 16, 2) == bit, keep[...], other[...]),
-        jnp.where(lax.rem(q // 16, 2) == bit, keep[...], other[...]),
+        jnp.where(lax.rem(p // 32, 2) == bit, keep[...], other[...]),
+        jnp.where(lax.rem(q // 32, 2) == bit, keep[...], other[...]),
     )
     corner = jnp.where(lax.rem(lanes(8) // PIVOT, 2) == 0, xy[row_p, 0:XY_P], xy[row_q, 0:XY_P])
     turn = 2 * lax.rem(z, 2) + core
@@ -235,12 +235,12 @@
         home = pivot // 64 * 8
         for n in range(HOLDERS):
             at = 32 * i + 4 * n
-            base = home + 4 * (n // 4) + n // 2 % 2
+            base = home + n // 2
             for b in range(2):
-                part = zed[n % 2, base + 2 * b, 0:Z_L]
+                part = zed[n % 2, base + 4 * b, 0:Z_L]
                 ct[at + 2 * b : at + 2 * b + 2, 0:128] = part[4 * i : 4 * i + 2]
                 ct[at + 2 * b : at + 2 * b + 2, 128:256] = part[4 * i + 2 : 4 * i + 4]
-            corner = zed[n % 2, base + 2 * lax.rem(pivot // 16, 2), Z_L:Z_ROWS]
+            corner = zed[n % 2, base + 4 * lax.rem(pivot // 32, 2), Z_L:Z_ROWS]
             kt[at : at + 4, :] = shift_lanes(corner, 64 * i)[4:8]
 
     lane = lanes(8)
@@ -342,20 +342,18 @@
         8,
         [SM] + [VM] * 4,
     )(*[pltpu.with_memory_space_constraint(x, pltpu.HBM) for x in (pivots, distances, edge_lengths.T)])
-    other_panel = lax.ppermute(panel, "row", [(i, i ^ 1) for i in range(NXY)])
-    scatter = lax.all_to_all(scatter, ("z2", "z0", "core"), 0, 0)
-    xy, keep, send = call(spread_kernel, [(NXY, XY_ROWS, 128), (8, 128), (8, 128)], [], [SM] + [VM] * 4, 8)(
-        piv, scatter, own_lengths, panel, other_panel
-    )
-    other_half = lax.ppermute(send, "z1", [(0, 1), (1, 0)])
     lane_ids, sub_ids, onehot = call(
         ids_kernel, [(3, 16, 128), (24, NEIGHBORS, 8, 128), ONEHOT], [(128, 128)], [SM, VM], 16
     )(piv, neighbor_ids)
+    other_panel = lax.ppermute(panel, "row", [(i, i ^ 1) for i in range(NXY)])
+    scatter = lax.all_to_all(scatter, ("z1", "z0", "core"), 0, 0)
+    scatter, lane_ids, sub_ids, onehot = lax.optimization_barrier((scatter, lane_ids, sub_ids, onehot))
+    xy, keep, send = call(spread_kernel, [(NXY, XY_ROWS, 128), (8, 128), (8, 128)], [], [SM] + [VM] * 4, 8)(
+        piv, scatter, own_lengths, panel, other_panel
+    )
+    other = lax.ppermute(send, "z2", [(0, 1), (1, 0)])
     xy = lax.all_to_all(xy, "row", 0, 0)
-    xy, lane_ids, sub_ids, onehot = lax.optimization_barrier((xy, lane_ids, sub_ids, onehot))
-    zed, rows = call(gather_kernel, [(NZ, Z_ROWS, 128), (64, 128)], [], [SM] + [VM] * 3, 8)(
-        piv, xy, keep, other_half
-    )
+    zed, rows = call(gather_kernel, [(NZ, Z_ROWS, 128), (64, 128)], [], [SM] + [VM] * 3, 8)(piv, xy, keep, other)
     zed = lax.all_to_all(zed, ("z3", "z2", "z1", "z0"), 0, 0)
     zed = lax.all_gather(zed, "core")
     (out,) = call(final_kernel, [(ROWS, COLS)], FINAL_SCRATCH, [SM] + [VM] * 6, 24)(

time: 70.9 us -> 66.5 us (0.938)
  waiting for transfers between devices: 6.56 us -> 2.96 us
  starting transfers between devices: 26.3 us -> 24.9 us
    ppermute x1, starting transfers between devices: 4.9 us -> 8.82 us  [on_device(): other = lax.ppermute(send, 'z2', [(0, 1), (1, 0)])]
    all_to_all x1, starting transfers between devices: 6.89 us -> 3.99 us  [on_device(): xy = lax.all_to_all(xy, 'row', 0, 0)]
    ppermute x1, waiting for transfers between devices: 1.74 us -> 0.01 us  [on_device(): other_panel = lax.ppermute(panel, 'row', [(i, i ^ 1) for i in range(NXY)])]
    all_to_all x1, waiting for transfers between devices: 1.68 us -> 0.01 us  [on_device(): xy = lax.all_to_all(xy, 'row', 0, 0)]
    ppermute x1, starting transfers between devices: 3.19 us -> 1.91 us  [on_device(): other_panel = lax.ppermute(panel, 'row', [(i, i ^ 1) for i in range(NXY)])]
    all_to_all x1, starting transfers between devices: 11.3 us -> 10.1 us  [on_device(): scatter = lax.all_to_all(scatter, ('z1', 'z0', 'core'), 0, 0)]
    all_to_all x1, waiting for transfers between devices: 3.14 us -> 1.98 us  [on_device(): scatter = lax.all_to_all(scatter, ('z1', 'z0', 'core'), 0, 0)]
    ppermute x1, waiting for transfers between devices: 0.01 us -> 0.98 us  [on_device(): other = lax.ppermute(send, 'z2', [(0, 1), (1, 0)])]
  transfers between devices with their start and end apart: 4 -> 4, of which waited for: 3 -> 2; matrix products, arithmetic and copies ran while one was open for 0% -> 0% of each run, Pallas kernels for 2% -> 2%
where the time goes in v11:
time: 66.5 us; the launch traced here: 66.1 us
  blocking collectives  28.6 us (43%)
  starting transfers between devices  24.9 us (37%)
  Pallas kernels  9.67 us (15%)
  waiting for transfers between devices  2.96 us (4%)
    all_to_all x1, blocking collectives, on_device(): zed = lax.all_to_all(zed, ('z3', 'z2', 'z1', 'z0'), 0, 0)  22.8 us
    all_to_all x1, starting transfers between devices, on_device(): scatter = lax.all_to_all(scatter, ('z1', 'z0', 'core'), 0, 0)  10.1 us
    ppermute x1, starting transfers between devices, on_device(): other = lax.ppermute(send, 'z2', [(0, 1), (1, 0)])  8.82 us
    all_gather x1, blocking collectives, on_device(): zed = lax.all_gather(zed, 'core')  5.74 us
    pallas_call x1, Pallas kernels, on_device(): call(final_kernel, [(ROWS, COLS)], FINAL_SCRATCH, [SM] + [VM] * 6, 24)  4.64 us
    all_to_all x1, starting transfers between devices, on_device(): xy = lax.all_to_all(xy, 'row', 0, 0)  3.99 us
    all_to_all x1, waiting for transfers between devices, on_device(): scatter = lax.all_to_all(scatter, ('z1', 'z0', 'core'), 0, 0)  1.98 us
    ppermute x1, starting transfers between devices, on_device(): other_panel = lax.ppermute(panel, 'row', [(i, i ^ 1) for i in range(NXY)])  1.91 us
  transfers between devices with their start and end apart: 4, of which 2 were waited for; matrix products, arithmetic and copies ran while one was open for 0% of the time, Pallas kernels for 2%

profile of v11, /device:TPU:1, one launch (start us, length us, event | category | flops | bytes accessed | tf_op | source)
XLA Modules:
  0.0 66.1 jit_solution(113997787991686619)
XLA Ops:
  0.0 0.0 copy-start
  0.0 1.7 %shard_map.46 = (s32[2]{0:T(128)S(1)}, f32[128,256]{1,0:T(8,128)S(1)}, f32[8,16,128]{2,1,0:T(8,128)}, f32[64,128]{1,0:T(8,128)S(1)}, f32[8,128]{1,0:T(8,128)S(1)}) custom-call(s32[2]{0:T(128)} %pivots.1, f32[256,128]{1,0:T(8,128)} %dist.1, f32[8,10]{1,0:T(8,128)} %bitcast.3), custom_call_target="tpu_custom_call" | custom-call | tf_op jit(solution)/shard_map/pallas_call | solution.py:337
  1.8 10.1 %all-to-all-start = ((f32[8,16,128]{2,1,0:T(8,128)}), f32[8,16,128]{2,1,0:T(8,128)S(1)}, u32[]{:S(2)}, u32[]{:S(2)}) async-start(f32[8,16,128]{2,1,0:T(8,128)} %get-tuple-element.24), calls=%async_computation | async-start | bytes 131072 | tf_op jit(solution)/shard_map/all_to_all | solution.py:349
  11.9 1.9 %collective-permute-start = (f32[64,128]{1,0:T(8,128)S(1)}, f32[64,128]{1,0:T(8,128)S(1)}, u32[]{:S(2)}, u32[]{:S(2)}) collective-permute-start(f32[64,128]{1,0:T(8,128)S(1)} %get-tuple-element.30.panel), channel_id=1, source_target_pairs={{0,32},{32,0},{64,96},{96,64},{128,160},{160,128},{192,224},{224,1... | collective-permute-start | bytes 98312 | tf_op jit(solution)/shard_map/ppermute | solution.py:348
  13.8 0.0 copy-done
  13.8 1.2 %shard_map.47 = (f32[3,16,128]{2,1,0:T(8,128)S(1)}, f32[24,10,8,128]{3,2,1,0:T(8,128)S(1)}, bf16[64,2048]{1,0:T(8,128)(2,1)S(1)}) custom-call(s32[2]{0:T(128)S(1)} %get-tuple-element.22.piv, s32[10,4096]{1,0:T(8,128)S(1)} %copy-done), custom_call_target="tpu_custom_call" | custom-call | tf_op jit(solution)/shard_map/pallas_call | solution.py:345
  15.0 2.0 %all-to-all-done.got = f32[8,16,128]{2,1,0:T(8,128)S(1)} async-done(((f32[8,16,128]{2,1,0:T(8,128)}), f32[8,16,128]{2,1,0:T(8,128)S(1)}, u32[]{:S(2)}, u32[]{:S(2)}) %all-to-all-start) | async-done | bytes 65568 | tf_op jit(solution)/shard_map/all_to_all | solution.py:349
  17.0 0.0 collective-permute-done.other_panel
  17.0 1.4 %shard_map.48 = (f32[16,40,128]{2,1,0:T(8,128)}, f32[8,128]{1,0:T(8,128)S(1)}, f32[8,128]{1,0:T(8,128)S(1)}) custom-call(s32[2]{0:T(128)S(1)} %get-tuple-element.22.piv, f32[8,16,128]{2,1,0:T(8,128)S(1)} %all-to-all-done.got, f32[8,128]{1,0:T(8,128)S(1)} %get-tuple-element.29.own_lengths, f32[64,128]{1,0:T(8,128)S(1)} %get-tuple-element.30.panel, ...), custom_call_target="tpu_custom_call" | custom-call | tf_op jit(solution)/shard_map/pallas_call | solution.py:351
  18.4 4.0 %all-to-all-start.1 = ((f32[16,40,128]{2,1,0:T(8,128)}), f32[16,40,128]{2,1,0:T(8,128)S(1)}, u32[]{:S(2)}, u32[]{:S(2)}) async-start(f32[16,40,128]{2,1,0:T(8,128)} %get-tuple-element.31), calls=%async_computation.1 | async-start | bytes 655360 | tf_op jit(solution)/shard_map/all_to_all | solution.py:355
  22.4 8.8 %collective-permute-start.1 = (f32[8,128]{1,0:T(8,128)S(1)}, f32[8,128]{1,0:T(8,128)S(1)}, u32[]{:S(2)}, u32[]{:S(2)}) collective-permute-start(f32[8,128]{1,0:T(8,128)S(1)} %get-tuple-element.33), channel_id=1, source_target_pairs={{0,8},{8,0},{1,9},{9,1},{2,10},{10,2},{3,11},{11,3},{4,12},{12,4},... | collective-permute-start | bytes 12296 | tf_op jit(solution)/shard_map/ppermute | solution.py:354
  31.2 1.0 %collective-permute-done.1.other = f32[8,128]{1,0:T(8,128)S(1)} collective-permute-done((f32[8,128]{1,0:T(8,128)S(1)}, f32[8,128]{1,0:T(8,128)S(1)}, u32[]{:S(2)}, u32[]{:S(2)}) %collective-permute-start.1) | collective-permute-done | bytes 4128 | tf_op jit(solution)/shard_map/ppermute | solution.py:354
  32.2 0.0 all-to-all-done.1.xy
  32.2 0.7 %shard_map.49 = (f32[16,16,128]{2,1,0:T(8,128)S(1)}, f32[64,128]{1,0:T(8,128)S(1)}) custom-call(s32[2]{0:T(128)S(1)} %get-tuple-element.22.piv, f32[16,40,128]{2,1,0:T(8,128)S(1)} %all-to-all-done.1.xy, f32[8,128]{1,0:T(8,128)S(1)} %get-tuple-element.32.keep, f32[8,128]{1,0:T(8,128)S(1)} %collective-permute-done.1.other), custom_call_target="tpu_custom_call" | custom-call | tf_op jit(solution)/shard_map/pallas_call | solution.py:356
  32.9 22.8 %all_to_all.15 = f32[16,16,128]{2,1,0:T(8,128)S(1)} all-to-all(f32[16,16,128]{2,1,0:T(8,128)S(1)} %get-tuple-element.35), channel_id=1, replica_groups=mesh['row'=16,'z3'=2,'z2'=2,'z1'=2,'z0'=2,'core'=2] {'z3','z2','z1','z0'}, dimensions={0} | all-to-all | bytes 262144 | tf_op jit(solution)/shard_map/all_to_all | solution.py:357
  55.8 5.7 %all-gather = f32[32,16,128]{2,1,0:T(8,128)S(1)} all-gather(f32[16,16,128]{2,1,0:T(8,128)S(1)} %all_to_all.15), channel_id=2, replica_groups=mesh['row'=16,'z3'=2,'z2'=2,'z1'=2,'z0'=2,'core'=2] {'core'}, dimensions={0}, use_global_device_ids=true | all-gather | bytes 393216 | tf_op jit(solution)/shard_map/all_gather | solution.py:358
  61.5 4.6 %shard_map.50 = f32[256,128]{1,0:T(8,128)} custom-call(s32[2]{0:T(128)S(1)} %get-tuple-element.22.piv, f32[128,256]{1,0:T(8,128)S(1)} %get-tuple-element.23.mt, f32[64,128]{1,0:T(8,128)S(1)} %get-tuple-element.34.rows, f32[2,16,16,128]{3,2,1,0:T(8,128)S(1)} %bitcast.2, f32[3,16,128]{2,1,0:T(8,128)S(1)} %get-tuple-element.36.lane_ids, ...), custom_call_target="tpu_custom_call" | custom-call | tf_op jit(solution)/shard_map/pallas_call | solution.py:359
Async XLA Ops:
  0.0 13.8 %copy-start = (s32[10,4096]{1,0:T(8,128)S(1)}, s32[10,4096]{1,0:T(8,128)}, u32[]{:S(2)}) copy-start(s32[10,4096]{1,0:T(8,128)} %ids.1) | copy-start | bytes 491524
  1.8 15.2 %all-to-all-start = ((f32[8,16,128]{2,1,0:T(8,128)}), f32[8,16,128]{2,1,0:T(8,128)S(1)}, u32[]{:S(2)}, u32[]{:S(2)}) async-start(f32[8,16,128]{2,1,0:T(8,128)} %get-tuple-element.24), calls=%async_computation | async-start | bytes 131072 | tf_op jit(solution)/shard_map/all_to_all | solution.py:349
  11.9 5.1 %collective-permute-start = (f32[64,128]{1,0:T(8,128)S(1)}, f32[64,128]{1,0:T(8,128)S(1)}, u32[]{:S(2)}, u32[]{:S(2)}) collective-permute-start(f32[64,128]{1,0:T(8,128)S(1)} %get-tuple-element.30.panel), channel_id=1, source_target_pairs={{0,32},{32,0},{64,96},{96,64},{128,160},{160,128},{192,224},{224,1... | collective-permute-start | bytes 98312 | tf_op jit(solution)/shard_map/ppermute | solution.py:348
  18.4 13.8 %all-to-all-start.1 = ((f32[16,40,128]{2,1,0:T(8,128)}), f32[16,40,128]{2,1,0:T(8,128)S(1)}, u32[]{:S(2)}, u32[]{:S(2)}) async-start(f32[16,40,128]{2,1,0:T(8,128)} %get-tuple-element.31), calls=%async_computation.1 | async-start | bytes 655360 | tf_op jit(solution)/shard_map/all_to_all | solution.py:355
  22.4 9.8 %collective-permute-start.1 = (f32[8,128]{1,0:T(8,128)S(1)}, f32[8,128]{1,0:T(8,128)S(1)}, u32[]{:S(2)}, u32[]{:S(2)}) collective-permute-start(f32[8,128]{1,0:T(8,128)S(1)} %get-tuple-element.33), channel_id=1, source_target_pairs={{0,8},{8,0},{1,9},{9,1},{2,10},{10,2},{3,11},{11,3},{4,12},{12,4},... | collective-permute-start | bytes 12296 | tf_op jit(solution)/shard_map/ppermute | solution.py:354

commit v12 on v11

--- a/solution.py
+++ b/solution.py
@@ -297,16 +297,15 @@
         ct[at : at + 8, 0:128] = state[0][tile]
         ct[at : at + 8, 128:256] = state[1][tile]
 
-    def body(i, carry):
-        at = pl.multiple_of(32 * i, 32)
-        for half in (0, 128):
-            here = new[pl.ds(at, 32), half : half + 128]
-            for t in range(2 * PIVOT):
-                here = jnp.minimum(here, spread[pl.ds(at, 32), 128 * t : 128 * t + 128] + ct[t : t + 1, half : half + 128])
-            new[pl.ds(at, 32), half : half + 128] = here
-        return carry
-
-    lax.fori_loop(0, COLS // 32, body, 0)
+    for at in range(0, COLS, 8):
+        one = new[at : at + 8, 0:128]
+        two = new[at : at + 8, 128:256]
+        for t in range(2 * PIVOT):
+            wide = spread[at : at + 8, 128 * t : 128 * t + 128]
+            one = jnp.minimum(one, wide + ct[t : t + 1, 0:128])
+            two = jnp.minimum(two, wide + ct[t : t + 1, 128:256])
+        new[at : at + 8, 0:128] = one
+        new[at : at + 8, 128:256] = two
     for h in range(2):
         out[128 * h : 128 * h + 128, :] = new[:, 128 * h : 128 * h + 128].T
 

time: 66.5 us -> 66.1 us (level)
  no operation moved by 1% of the time
where the time goes in v12:
time: 66.1 us; the launch traced here: 65.7 us
  blocking collectives  28.6 us (43%)
  starting transfers between devices  24.9 us (38%)
  Pallas kernels  9.22 us (14%)
  waiting for transfers between devices  2.96 us (4%)
    all_to_all x1, blocking collectives, on_device(): zed = lax.all_to_all(zed, ('z3', 'z2', 'z1', 'z0'), 0, 0)  22.8 us
    all_to_all x1, starting transfers between devices, on_device(): scatter = lax.all_to_all(scatter, ('z1', 'z0', 'core'), 0, 0)  10.1 us
    ppermute x1, starting transfers between devices, on_device(): other = lax.ppermute(send, 'z2', [(0, 1), (1, 0)])  8.82 us
    all_gather x1, blocking collectives, on_device(): zed = lax.all_gather(zed, 'core')  5.74 us
    pallas_call x1, Pallas kernels, on_device(): call(final_kernel, [(ROWS, COLS)], FINAL_SCRATCH, [SM] + [VM] * 6, 24)  4.18 us
    all_to_all x1, starting transfers between devices, on_device(): xy = lax.all_to_all(xy, 'row', 0, 0)  3.99 us
    all_to_all x1, waiting for transfers between devices, on_device(): scatter = lax.all_to_all(scatter, ('z1', 'z0', 'core'), 0, 0)  1.98 us
    ppermute x1, starting transfers between devices, on_device(): other_panel = lax.ppermute(panel, 'row', [(i, i ^ 1) for i in range(NXY)])  1.91 us
  transfers between devices with their start and end apart: 4, of which 2 were waited for; matrix products, arithmetic and copies ran while one was open for 0% of the time, Pallas kernels for 2%

profile of v12, /device:TPU:1, one launch (start us, length us, event | category | flops | bytes accessed | tf_op | source)
XLA Modules:
  0.0 65.7 jit_solution(2344318857996619342)
XLA Ops:
  0.0 0.0 copy-start
  0.0 1.7 %shard_map.46 = (s32[2]{0:T(128)S(1)}, f32[128,256]{1,0:T(8,128)S(1)}, f32[8,16,128]{2,1,0:T(8,128)}, f32[64,128]{1,0:T(8,128)S(1)}, f32[8,128]{1,0:T(8,128)S(1)}) custom-call(s32[2]{0:T(128)} %pivots.1, f32[256,128]{1,0:T(8,128)} %dist.1, f32[8,10]{1,0:T(8,128)} %bitcast.3), custom_call_target="tpu_custom_call" | custom-call | tf_op jit(solution)/shard_map/pallas_call | solution.py:336
  1.8 10.1 %all-to-all-start = ((f32[8,16,128]{2,1,0:T(8,128)}), f32[8,16,128]{2,1,0:T(8,128)S(1)}, u32[]{:S(2)}, u32[]{:S(2)}) async-start(f32[8,16,128]{2,1,0:T(8,128)} %get-tuple-element.24), calls=%async_computation | async-start | bytes 131072 | tf_op jit(solution)/shard_map/all_to_all | solution.py:348
  11.9 1.9 %collective-permute-start = (f32[64,128]{1,0:T(8,128)S(1)}, f32[64,128]{1,0:T(8,128)S(1)}, u32[]{:S(2)}, u32[]{:S(2)}) collective-permute-start(f32[64,128]{1,0:T(8,128)S(1)} %get-tuple-element.30.panel), channel_id=1, source_target_pairs={{0,32},{32,0},{64,96},{96,64},{128,160},{160,128},{192,224},{224,1... | collective-permute-start | bytes 98312 | tf_op jit(solution)/shard_map/ppermute | solution.py:347
  13.8 0.0 copy-done
  13.8 1.2 %shard_map.47 = (f32[3,16,128]{2,1,0:T(8,128)S(1)}, f32[24,10,8,128]{3,2,1,0:T(8,128)S(1)}, bf16[64,2048]{1,0:T(8,128)(2,1)S(1)}) custom-call(s32[2]{0:T(128)S(1)} %get-tuple-element.22.piv, s32[10,4096]{1,0:T(8,128)S(1)} %copy-done), custom_call_target="tpu_custom_call" | custom-call | tf_op jit(solution)/shard_map/pallas_call | solution.py:344
  15.0 2.0 %all-to-all-done.got = f32[8,16,128]{2,1,0:T(8,128)S(1)} async-done(((f32[8,16,128]{2,1,0:T(8,128)}), f32[8,16,128]{2,1,0:T(8,128)S(1)}, u32[]{:S(2)}, u32[]{:S(2)}) %all-to-all-start) | async-done | bytes 65568 | tf_op jit(solution)/shard_map/all_to_all | solution.py:348
  17.0 0.0 collective-permute-done.other_panel
  17.0 1.4 %shard_map.48 = (f32[16,40,128]{2,1,0:T(8,128)}, f32[8,128]{1,0:T(8,128)S(1)}, f32[8,128]{1,0:T(8,128)S(1)}) custom-call(s32[2]{0:T(128)S(1)} %get-tuple-element.22.piv, f32[8,16,128]{2,1,0:T(8,128)S(1)} %all-to-all-done.got, f32[8,128]{1,0:T(8,128)S(1)} %get-tuple-element.29.own_lengths, f32[64,128]{1,0:T(8,128)S(1)} %get-tuple-element.30.panel, ...), custom_call_target="tpu_custom_call" | custom-call | tf_op jit(solution)/shard_map/pallas_call | solution.py:350
  18.4 4.0 %all-to-all-start.1 = ((f32[16,40,128]{2,1,0:T(8,128)}), f32[16,40,128]{2,1,0:T(8,128)S(1)}, u32[]{:S(2)}, u32[]{:S(2)}) async-start(f32[16,40,128]{2,1,0:T(8,128)} %get-tuple-element.31), calls=%async_computation.1 | async-start | bytes 655360 | tf_op jit(solution)/shard_map/all_to_all | solution.py:354
  22.4 8.8 %collective-permute-start.1 = (f32[8,128]{1,0:T(8,128)S(1)}, f32[8,128]{1,0:T(8,128)S(1)}, u32[]{:S(2)}, u32[]{:S(2)}) collective-permute-start(f32[8,128]{1,0:T(8,128)S(1)} %get-tuple-element.33), channel_id=1, source_target_pairs={{0,8},{8,0},{1,9},{9,1},{2,10},{10,2},{3,11},{11,3},{4,12},{12,4},... | collective-permute-start | bytes 12296 | tf_op jit(solution)/shard_map/ppermute | solution.py:353
  31.2 1.0 %collective-permute-done.1.other = f32[8,128]{1,0:T(8,128)S(1)} collective-permute-done((f32[8,128]{1,0:T(8,128)S(1)}, f32[8,128]{1,0:T(8,128)S(1)}, u32[]{:S(2)}, u32[]{:S(2)}) %collective-permute-start.1) | collective-permute-done | bytes 4128 | tf_op jit(solution)/shard_map/ppermute | solution.py:353
  32.2 0.0 all-to-all-done.1.xy
  32.2 0.7 %shard_map.49 = (f32[16,16,128]{2,1,0:T(8,128)S(1)}, f32[64,128]{1,0:T(8,128)S(1)}) custom-call(s32[2]{0:T(128)S(1)} %get-tuple-element.22.piv, f32[16,40,128]{2,1,0:T(8,128)S(1)} %all-to-all-done.1.xy, f32[8,128]{1,0:T(8,128)S(1)} %get-tuple-element.32.keep, f32[8,128]{1,0:T(8,128)S(1)} %collective-permute-done.1.other), custom_call_target="tpu_custom_call" | custom-call | tf_op jit(solution)/shard_map/pallas_call | solution.py:355
  32.9 22.8 %all_to_all.15 = f32[16,16,128]{2,1,0:T(8,128)S(1)} all-to-all(f32[16,16,128]{2,1,0:T(8,128)S(1)} %get-tuple-element.35), channel_id=1, replica_groups=mesh['row'=16,'z3'=2,'z2'=2,'z1'=2,'z0'=2,'core'=2] {'z3','z2','z1','z0'}, dimensions={0} | all-to-all | bytes 262144 | tf_op jit(solution)/shard_map/all_to_all | solution.py:356
  55.8 5.7 %all-gather = f32[32,16,128]{2,1,0:T(8,128)S(1)} all-gather(f32[16,16,128]{2,1,0:T(8,128)S(1)} %all_to_all.15), channel_id=2, replica_groups=mesh['row'=16,'z3'=2,'z2'=2,'z1'=2,'z0'=2,'core'=2] {'core'}, dimensions={0}, use_global_device_ids=true | all-gather | bytes 393216 | tf_op jit(solution)/shard_map/all_gather | solution.py:357
  61.5 4.2 %shard_map.50 = f32[256,128]{1,0:T(8,128)} custom-call(s32[2]{0:T(128)S(1)} %get-tuple-element.22.piv, f32[128,256]{1,0:T(8,128)S(1)} %get-tuple-element.23.mt, f32[64,128]{1,0:T(8,128)S(1)} %get-tuple-element.34.rows, f32[2,16,16,128]{3,2,1,0:T(8,128)S(1)} %bitcast.2, f32[3,16,128]{2,1,0:T(8,128)S(1)} %get-tuple-element.36.lane_ids, ...), custom_call_target="tpu_custom_call" | custom-call | tf_op jit(solution)/shard_map/pallas_call | solution.py:358
Async XLA Ops:
  0.0 13.8 %copy-start = (s32[10,4096]{1,0:T(8,128)S(1)}, s32[10,4096]{1,0:T(8,128)}, u32[]{:S(2)}) copy-start(s32[10,4096]{1,0:T(8,128)} %ids.1) | copy-start | bytes 491524
  1.8 15.2 %all-to-all-start = ((f32[8,16,128]{2,1,0:T(8,128)}), f32[8,16,128]{2,1,0:T(8,128)S(1)}, u32[]{:S(2)}, u32[]{:S(2)}) async-start(f32[8,16,128]{2,1,0:T(8,128)} %get-tuple-element.24), calls=%async_computation | async-start | bytes 131072 | tf_op jit(solution)/shard_map/all_to_all | solution.py:348
  11.9 5.1 %collective-permute-start = (f32[64,128]{1,0:T(8,128)S(1)}, f32[64,128]{1,0:T(8,128)S(1)}, u32[]{:S(2)}, u32[]{:S(2)}) collective-permute-start(f32[64,128]{1,0:T(8,128)S(1)} %get-tuple-element.30.panel), channel_id=1, source_target_pairs={{0,32},{32,0},{64,96},{96,64},{128,160},{160,128},{192,224},{224,1... | collective-permute-start | bytes 98312 | tf_op jit(solution)/shard_map/ppermute | solution.py:347
  18.4 13.8 %all-to-all-start.1 = ((f32[16,40,128]{2,1,0:T(8,128)}), f32[16,40,128]{2,1,0:T(8,128)S(1)}, u32[]{:S(2)}, u32[]{:S(2)}) async-start(f32[16,40,128]{2,1,0:T(8,128)} %get-tuple-element.31), calls=%async_computation.1 | async-start | bytes 655360 | tf_op jit(solution)/shard_map/all_to_all | solution.py:354
  22.4 9.8 %collective-permute-start.1 = (f32[8,128]{1,0:T(8,128)S(1)}, f32[8,128]{1,0:T(8,128)S(1)}, u32[]{:S(2)}, u32[]{:S(2)}) collective-permute-start(f32[8,128]{1,0:T(8,128)S(1)} %get-tuple-element.33), channel_id=1, source_target_pairs={{0,8},{8,0},{1,9},{9,1},{2,10},{10,2},{3,11},{11,3},{4,12},{12,4},... | collective-permute-start | bytes 12296 | tf_op jit(solution)/shard_map/ppermute | solution.py:353

commit v13 on v12

--- a/solution.py
+++ b/solution.py
@@ -41,17 +41,19 @@
 
 
 def pack_kernel(pivots, dist, lengths, piv, mt, scatter, panel, own_lengths, block, held, sems):
-    copies = [
-        pltpu.make_async_copy(dist, block, sems.at[0]),
-        pltpu.make_async_copy(lengths, held, sems.at[1]),
+    halves = [pl.ds(128 * h, 128) for h in range(2)]
+    parts = [pltpu.make_async_copy(dist.at[half], block.at[half], sems.at[h]) for h, half in enumerate(halves)]
+    others = [
         pltpu.make_async_copy(pivots, piv, sems.at[2]),
+        pltpu.make_async_copy(lengths, held, sems.at[3]),
     ]
-    for copy in copies:
+    for copy in parts + others:
         copy.start()
-    for copy in copies:
+    for h in range(2):
+        parts[h].wait()
+        mt[:, 128 * h : 128 * h + 128] = block[128 * h : 128 * h + 128, :].T
+    for copy in others:
         copy.wait()
-    for h in range(2):
-        mt[:, 128 * h : 128 * h + 128] = block[128 * h : 128 * h + 128, :].T
     for i in range(2):
         off = lax.rem(piv[i], 4) * PIVOT
         for n in range(0, HOLDERS, 2):
@@ -287,10 +289,10 @@
         else:
             if b == 4:
                 parts = thirds(rt[...])
-            for c in range(4):
-                at = 2048 * (b - 4) + 512 * c
-                spread[:, at : at + 512] = jnp.dot(
-                    parts[b - 4], onehot[:, 512 * c : 512 * c + 512], preferred_element_type=F32
+            for c in range(8):
+                at = 2048 * (b - 4) + 256 * c
+                spread[:, at : at + 256] = jnp.dot(
+                    parts[b - 4], onehot[:, 256 * c : 256 * c + 256], preferred_element_type=F32
                 )
     for tile in range(8):
         at = 8 * tile
@@ -336,7 +338,7 @@
     piv, mt, scatter, panel, own_lengths = call(
         pack_kernel,
         [PIVOTS, (COLS, ROWS), (HOLDERS, 16, 128), (64, 128), (8, 128)],
-        [(ROWS, COLS), (8, NEIGHBORS), pltpu.SemaphoreType.DMA((3,))],
+        [(ROWS, COLS), (8, NEIGHBORS), pltpu.SemaphoreType.DMA((4,))],
         [HBM] * 3,
         8,
         [SM] + [VM] * 4,

time: 66.1 us -> 66.2 us (level)
  no operation moved by 1% of the time
where the time goes in v13:
time: 66.2 us; the launch traced here: 65.8 us
  blocking collectives  28.6 us (43%)
  starting transfers between devices  24.9 us (38%)
  Pallas kernels  9.32 us (14%)
  waiting for transfers between devices  2.96 us (4%)
    all_to_all x1, blocking collectives, on_device(): zed = lax.all_to_all(zed, ('z3', 'z2', 'z1', 'z0'), 0, 0)  22.8 us
    all_to_all x1, starting transfers between devices, on_device(): scatter = lax.all_to_all(scatter, ('z1', 'z0', 'core'), 0, 0)  10.1 us
    ppermute x1, starting transfers between devices, on_device(): other = lax.ppermute(send, 'z2', [(0, 1), (1, 0)])  8.82 us
    all_gather x1, blocking collectives, on_device(): zed = lax.all_gather(zed, 'core')  5.74 us
    pallas_call x1, Pallas kernels, on_device(): call(final_kernel, [(ROWS, COLS)], FINAL_SCRATCH, [SM] + [VM] * 6, 24)  4.19 us
    all_to_all x1, starting transfers between devices, on_device(): xy = lax.all_to_all(xy, 'row', 0, 0)  3.99 us
    all_to_all x1, waiting for transfers between devices, on_device(): scatter = lax.all_to_all(scatter, ('z1', 'z0', 'core'), 0, 0)  1.98 us
    ppermute x1, starting transfers between devices, on_device(): other_panel = lax.ppermute(panel, 'row', [(i, i ^ 1) for i in range(NXY)])  1.91 us
  transfers between devices with their start and end apart: 4, of which 2 were waited for; matrix products, arithmetic and copies ran while one was open for 0% of the time, Pallas kernels for 2%

profile of v13, /device:TPU:1, one launch (start us, length us, event | category | flops | bytes accessed | tf_op | source)
XLA Modules:
  0.0 65.8 jit_solution(3533774123002936963)
XLA Ops:
  0.0 0.0 copy-start
  0.0 1.8 %shard_map.46 = (s32[2]{0:T(128)S(1)}, f32[128,256]{1,0:T(8,128)S(1)}, f32[8,16,128]{2,1,0:T(8,128)}, f32[64,128]{1,0:T(8,128)S(1)}, f32[8,128]{1,0:T(8,128)S(1)}) custom-call(s32[2]{0:T(128)} %pivots.1, f32[256,128]{1,0:T(8,128)} %dist.1, f32[8,10]{1,0:T(8,128)} %bitcast.3), custom_call_target="tpu_custom_call" | custom-call | tf_op jit(solution)/shard_map/pallas_call | solution.py:338
  1.8 10.1 %all-to-all-start = ((f32[8,16,128]{2,1,0:T(8,128)}), f32[8,16,128]{2,1,0:T(8,128)S(1)}, u32[]{:S(2)}, u32[]{:S(2)}) async-start(f32[8,16,128]{2,1,0:T(8,128)} %get-tuple-element.24), calls=%async_computation | async-start | bytes 131072 | tf_op jit(solution)/shard_map/all_to_all | solution.py:350
  12.0 1.9 %collective-permute-start = (f32[64,128]{1,0:T(8,128)S(1)}, f32[64,128]{1,0:T(8,128)S(1)}, u32[]{:S(2)}, u32[]{:S(2)}) collective-permute-start(f32[64,128]{1,0:T(8,128)S(1)} %get-tuple-element.30.panel), channel_id=1, source_target_pairs={{0,32},{32,0},{64,96},{96,64},{128,160},{160,128},{192,224},{224,1... | collective-permute-start | bytes 98312 | tf_op jit(solution)/shard_map/ppermute | solution.py:349
  13.9 0.0 copy-done
  13.9 1.2 %shard_map.47 = (f32[3,16,128]{2,1,0:T(8,128)S(1)}, f32[24,10,8,128]{3,2,1,0:T(8,128)S(1)}, bf16[64,2048]{1,0:T(8,128)(2,1)S(1)}) custom-call(s32[2]{0:T(128)S(1)} %get-tuple-element.22.piv, s32[10,4096]{1,0:T(8,128)S(1)} %copy-done), custom_call_target="tpu_custom_call" | custom-call | tf_op jit(solution)/shard_map/pallas_call | solution.py:346
  15.1 2.0 %all-to-all-done.got = f32[8,16,128]{2,1,0:T(8,128)S(1)} async-done(((f32[8,16,128]{2,1,0:T(8,128)}), f32[8,16,128]{2,1,0:T(8,128)S(1)}, u32[]{:S(2)}, u32[]{:S(2)}) %all-to-all-start) | async-done | bytes 65568 | tf_op jit(solution)/shard_map/all_to_all | solution.py:350
  17.1 0.0 collective-permute-done.other_panel
  17.1 1.4 %shard_map.48 = (f32[16,40,128]{2,1,0:T(8,128)}, f32[8,128]{1,0:T(8,128)S(1)}, f32[8,128]{1,0:T(8,128)S(1)}) custom-call(s32[2]{0:T(128)S(1)} %get-tuple-element.22.piv, f32[8,16,128]{2,1,0:T(8,128)S(1)} %all-to-all-done.got, f32[8,128]{1,0:T(8,128)S(1)} %get-tuple-element.29.own_lengths, f32[64,128]{1,0:T(8,128)S(1)} %get-tuple-element.30.panel, ...), custom_call_target="tpu_custom_call" | custom-call | tf_op jit(solution)/shard_map/pallas_call | solution.py:352
  18.5 4.0 %all-to-all-start.1 = ((f32[16,40,128]{2,1,0:T(8,128)}), f32[16,40,128]{2,1,0:T(8,128)S(1)}, u32[]{:S(2)}, u32[]{:S(2)}) async-start(f32[16,40,128]{2,1,0:T(8,128)} %get-tuple-element.31), calls=%async_computation.1 | async-start | bytes 655360 | tf_op jit(solution)/shard_map/all_to_all | solution.py:356
  22.5 8.8 %collective-permute-start.1 = (f32[8,128]{1,0:T(8,128)S(1)}, f32[8,128]{1,0:T(8,128)S(1)}, u32[]{:S(2)}, u32[]{:S(2)}) collective-permute-start(f32[8,128]{1,0:T(8,128)S(1)} %get-tuple-element.33), channel_id=1, source_target_pairs={{0,8},{8,0},{1,9},{9,1},{2,10},{10,2},{3,11},{11,3},{4,12},{12,4},... | collective-permute-start | bytes 12296 | tf_op jit(solution)/shard_map/ppermute | solution.py:355
  31.3 1.0 %collective-permute-done.1.other = f32[8,128]{1,0:T(8,128)S(1)} collective-permute-done((f32[8,128]{1,0:T(8,128)S(1)}, f32[8,128]{1,0:T(8,128)S(1)}, u32[]{:S(2)}, u32[]{:S(2)}) %collective-permute-start.1) | collective-permute-done | bytes 4128 | tf_op jit(solution)/shard_map/ppermute | solution.py:355
  32.3 0.0 all-to-all-done.1.xy
  32.3 0.7 %shard_map.49 = (f32[16,16,128]{2,1,0:T(8,128)S(1)}, f32[64,128]{1,0:T(8,128)S(1)}) custom-call(s32[2]{0:T(128)S(1)} %get-tuple-element.22.piv, f32[16,40,128]{2,1,0:T(8,128)S(1)} %all-to-all-done.1.xy, f32[8,128]{1,0:T(8,128)S(1)} %get-tuple-element.32.keep, f32[8,128]{1,0:T(8,128)S(1)} %collective-permute-done.1.other), custom_call_target="tpu_custom_call" | custom-call | tf_op jit(solution)/shard_map/pallas_call | solution.py:357
  33.0 22.8 %all_to_all.15 = f32[16,16,128]{2,1,0:T(8,128)S(1)} all-to-all(f32[16,16,128]{2,1,0:T(8,128)S(1)} %get-tuple-element.35), channel_id=1, replica_groups=mesh['row'=16,'z3'=2,'z2'=2,'z1'=2,'z0'=2,'core'=2] {'z3','z2','z1','z0'}, dimensions={0} | all-to-all | bytes 262144 | tf_op jit(solution)/shard_map/all_to_all | solution.py:358
  55.8 5.7 %all-gather = f32[32,16,128]{2,1,0:T(8,128)S(1)} all-gather(f32[16,16,128]{2,1,0:T(8,128)S(1)} %all_to_all.15), channel_id=2, replica_groups=mesh['row'=16,'z3'=2,'z2'=2,'z1'=2,'z0'=2,'core'=2] {'core'}, dimensions={0}, use_global_device_ids=true | all-gather | bytes 393216 | tf_op jit(solution)/shard_map/all_gather | solution.py:359
  61.6 4.2 %shard_map.50 = f32[256,128]{1,0:T(8,128)} custom-call(s32[2]{0:T(128)S(1)} %get-tuple-element.22.piv, f32[128,256]{1,0:T(8,128)S(1)} %get-tuple-element.23.mt, f32[64,128]{1,0:T(8,128)S(1)} %get-tuple-element.34.rows, f32[2,16,16,128]{3,2,1,0:T(8,128)S(1)} %bitcast.2, f32[3,16,128]{2,1,0:T(8,128)S(1)} %get-tuple-element.36.lane_ids, ...), custom_call_target="tpu_custom_call" | custom-call | tf_op jit(solution)/shard_map/pallas_call | solution.py:360
Async XLA Ops:
  0.0 13.9 %copy-start = (s32[10,4096]{1,0:T(8,128)S(1)}, s32[10,4096]{1,0:T(8,128)}, u32[]{:S(2)}) copy-start(s32[10,4096]{1,0:T(8,128)} %ids.1) | copy-start | bytes 491524
  1.8 15.2 %all-to-all-start = ((f32[8,16,128]{2,1,0:T(8,128)}), f32[8,16,128]{2,1,0:T(8,128)S(1)}, u32[]{:S(2)}, u32[]{:S(2)}) async-start(f32[8,16,128]{2,1,0:T(8,128)} %get-tuple-element.24), calls=%async_computation | async-start | bytes 131072 | tf_op jit(solution)/shard_map/all_to_all | solution.py:350
  12.0 5.1 %collective-permute-start = (f32[64,128]{1,0:T(8,128)S(1)}, f32[64,128]{1,0:T(8,128)S(1)}, u32[]{:S(2)}, u32[]{:S(2)}) collective-permute-start(f32[64,128]{1,0:T(8,128)S(1)} %get-tuple-element.30.panel), channel_id=1, source_target_pairs={{0,32},{32,0},{64,96},{96,64},{128,160},{160,128},{192,224},{224,1... | collective-permute-start | bytes 98312 | tf_op jit(solution)/shard_map/ppermute | solution.py:349
  18.5 13.8 %all-to-all-start.1 = ((f32[16,40,128]{2,1,0:T(8,128)}), f32[16,40,128]{2,1,0:T(8,128)S(1)}, u32[]{:S(2)}, u32[]{:S(2)}) async-start(f32[16,40,128]{2,1,0:T(8,128)} %get-tuple-element.31), calls=%async_computation.1 | async-start | bytes 655360 | tf_op jit(solution)/shard_map/all_to_all | solution.py:356
  22.5 9.8 %collective-permute-start.1 = (f32[8,128]{1,0:T(8,128)S(1)}, f32[8,128]{1,0:T(8,128)S(1)}, u32[]{:S(2)}, u32[]{:S(2)}) collective-permute-start(f32[8,128]{1,0:T(8,128)S(1)} %get-tuple-element.33), channel_id=1, source_target_pairs={{0,8},{8,0},{1,9},{9,1},{2,10},{10,2},{3,11},{11,3},{4,12},{12,4},... | collective-permute-start | bytes 12296 | tf_op jit(solution)/shard_map/ppermute | solution.py:355

commit v14 on v12

--- a/solution.py
+++ b/solution.py
@@ -34,6 +34,10 @@
     for bit in ("z3", "z2", "z1", "z0"):
         z = 2 * z + lax.axis_index(bit)
     return lax.axis_index("row"), z, lax.axis_index("core")
+
+
+def rank(z):
+    return z // 8 * 8 + z // 2 % 2 * 4 + z // 4 % 2 * 2 + z % 2
 
 
 def upper_half():
@@ -122,8 +126,8 @@
 
     fixed = take(row, 0) + take(row_p, 2) + take(row_q, 3)
     for d in range(NZ):
-        zchunk[d, 0:Z_L] = piece
-        zchunk[d, Z_L:Z_ROWS] = jnp.where(upper, fixed + take(d, 1), corner)
+        zchunk[rank(d), 0:Z_L] = piece
+        zchunk[rank(d), Z_L:Z_ROWS] = jnp.where(upper, fixed + take(d, 1), corner)
 
 
 def ids_kernel(piv, ids, lane_ids, sub_ids, onehot, held):
@@ -208,7 +212,7 @@
             merged = None
             for w in range(4):
                 device = first + 4 * v + w
-                tile = zed[w % 2, device // 2, Z_L:Z_ROWS]
+                tile = zed[w % 2, rank(device // 2), Z_L:Z_ROWS]
                 merged = tile if w == 0 else jnp.where(slot == (at + w) % 4, tile, merged)
             for g in range(3):
                 moved = shift_lanes(merged, 32 * (v - g))
@@ -237,10 +241,10 @@
             at = 32 * i + 4 * n
             base = home + n // 2
             for b in range(2):
-                part = zed[n % 2, base + 4 * b, 0:Z_L]
+                part = zed[n % 2, rank(base + 4 * b), 0:Z_L]
                 ct[at + 2 * b : at + 2 * b + 2, 0:128] = part[4 * i : 4 * i + 2]
                 ct[at + 2 * b : at + 2 * b + 2, 128:256] = part[4 * i + 2 : 4 * i + 4]
-            corner = zed[n % 2, base + 4 * lax.rem(pivot // 32, 2), Z_L:Z_ROWS]
+            corner = zed[n % 2, rank(base + 4 * lax.rem(pivot // 32, 2)), Z_L:Z_ROWS]
             kt[at : at + 4, :] = shift_lanes(corner, 64 * i)[4:8]
 
     lane = lanes(8)
@@ -353,7 +357,7 @@
     other = lax.ppermute(send, "z2", [(0, 1), (1, 0)])
     xy = lax.all_to_all(xy, "row", 0, 0)
     zed, rows = call(gather_kernel, [(NZ, Z_ROWS, 128), (64, 128)], [], [SM] + [VM] * 3, 8)(piv, xy, keep, other)
-    zed = lax.all_to_all(zed, ("z3", "z2", "z1", "z0"), 0, 0)
+    zed = lax.all_to_all(zed, ("z3", "z1", "z2", "z0"), 0, 0)
     zed = lax.all_gather(zed, "core")
     (out,) = call(final_kernel, [(ROWS, COLS)], FINAL_SCRATCH, [SM] + [VM] * 6, 24)(
         piv, mt, rows, zed, lane_ids, sub_ids, onehot

time: 66.1 us -> 66.7 us (level)
  no operation moved by 1% of the time
where the time goes in v14:
time: 66.7 us; the launch traced here: 66.3 us
  blocking collectives  28.6 us (43%)
  starting transfers between devices  24.9 us (37%)
  Pallas kernels  9.78 us (15%)
  waiting for transfers between devices  2.96 us (4%)
    all_to_all x1, blocking collectives, on_device(): zed = lax.all_to_all(zed, ('z3', 'z1', 'z2', 'z0'), 0, 0)  22.9 us
    all_to_all x1, starting transfers between devices, on_device(): scatter = lax.all_to_all(scatter, ('z1', 'z0', 'core'), 0, 0)  10.1 us
    ppermute x1, starting transfers between devices, on_device(): other = lax.ppermute(send, 'z2', [(0, 1), (1, 0)])  8.82 us
    all_gather x1, blocking collectives, on_device(): zed = lax.all_gather(zed, 'core')  5.7 us
    pallas_call x1, Pallas kernels, on_device(): call(final_kernel, [(ROWS, COLS)], FINAL_SCRATCH, [SM] + [VM] * 6, 24)  4.75 us
    all_to_all x1, starting transfers between devices, on_device(): xy = lax.all_to_all(xy, 'row', 0, 0)  3.99 us
    all_to_all x1, waiting for transfers between devices, on_device(): scatter = lax.all_to_all(scatter, ('z1', 'z0', 'core'), 0, 0)  1.98 us
    ppermute x1, starting transfers between devices, on_device(): other_panel = lax.ppermute(panel, 'row', [(i, i ^ 1) for i in range(NXY)])  1.91 us
  transfers between devices with their start and end apart: 4, of which 2 were waited for; matrix products, arithmetic and copies ran while one was open for 0% of the time, Pallas kernels for 2%

profile of v14, /device:TPU:1, one launch (start us, length us, event | category | flops | bytes accessed | tf_op | source)
XLA Modules:
  0.0 66.3 jit_solution(10021556550295749431)
XLA Ops:
  0.0 0.0 copy-start
  0.0 1.7 %shard_map.46 = (s32[2]{0:T(128)S(1)}, f32[128,256]{1,0:T(8,128)S(1)}, f32[8,16,128]{2,1,0:T(8,128)}, f32[64,128]{1,0:T(8,128)S(1)}, f32[8,128]{1,0:T(8,128)S(1)}) custom-call(s32[2]{0:T(128)} %pivots.1, f32[256,128]{1,0:T(8,128)} %dist.1, f32[8,10]{1,0:T(8,128)} %bitcast.3), custom_call_target="tpu_custom_call" | custom-call | tf_op jit(solution)/shard_map/pallas_call | solution.py:340
  1.7 10.1 %all-to-all-start = ((f32[8,16,128]{2,1,0:T(8,128)}), f32[8,16,128]{2,1,0:T(8,128)S(1)}, u32[]{:S(2)}, u32[]{:S(2)}) async-start(f32[8,16,128]{2,1,0:T(8,128)} %get-tuple-element.24), calls=%async_computation | async-start | bytes 131072 | tf_op jit(solution)/shard_map/all_to_all | solution.py:352
  11.9 1.9 %collective-permute-start = (f32[64,128]{1,0:T(8,128)S(1)}, f32[64,128]{1,0:T(8,128)S(1)}, u32[]{:S(2)}, u32[]{:S(2)}) collective-permute-start(f32[64,128]{1,0:T(8,128)S(1)} %get-tuple-element.30.panel), channel_id=1, source_target_pairs={{0,32},{32,0},{64,96},{96,64},{128,160},{160,128},{192,224},{224,1... | collective-permute-start | bytes 98312 | tf_op jit(solution)/shard_map/ppermute | solution.py:351
  13.8 0.0 copy-done
  13.8 1.2 %shard_map.47 = (f32[3,16,128]{2,1,0:T(8,128)S(1)}, f32[24,10,8,128]{3,2,1,0:T(8,128)S(1)}, bf16[64,2048]{1,0:T(8,128)(2,1)S(1)}) custom-call(s32[2]{0:T(128)S(1)} %get-tuple-element.22.piv, s32[10,4096]{1,0:T(8,128)S(1)} %copy-done), custom_call_target="tpu_custom_call" | custom-call | tf_op jit(solution)/shard_map/pallas_call | solution.py:348
  15.0 2.0 %all-to-all-done.got = f32[8,16,128]{2,1,0:T(8,128)S(1)} async-done(((f32[8,16,128]{2,1,0:T(8,128)}), f32[8,16,128]{2,1,0:T(8,128)S(1)}, u32[]{:S(2)}, u32[]{:S(2)}) %all-to-all-start) | async-done | bytes 65568 | tf_op jit(solution)/shard_map/all_to_all | solution.py:352
  17.0 0.0 collective-permute-done.other_panel
  17.0 1.4 %shard_map.48 = (f32[16,40,128]{2,1,0:T(8,128)}, f32[8,128]{1,0:T(8,128)S(1)}, f32[8,128]{1,0:T(8,128)S(1)}) custom-call(s32[2]{0:T(128)S(1)} %get-tuple-element.22.piv, f32[8,16,128]{2,1,0:T(8,128)S(1)} %all-to-all-done.got, f32[8,128]{1,0:T(8,128)S(1)} %get-tuple-element.29.own_lengths, f32[64,128]{1,0:T(8,128)S(1)} %get-tuple-element.30.panel, ...), custom_call_target="tpu_custom_call" | custom-call | tf_op jit(solution)/shard_map/pallas_call | solution.py:354
  18.4 4.0 %all-to-all-start.1 = ((f32[16,40,128]{2,1,0:T(8,128)}), f32[16,40,128]{2,1,0:T(8,128)S(1)}, u32[]{:S(2)}, u32[]{:S(2)}) async-start(f32[16,40,128]{2,1,0:T(8,128)} %get-tuple-element.31), calls=%async_computation.1 | async-start | bytes 655360 | tf_op jit(solution)/shard_map/all_to_all | solution.py:358
  22.4 8.8 %collective-permute-start.1 = (f32[8,128]{1,0:T(8,128)S(1)}, f32[8,128]{1,0:T(8,128)S(1)}, u32[]{:S(2)}, u32[]{:S(2)}) collective-permute-start(f32[8,128]{1,0:T(8,128)S(1)} %get-tuple-element.33), channel_id=1, source_target_pairs={{0,8},{8,0},{1,9},{9,1},{2,10},{10,2},{3,11},{11,3},{4,12},{12,4},... | collective-permute-start | bytes 12296 | tf_op jit(solution)/shard_map/ppermute | solution.py:357
  31.2 1.0 %collective-permute-done.1.other = f32[8,128]{1,0:T(8,128)S(1)} collective-permute-done((f32[8,128]{1,0:T(8,128)S(1)}, f32[8,128]{1,0:T(8,128)S(1)}, u32[]{:S(2)}, u32[]{:S(2)}) %collective-permute-start.1) | collective-permute-done | bytes 4128 | tf_op jit(solution)/shard_map/ppermute | solution.py:357
  32.2 0.0 all-to-all-done.1.xy
  32.2 0.7 %shard_map.49 = (f32[16,16,128]{2,1,0:T(8,128)S(1)}, f32[64,128]{1,0:T(8,128)S(1)}) custom-call(s32[2]{0:T(128)S(1)} %get-tuple-element.22.piv, f32[16,40,128]{2,1,0:T(8,128)S(1)} %all-to-all-done.1.xy, f32[8,128]{1,0:T(8,128)S(1)} %get-tuple-element.32.keep, f32[8,128]{1,0:T(8,128)S(1)} %collective-permute-done.1.other), custom_call_target="tpu_custom_call" | custom-call | tf_op jit(solution)/shard_map/pallas_call | solution.py:359
  32.9 22.9 %all_to_all.15 = f32[16,16,128]{2,1,0:T(8,128)S(1)} all-to-all(f32[16,16,128]{2,1,0:T(8,128)S(1)} %get-tuple-element.35), channel_id=1, replica_groups=mesh['row'=16,'z3'=2,'z2'=2,'z1'=2,'z0'=2,'core'=2] {'z3','z1','z2','z0'}, dimensions={0} | all-to-all | bytes 262144 | tf_op jit(solution)/shard_map/all_to_all | solution.py:360
  55.8 5.7 %all-gather = f32[32,16,128]{2,1,0:T(8,128)S(1)} all-gather(f32[16,16,128]{2,1,0:T(8,128)S(1)} %all_to_all.15), channel_id=2, replica_groups=mesh['row'=16,'z3'=2,'z2'=2,'z1'=2,'z0'=2,'core'=2] {'core'}, dimensions={0}, use_global_device_ids=true | all-gather | bytes 393216 | tf_op jit(solution)/shard_map/all_gather | solution.py:361
  61.5 4.8 %shard_map.50 = f32[256,128]{1,0:T(8,128)} custom-call(s32[2]{0:T(128)S(1)} %get-tuple-element.22.piv, f32[128,256]{1,0:T(8,128)S(1)} %get-tuple-element.23.mt, f32[64,128]{1,0:T(8,128)S(1)} %get-tuple-element.34.rows, f32[2,16,16,128]{3,2,1,0:T(8,128)S(1)} %bitcast.2, f32[3,16,128]{2,1,0:T(8,128)S(1)} %get-tuple-element.36.lane_ids, ...), custom_call_target="tpu_custom_call" | custom-call | tf_op jit(solution)/shard_map/pallas_call | solution.py:362
Async XLA Ops:
  0.0 13.8 %copy-start = (s32[10,4096]{1,0:T(8,128)S(1)}, s32[10,4096]{1,0:T(8,128)}, u32[]{:S(2)}) copy-start(s32[10,4096]{1,0:T(8,128)} %ids.1) | copy-start | bytes 491524
  1.7 15.2 %all-to-all-start = ((f32[8,16,128]{2,1,0:T(8,128)}), f32[8,16,128]{2,1,0:T(8,128)S(1)}, u32[]{:S(2)}, u32[]{:S(2)}) async-start(f32[8,16,128]{2,1,0:T(8,128)} %get-tuple-element.24), calls=%async_computation | async-start | bytes 131072 | tf_op jit(solution)/shard_map/all_to_all | solution.py:352
  11.9 5.1 %collective-permute-start = (f32[64,128]{1,0:T(8,128)S(1)}, f32[64,128]{1,0:T(8,128)S(1)}, u32[]{:S(2)}, u32[]{:S(2)}) collective-permute-start(f32[64,128]{1,0:T(8,128)S(1)} %get-tuple-element.30.panel), channel_id=1, source_target_pairs={{0,32},{32,0},{64,96},{96,64},{128,160},{160,128},{192,224},{224,1... | collective-permute-start | bytes 98312 | tf_op jit(solution)/shard_map/ppermute | solution.py:351
  18.4 13.8 %all-to-all-start.1 = ((f32[16,40,128]{2,1,0:T(8,128)}), f32[16,40,128]{2,1,0:T(8,128)S(1)}, u32[]{:S(2)}, u32[]{:S(2)}) async-start(f32[16,40,128]{2,1,0:T(8,128)} %get-tuple-element.31), calls=%async_computation.1 | async-start | bytes 655360 | tf_op jit(solution)/shard_map/all_to_all | solution.py:358
  22.4 9.8 %collective-permute-start.1 = (f32[8,128]{1,0:T(8,128)S(1)}, f32[8,128]{1,0:T(8,128)S(1)}, u32[]{:S(2)}, u32[]{:S(2)}) collective-permute-start(f32[8,128]{1,0:T(8,128)S(1)} %get-tuple-element.33), channel_id=1, source_target_pairs={{0,8},{8,0},{1,9},{9,1},{2,10},{10,2},{3,11},{11,3},{4,12},{12,4},... | collective-permute-start | bytes 12296 | tf_op jit(solution)/shard_map/ppermute | solution.py:357
